TPU v7x, 512 devices: a whole 4x4x16 slice. The times are simulated.
512 devices in a mesh: row: 32 (over y, z_hi, core), col: 16 (over x, z_lo).
Axes of the slice: x: 4, y: 4, z: 16 (z_hi: 4, z_lo: 4; z = z_hi * 4 + z_lo), core: 2. Of those that a mesh axis runs over, the one named last changes fastest.
Arguments:
- tokens: bfloat16 [4096, 6144], P('row', 'col'), may hold values from -6 to 6
- ln_gain: float32 [6144], P('col'), may hold values from 0.1 to 1.9
- qkv_weight: bfloat16 [6144, 32, 384], P('col', 'row'), may hold values from -0.078125 to 0.078125
- q_gain: float32 [32, 128], P('row'), may hold values from 0.6 to 1.6
- k_gain: float32 [32, 128], P('row'), may hold values from 0.6 to 1.6
Outputs:
- attended: float32 [4096, 32, 128], P('col', 'row')
All inputs are finite; a program needn't handle non-finite values.
Results may differ from a plain program's by a relative error of at most 0.04.
Values may be sent and summed in bfloat16 or wider, within the bound.
No kernel may reach another device: no remote copies, remote signals or barrier semaphores. Data moves between devices by JAX's collectives and lax.ppermute only.
A program may use at most 64 MiB of HBM per device.

v0:
```python
import jax
import jax.numpy as jnp
from jax import lax
from jax.sharding import PartitionSpec as P

D = 6144
HS = 128


epsilon = 1e-06


def layer_norm(inputs, row_sums, row_squares, ln_gain):
    average = row_sums / D
    variance = row_squares / D - average * average
    scaled = (inputs.astype(jnp.float32) - average[:, None]) * lax.rsqrt(variance + epsilon)[
        :, None
    ]
    return (scaled * ln_gain).astype(jnp.bfloat16)


def head_norm(vectors, gain):
    average = jnp.mean(vectors, axis=-1, keepdims=True)
    centred = vectors - average
    variance = jnp.mean(centred * centred, axis=-1, keepdims=True)
    return (centred * lax.rsqrt(variance + epsilon) * gain).astype(jnp.bfloat16)


def attend(queries, keys, values):
    scores = jnp.einsum("qhd,khd->hqk", queries, keys, preferred_element_type=jnp.float32) * HS ** (
        -0.5
    )
    raised = jnp.exp(scores)
    weights = (raised / jnp.sum(raised, axis=-1, keepdims=True)).astype(jnp.bfloat16)
    return jnp.einsum("hqk,khd->qhd", weights, values, preferred_element_type=jnp.float32)


def body(tokens, ln_gain, qkv_weight, q_gain, k_gain):
    widened = tokens.astype(jnp.float32)
    row_sums, row_squares = lax.psum(
        (jnp.sum(widened, axis=1), jnp.sum(widened * widened, axis=1)), "col"
    )
    normed = layer_norm(tokens, row_sums, row_squares, ln_gain)
    gathered = lax.all_gather(normed, "row", axis=0, tiled=True)
    width_dev, heads_dev, triple = qkv_weight.shape
    head_size = triple // 3
    query_rows = gathered.shape[0] // lax.axis_size("col")
    flat_weight = qkv_weight.reshape(width_dev, heads_dev * triple)
    projected = (
        lax.psum_scatter(
            jnp.dot(gathered, flat_weight, preferred_element_type=jnp.float32).astype(jnp.bfloat16),
            "col",
            scatter_dimension=0,
            tiled=True,
        )
        .astype(jnp.float32)
        .reshape(query_rows, heads_dev, 3, head_size)
    )
    queries = head_norm(projected[:, :, 0], q_gain)
    own_keys = head_norm(projected[:, :, 1], k_gain)
    own_values = projected[:, :, 2].astype(jnp.bfloat16)
    keys, values = (
        lax.all_gather(own_keys, "col", axis=0, tiled=True),
        lax.all_gather(own_values, "col", axis=0, tiled=True),
    )
    return attend(queries, keys, values)


def solution(mesh):
    return jax.shard_map(
        body,
        mesh=mesh,
        in_specs=(P("row", "col"), P("col"), P("col", "row", None), P("row", None), P("row", None)),
        out_specs=P("col", "row", None),
        check_vma=False,
    )
```

profile of v0, /device:TPU:24, one launch (start us, length us, event | category | flops | bytes accessed | tf_op | source)
XLA Modules:
  0.0 406.8 jit_solution(5680944941722665466)
XLA Ops:
  6.5 0.0 copy-start
  6.5 0.0 all-gather.5.cloned.1.call-start
  6.5 1.1 convert_reduce_fusion
  7.6 44.8 %all-reduce = (f32[128]{0:T(128)S(1)}, f32[128]{0:T(128)S(1)}) all-reduce(f32[128]{0:T(128)S(1)} %get-tuple-element.10, f32[128]{0:T(128)S(1)} %get-tuple-element.9), channel_id=1, replica_groups=mesh['row'=32,'col'=16] {'col'}, use_global_device_ids=true, to_apply=%region_3.0 | all-reduce | flops 256 | bytes 2048 | tf_op jit(solution)/shard_map/psum | solution.py:40
  52.4 1.6 fusion.8
  54.0 0.0 all-gather.5.cloned.1.call-update
  54.1 0.0 reduce-scatter.2.cloned.1.call-start
  54.1 87.0 %all-gather.5.cloned.1.call-done = bf16[4096,384]{1,0:T(8,128)(2,1)} async-done(((bf16[128,384]{1,0:T(8,128)(2,1)}), bf16[4096,384]{1,0:T(8,128)(2,1)}) %all-gather.5.cloned.1.call-update) | async-done | bytes 3145744 | tf_op jit(solution)/shard_map/all_gather | solution.py:44
  141.1 0.0 copy-done
  141.1 5.6 %convolution_convert_fusion = bf16[4096,384]{1,0:T(8,128)(2,1)} fusion(bf16[4096,384]{1,0:T(8,128)(2,1)} %all-gather.5.cloned.1.call-done, bf16[384,1,384]{2,0,1:T(8,128)(2,1)S(1)} %copy-done), kind=kOutput, calls=%fused_computation | convolution fusion | flops 1209532416 | bytes 6586368 | tf_op jit(solution)/shard_map/dot_general | solution.py:51
  146.8 0.0 copy-start.2
  146.8 0.0 copy-start.1
  146.8 0.0 reduce-scatter.2.cloned.1.call-update
  146.8 0.0 all-gather.7.cloned.1.call-start
  146.8 97.2 %reduce-scatter.2.cloned.1.call-done = bf16[256,384]{1,0:T(8,128)(2,1)} async-done(((bf16[4096,384]{1,0:T(8,128)(2,1)}), bf16[256,384]{1,0:T(8,128)(2,1)}) %reduce-scatter.2.cloned.1.call-update) | async-done | bytes 196624 | tf_op jit(solution)/shard_map/reduce_scatter | solution.py:50
  244.0 1.1 copy.7
  245.2 0.0 copy-done.2
  245.2 0.7 multiply_convert_fusion
  246.0 0.0 all-gather.7.cloned.1.call-update
  246.0 0.0 all-gather.9.cloned.1.call-start
  246.0 0.6 slice.13
  246.7 0.0 all-gather.9.cloned.1.call-update
  246.7 72.3 %all-gather.7.cloned.1.call-done = bf16[4096,1,128]{0,2,1:T(8,128)(2,1)} async-done(((bf16[256,1,128]{0,2,1:T(8,128)(2,1)}), bf16[4096,1,128]{0,2,1:T(8,128)(2,1)}) %all-gather.7.cloned.1.call-update) | async-done | bytes 1048592 | tf_op jit(solution)/shard_map/all_gather | solution.py:63
  319.0 0.0 copy-done.1
  319.0 4.1 %fusion.17 = (f32[256]{0:T(256)S(1)}, f32[256,4096]{1,0:T(8,128)}) fusion(bf16[4096,1,128]{0,2,1:T(8,128)(2,1)} %all-gather.7.cloned.1.call-done, f32[256,1,3,128]{0,3,2,1:T(8,128)S(1)} %reshape.270, f32[128]{0:T(128)S(1)} %bitcast.40, f32[256]{0:T(256)S(1)} %add_rsqrt_fusion.1, f32[256]{0:T(256)S(1)} %get-tuple-element.18), kind=kOutput, calls=%fused_computation.35 | convolution fusion | flops 270663424 | bytes 5377536 | tf_op jit(solution)/shard_map/qhd,khd->hqk/dot_general | solution.py:30
  323.1 73.0 %all-gather.9.cloned.1.call-done = bf16[4096,1,1,128]{0,3,2,1:T(8,128)(2,1)} async-done(((bf16[256,1,1,128]{0,3,2,1:T(8,128)(2,1)}), bf16[4096,1,1,128]{0,3,2,1:T(8,128)(2,1)}) %all-gather.9.cloned.1.call-update) | async-done | bytes 1048592 | tf_op jit(solution)/shard_map/all_gather | solution.py:64
  396.1 3.4 fusion.2
  399.5 0.8 copy.10
  (7 shorter events, 0.1 us)
Async XLA Ops:
  6.5 134.6 %copy-start = (bf16[384,1,384]{2,0,1:T(8,128)(2,1)S(1)}, bf16[384,1,384]{2,0,1:T(8,128)(2,1)}, u32[]{:S(2)}) copy-start(bf16[384,1,384]{2,0,1:T(8,128)(2,1)} %param.7) | copy-start | bytes 884740
  6.5 134.6 %all-gather.5.cloned.1.call-start = ((), (), s32[]{:S(2)}) async-start(), calls=%async_computation.1 | async-start | bytes 3244032 | tf_op jit(solution)/shard_map/all_gather | solution.py:44
  54.1 189.9 %reduce-scatter.2.cloned.1.call-start = ((), (), s32[]{:S(2)}) async-start(), calls=%async_computation.2 | async-start | bytes 3342336 | tf_op jit(solution)/shard_map/reduce_scatter | solution.py:50
  146.8 98.5 %copy-start.2 = (f32[1,128]{1,0:T(1,128)S(1)}, f32[1,128]{1,0:T(1,128)}, u32[]{:S(2)}) copy-start(f32[1,128]{1,0:T(1,128)} %param.9) | copy-start | bytes 1540
  146.8 172.3 %copy-start.1 = (f32[1,128]{1,0:T(1,128)S(1)}, f32[1,128]{1,0:T(1,128)}, u32[]{:S(2)}) copy-start(f32[1,128]{1,0:T(1,128)} %param.8) | copy-start | bytes 1540
  146.8 172.2 %all-gather.7.cloned.1.call-start = ((), (), s32[]{:S(2)}) async-start(), calls=%async_computation.3 | async-start | bytes 1114112 | tf_op jit(solution)/shard_map/all_gather | solution.py:63
  246.0 150.1 %all-gather.9.cloned.1.call-start = ((), (), s32[]{:S(2)}) async-start(), calls=%async_computation.4 | async-start | bytes 1114112 | tf_op jit(solution)/shard_map/all_gather | solution.py:64
Sparse Core Ops, SparseCore 0:
  54.2 86.9 all-gather.4
  146.9 97.0 reduce-scatter.1
  246.1 72.8 all-gather.6
  320.9 75.1 all-gather.8
where the time goes:
time: 408 us; the launch traced here: 407 us
  waiting for transfers between devices  330 us (81%)
  blocking collectives  44.8 us (11%)
  between operations  13.2 us (3%)
  matrix products  13.1 us (3%)
    reduce_scatter x1, waiting for transfers between devices, body(): lax.psum_scatter(jnp.dot(gathered, flat_weight, preferred_element_type=jn...  97.2 us
    all_gather x1, waiting for transfers between devices, body(): gathered = lax.all_gather(normed, 'row', axis=0, tiled=True)  87 us
    all_gather x1, waiting for transfers between devices, body(): lax.all_gather(own_values, 'col', axis=0, tiled=True)  73 us
    all_gather x1, waiting for transfers between devices, body(): lax.all_gather(own_keys, 'col', axis=0, tiled=True)  72.3 us
    psum x1, blocking collectives, body(): lax.psum((jnp.sum(widened, axis=1), jnp.sum(widened * widened, axis=1)),...  44.8 us
  transfers between devices with their start and end apart: 4, of which 4 were waited for; matrix products, arithmetic and copies ran while one was open for 1% of the time, Pallas kernels for 0%

commit v1 on v0

v1 whole, which is shorter than its diff:
```python
import jax
import jax.numpy as jnp
from jax import lax
from jax.experimental import pallas as pl
from jax.experimental.pallas import tpu as pltpu
from jax.sharding import Mesh, PartitionSpec as P

D = 6144
HS = 128
FB = 384
FD = 4 * FB
TB = 128
EXTRA = 16
EPS = 1e-06

bf16 = jnp.bfloat16
f32 = jnp.float32

AXES = ("y", "zh", "core", "x", "zl")


def pieces(v):
    a = v.astype(bf16)
    r = v - a.astype(f32)
    b = r.astype(bf16)
    c = (r - b.astype(f32)).astype(bf16)
    return a.astype(f32), b.astype(f32), c.astype(f32)


def shift(x, axis, k):
    return lax.ppermute(x, axis, [(i, (i + k) % 4) for i in range(4)])


def call(kernel, out_shape, n_vmem, limit, flops, nbytes, trans=0, name=None):
    return pl.pallas_call(
        kernel,
        out_shape=out_shape,
        in_specs=[pl.BlockSpec(memory_space=pltpu.SMEM)] + [pl.BlockSpec(memory_space=pltpu.VMEM)] * n_vmem,
        out_specs=jax.tree.map(lambda _: pl.BlockSpec(memory_space=pltpu.VMEM), out_shape),
        compiler_params=pltpu.CompilerParams(vmem_limit_bytes=limit << 20),
        cost_estimate=pl.CostEstimate(flops=flops, bytes_accessed=nbytes, transcendentals=trans),
        name=name,
    )


def prep_kernel(s_ref, own_ref, oth_ref, w_ref, sums_ref):
    turn, core = s_ref[0], s_ref[1]
    for k in range(4):
        j = lax.rem(k + turn, 4)
        own, oth = own_ref[j], oth_ref[j]
        w_ref[k * FB : (k + 1) * FB, 0:FB] = jnp.where(core == 0, own, oth)
        w_ref[k * FB : (k + 1) * FB, FB : 2 * FB] = jnp.where(core == 0, oth, own)
    sums_ref[...] = jnp.dot(jnp.ones((8, FD), bf16), w_ref[...], preferred_element_type=f32)


def project_kernel(s_ref, x0, x1, x2, x3, w_ref, sums_ref, out_ref):
    y = s_ref[2]
    ones = jnp.ones((8, 128), f32)
    colsum = sums_ref[0:1, :]
    col_rows = jnp.concatenate(pieces(colsum), axis=0)
    for k, x_ref in enumerate((x0, x1, x2, x3)):
        x = x_ref[...]
        total = jnp.zeros((TB, 128), f32)
        squares = jnp.zeros((TB, 128), f32)
        for i in range(FD // 128):
            t = x[:, i * 128 : (i + 1) * 128].astype(f32)
            total = total + t
            squares = squares + t * t
        mean = jnp.sum(total, axis=1, keepdims=True) * (1.0 / FD)
        nt = (((1,), (1,)), ((), ()))
        s1 = lax.dot_general(ones, total, nt, precision=lax.Precision.HIGHEST, preferred_element_type=f32)
        s2 = lax.dot_general(ones, squares, nt, precision=lax.Precision.HIGHEST, preferred_element_type=f32)
        stats = jnp.concatenate(pieces(s1[0:1]) + pieces(s2[0:1]), axis=0)
        stats = jnp.concatenate([stats, jnp.zeros((6, FB - TB), f32)], axis=1)
        prod = jnp.dot(x, w_ref[...], preferred_element_type=f32) - mean * colsum
        at = lax.rem(y - k + 4, 4)
        for h in range(2):
            out_ref[h * 4 + at, 0:TB, :] = prod[:, h * FB : (h + 1) * FB].astype(bf16)
            out_ref[h * 4 + at, TB : TB + EXTRA, :] = jnp.concatenate(
                [stats, col_rows[:, h * FB : (h + 1) * FB], jnp.zeros((EXTRA - 9, FB), f32)], axis=0
            ).astype(bf16)


def norm_kernel(s_ref, r_ref, qg_ref, kg_ref, q_ref, kv_ref):
    for half in range(2):
        s1, s2, cs = [], [], []
        acc = jnp.zeros((TB, 3 * HS), f32)
        for x in range(4):
            blk = half * 4 + x
            acc = acc + r_ref[blk, 0:TB, :].astype(f32)
            e = r_ref[blk, TB : TB + EXTRA, :].astype(f32)
            s1.append(e[0:1, 0:TB] + e[1:2, 0:TB] + e[2:3, 0:TB])
            s2.append(e[3:4, 0:TB] + e[4:5, 0:TB] + e[5:6, 0:TB])
            cs.append(e[6:7] + e[7:8] + e[8:9])
        mean = (s1[0] + s1[1] + s1[2] + s1[3]) * (1.0 / D)
        var = (s2[0] + s2[1] + s2[2] + s2[3]) * (1.0 / D) - mean * mean
        rows = [s * (1.0 / FD) - mean for s in s1] + [lax.rsqrt(var + EPS)]
        cols = jnp.concatenate(rows + [jnp.zeros((TB - 5, TB), f32)], axis=0).T
        for x in range(4):
            acc = acc + cols[:, x : x + 1] * cs[x]
        proj = acc * cols[:, 4:5]

        def head_norm(v, gain):
            c = v - jnp.mean(v, axis=1, keepdims=True)
            return c * lax.rsqrt(jnp.mean(c * c, axis=1, keepdims=True) + EPS) * gain

        at = slice(half * TB, (half + 1) * TB)
        q_ref[at, :] = head_norm(proj[:, 0:HS], qg_ref[...]).astype(bf16)
        kv_ref[at, 0:HS] = head_norm(proj[:, HS : 2 * HS], kg_ref[...]).astype(bf16)
        kv_ref[at, HS : 2 * HS] = proj[:, 2 * HS : 3 * HS].astype(bf16)


def attend_kernel(s_ref, q0, q1, q2, q3, c0, c1, c2, c3, out_ref):
    zl = s_ref[3]
    kvs = (c0, c1, c2, c3)
    vts = [c[:, HS : 2 * HS].T for c in kvs]
    for j, q_ref in enumerate((q0, q1, q2, q3)):
        q = q_ref[...]
        n = q.shape[0]
        total = jnp.zeros((HS, n), f32)
        denom = jnp.zeros((1, n), f32)
        for c, vt in zip(kvs, vts):
            s = lax.dot_general(c[:, 0:HS], q, (((1,), (1,)), ((), ())), preferred_element_type=f32)
            p = jnp.exp(s * (HS ** -0.5))
            denom = denom + jnp.sum(p, axis=0, keepdims=True)
            total = total + jnp.dot(vt, p.astype(bf16), preferred_element_type=f32)
        at = lax.rem(zl - j + 4, 4)
        out_ref[at, 0:HS, :] = total.astype(bf16)
        out_ref[at, HS : HS + EXTRA, :] = jnp.concatenate(
            pieces(denom) + (jnp.zeros((EXTRA - 3, n), f32),), axis=0
        ).astype(bf16)


def combine_kernel(s_ref, r_ref, out_ref):
    total = jnp.zeros((HS, r_ref.shape[2]), f32)
    denom = jnp.zeros((1, r_ref.shape[2]), f32)
    for j in range(4):
        total = total + r_ref[j, 0:HS, :].astype(f32)
        e = r_ref[j, HS : HS + EXTRA, :].astype(f32)
        denom = denom + (e[0:1] + e[1:2] + e[2:3])
    out_ref[...] = (total / denom).T


def body(tokens, ln_gain, qkv_weight, q_gain, k_gain):
    y, zh, core, zl = (lax.axis_index(a).astype(jnp.int32) for a in ("y", "zh", "core", "zl"))
    where = jnp.stack([lax.rem(zl - zh + 4, 4), core, y, zl])

    parts = [
        lax.ppermute(tokens, ("zh", "zl"), [(a * 4 + b, ((b + k) % 4) * 4 + a) for a in range(4) for b in range(4)])
        for k in range(4)
    ]
    w = (ln_gain[:, None] * qkv_weight.reshape(FB, 3 * HS).astype(f32)).astype(bf16)
    own = jnp.stack([w] + [shift(w, "zl", k) for k in (1, 2, 3)])
    other = lax.ppermute(own, "core", [(0, 1), (1, 0)])
    weights, sums = call(
        prep_kernel,
        (jax.ShapeDtypeStruct((FD, 2 * FB), bf16), jax.ShapeDtypeStruct((8, 2 * FB), f32)),
        2, 24, 2 * 8 * FD * 2 * FB, 4 * FD * 2 * FB, name="prep",
    )(where, own, other)

    x0 = jnp.concatenate(parts, axis=1)
    xs = [x0] + [shift(x0, "y", k) for k in (1, 2, 3)]
    products = call(
        project_kernel,
        jax.ShapeDtypeStruct((8, TB + EXTRA, FB), bf16),
        6, 40, 2 * 4 * TB * FD * 2 * FB, 6 << 20, name="project",
    )(where, *xs, weights, sums)
    received = lax.all_to_all(products, ("core", "x"), split_axis=0, concat_axis=0, tiled=True)
    q, kv = call(
        norm_kernel,
        (jax.ShapeDtypeStruct((2 * TB, HS), bf16), jax.ShapeDtypeStruct((2 * TB, 2 * HS), bf16)),
        3, 24, 10 * 8 * TB * FB, 2 << 20, name="norm",
    )(where, received, q_gain, k_gain)

    qs = [q] + [shift(q, "zl", k) for k in (1, 2, 3)]
    kvs = [kv] + [shift(kv, "x", k) for k in (1, 2, 3)]
    partial = call(
        attend_kernel,
        jax.ShapeDtypeStruct((4, HS + EXTRA, 2 * TB), bf16),
        8, 40, 4 * 1024 * 1024 * HS, 2 << 20, 1 << 20, name="attend",
    )(where, *qs, *kvs)
    gathered = lax.all_to_all(partial, "zl", split_axis=0, concat_axis=0, tiled=True)
    out = call(
        combine_kernel,
        jax.ShapeDtypeStruct((2 * TB, HS), f32),
        1, 16, 8 * HS * 2 * TB, 1 << 20, name="combine",
    )(where, gathered)
    return out.reshape(2 * TB, 1, HS)


def solution(mesh):
    split = Mesh(mesh.devices.reshape(4, 4, 2, 4, 4), AXES)
    row, col = ("y", "zh", "core"), ("x", "zl")
    return jax.shard_map(
        body,
        mesh=split,
        in_specs=(P(row, col), P(col), P(col, row, None), P(row, None), P(row, None)),
        out_specs=P(col, row, None),
        check_vma=False,
    )
```

time: 408 us -> 160 us (0.39)
  the two profiles are of different devices: /device:TPU:24 before, /device:TPU:136 now
where the time goes in v1:
time: 160 us
  starting transfers between devices  80 us (50%)
  waiting for transfers between devices  38.6 us (24%)
  blocking collectives  29.1 us (18%)
  Pallas kernels  9.18 us (6%)
  other arithmetic  2.42 us (2%)
    ppermute x12, starting transfers between devices, shift(): return lax.ppermute(x, axis, [(i, (i + k) % 4) for i in range(4)])  54.1 us
    ppermute x12, waiting for transfers between devices, shift(): return lax.ppermute(x, axis, [(i, (i + k) % 4) for i in range(4)])  31.8 us
    ppermute x4, starting transfers between devices, body(): lax.ppermute(tokens, ('zh', 'zl'), [(a * 4 + b, (b + k) % 4 * 4 + a) for...  24 us
    all_to_all x1, blocking collectives, body(): lax.all_to_all(products, ('core', 'x'), split_axis=0, concat_axis=0, tile...  17.9 us
    all_to_all x1, blocking collectives, body(): lax.all_to_all(partial, 'zl', split_axis=0, concat_axis=0, tiled=True)  11.1 us
    ppermute x4, waiting for transfers between devices, body(): lax.ppermute(tokens, ('zh', 'zl'), [(a * 4 + b, (b + k) % 4 * 4 + a) for...  6.79 us
    pallas_call x1, Pallas kernels, body(): call(project_kernel, jax.ShapeDtypeStruct((8, TB + EXTRA, FB), bf16), 6,...  3.43 us
  transfers between devices with their start and end apart: 17, of which 8 were waited for; matrix products, arithmetic and copies ran while one was open for 1% of the time, Pallas kernels for 1%

profile of v1, /device:TPU:136, one launch (start us, length us, event | category | flops | bytes accessed | tf_op | source)
XLA Modules:
  0.0 159.6 jit_solution(41299786009609773)
XLA Ops:
  0.0 1.1 fusion.3
  1.1 3.8 %collective-permute-start.7 = (bf16[384,384]{1,0:T(8,128)(2,1)S(1)}, bf16[384,384]{1,0:T(8,128)(2,1)S(1)}, u32[]{:S(2)}, u32[]{:S(2)}) collective-permute-start(bf16[384,384]{1,0:T(8,128)(2,1)S(1)} %fusion.3), channel_id=1, source_target_pairs={{0,1},{1,2},{2,3},{3,0},{4,5},{5,6},{6,7},{7,4},{8,9},{9,10},{10,1... | collective-permute-start | bytes 884744 | tf_op jit(solution)/shard_map/ppermute | solution.py:31
  4.9 5.2 %collective-permute-start.8 = (bf16[384,384]{1,0:T(8,128)(2,1)S(1)}, bf16[384,384]{1,0:T(8,128)(2,1)S(1)}, u32[]{:S(2)}, u32[]{:S(2)}) collective-permute-start(bf16[384,384]{1,0:T(8,128)(2,1)S(1)} %fusion.3), channel_id=1, source_target_pairs={{0,2},{1,3},{2,0},{3,1},{4,6},{5,7},{6,4},{7,5},{8,10},{9,11},{10,... | collective-permute-start | bytes 884744 | tf_op jit(solution)/shard_map/ppermute | solution.py:31
  10.1 2.9 %collective-permute-start.9 = (bf16[384,384]{1,0:T(8,128)(2,1)S(1)}, bf16[384,384]{1,0:T(8,128)(2,1)S(1)}, u32[]{:S(2)}, u32[]{:S(2)}) collective-permute-start(bf16[384,384]{1,0:T(8,128)(2,1)S(1)} %fusion.3), channel_id=1, source_target_pairs={{0,3},{1,0},{2,1},{3,2},{4,7},{5,4},{6,5},{7,6},{8,11},{9,8},{10,9... | collective-permute-start | bytes 884744 | tf_op jit(solution)/shard_map/ppermute | solution.py:31
  13.0 1.1 fusion.1
  14.1 1.4 collective-permute-done.7
  15.5 11.8 %collective-permute-done.8 = bf16[384,384]{1,0:T(8,128)(2,1)S(1)} collective-permute-done((bf16[384,384]{1,0:T(8,128)(2,1)S(1)}, bf16[384,384]{1,0:T(8,128)(2,1)S(1)}, u32[]{:S(2)}, u32[]{:S(2)}) %collective-permute-start.8) | collective-permute-done | bytes 294944 | tf_op jit(solution)/shard_map/ppermute | solution.py:31
  27.4 0.0 collective-permute-done.9
  27.4 0.2 pad_maximum_fusion.own_ref
  27.5 1.9 %collective-permute-start.10 = (bf16[4,384,384]{2,1,0:T(8,128)(2,1)S(1)}, bf16[4,384,384]{2,1,0:T(8,128)(2,1)S(1)}, u32[]{:S(2)}, u32[]{:S(2)}) collective-permute-start(bf16[4,384,384]{2,1,0:T(8,128)(2,1)S(1)} %pad_maximum_fusion.own_ref), channel_id=1, source_target_pairs={{0,16},{16,0},{1,17},{17,1},{2,18},{18,2},{3,19},{19,3},{4,20},{20... | collective-permute-start | bytes 3538952 | tf_op jit(solution)/shard_map/ppermute | solution.py:154
  29.5 6.0 %collective-permute-start = (bf16[128,384]{1,0:T(8,128)(2,1)S(1)}, bf16[128,384]{1,0:T(8,128)(2,1)S(1)}, u32[]{:S(2)}, u32[]{:S(2)}) collective-permute-start(bf16[128,384]{1,0:T(8,128)(2,1)S(1)} %copy-done.2), channel_id=1, source_target_pairs={{0,0},{1,32},{2,64},{3,96},{32,1},{33,33},{34,65},{35,97},{64,2},{... | collective-permute-start | bytes 294920 | tf_op jit(solution)/shard_map/ppermute | solution.py:149
  35.5 3.4 %collective-permute-start.1 = (bf16[128,384]{1,0:T(8,128)(2,1)S(1)}, bf16[128,384]{1,0:T(8,128)(2,1)S(1)}, u32[]{:S(2)}, u32[]{:S(2)}) collective-permute-start(bf16[128,384]{1,0:T(8,128)(2,1)S(1)} %copy-done.2), channel_id=1, source_target_pairs={{0,32},{1,64},{2,96},{3,0},{32,33},{33,65},{34,97},{35,1},{64,34},... | collective-permute-start | bytes 294920 | tf_op jit(solution)/shard_map/ppermute | solution.py:149
  38.9 8.7 %collective-permute-start.2 = (bf16[128,384]{1,0:T(8,128)(2,1)S(1)}, bf16[128,384]{1,0:T(8,128)(2,1)S(1)}, u32[]{:S(2)}, u32[]{:S(2)}) collective-permute-start(bf16[128,384]{1,0:T(8,128)(2,1)S(1)} %copy-done.2), channel_id=1, source_target_pairs={{0,64},{1,96},{2,0},{3,32},{32,65},{33,97},{34,1},{35,33},{64,66},... | collective-permute-start | bytes 294920 | tf_op jit(solution)/shard_map/ppermute | solution.py:149
  47.6 5.9 %collective-permute-start.3 = (bf16[128,384]{1,0:T(8,128)(2,1)S(1)}, bf16[128,384]{1,0:T(8,128)(2,1)S(1)}, u32[]{:S(2)}, u32[]{:S(2)}) collective-permute-start(bf16[128,384]{1,0:T(8,128)(2,1)S(1)} %copy-done.2), channel_id=1, source_target_pairs={{0,96},{1,0},{2,32},{3,64},{32,97},{33,1},{34,33},{35,65},{64,98},... | collective-permute-start | bytes 294920 | tf_op jit(solution)/shard_map/ppermute | solution.py:149
  53.5 0.0 collective-permute-done
  53.6 0.0 collective-permute-done.1
  53.6 0.0 collective-permute-done.2
  53.6 6.8 %collective-permute-done.3 = bf16[128,384]{1,0:T(8,128)(2,1)S(1)} collective-permute-done((bf16[128,384]{1,0:T(8,128)(2,1)S(1)}, bf16[128,384]{1,0:T(8,128)(2,1)S(1)}, u32[]{:S(2)}, u32[]{:S(2)}) %collective-permute-start.3) | collective-permute-done | bytes 98336 | tf_op jit(solution)/shard_map/ppermute | solution.py:149
  60.4 3.5 %collective-permute-start.4 = (bf16[128,1536]{1,0:T(8,128)(2,1)S(1)}, bf16[128,1536]{1,0:T(8,128)(2,1)S(1)}, u32[]{:S(2)}, u32[]{:S(2)}) collective-permute-start(bf16[128,1536]{1,0:T(8,128)(2,1)S(1)} %constant_dynamic-update-slice_fusion.x0), channel_id=1, source_target_pairs={{0,128},{128,256},{256,384},{384,0},{1,129},{129,257},{257,385},{3... | collective-permute-start | bytes 1179656 | tf_op jit(solution)/shard_map/ppermute | solution.py:31
  63.9 2.8 %collective-permute-start.5 = (bf16[128,1536]{1,0:T(8,128)(2,1)S(1)}, bf16[128,1536]{1,0:T(8,128)(2,1)S(1)}, u32[]{:S(2)}, u32[]{:S(2)}) collective-permute-start(bf16[128,1536]{1,0:T(8,128)(2,1)S(1)} %constant_dynamic-update-slice_fusion.x0), channel_id=1, source_target_pairs={{0,256},{128,384},{256,0},{384,128},{1,257},{129,385},{257,1},{385... | collective-permute-start | bytes 1179656 | tf_op jit(solution)/shard_map/ppermute | solution.py:31
  66.7 4.4 %collective-permute-start.6 = (bf16[128,1536]{1,0:T(8,128)(2,1)S(1)}, bf16[128,1536]{1,0:T(8,128)(2,1)}, u32[]{:S(2)}, u32[]{:S(2)}) collective-permute-start(bf16[128,1536]{1,0:T(8,128)(2,1)S(1)} %constant_dynamic-update-slice_fusion.x0), channel_id=1, source_target_pairs={{0,384},{128,0},{256,128},{384,256},{1,385},{129,1},{257,129},{385... | collective-permute-start | bytes 1179656 | tf_op jit(solution)/shard_map/ppermute | solution.py:31
  71.1 0.1 pad_add_fusion.s_ref
  71.2 0.0 collective-permute-done.10.oth_ref
  71.2 1.1 prep.1
  72.3 2.0 %collective-permute-done.4.x1 = bf16[128,1536]{1,0:T(8,128)(2,1)S(1)} collective-permute-done((bf16[128,1536]{1,0:T(8,128)(2,1)S(1)}, bf16[128,1536]{1,0:T(8,128)(2,1)S(1)}, u32[]{:S(2)}, u32[]{:S(2)}) %collective-permute-start.4) | collective-permute-done | bytes 393248 | tf_op jit(solution)/shard_map/ppermute | solution.py:31
  74.3 5.1 %collective-permute-done.5.x2 = bf16[128,1536]{1,0:T(8,128)(2,1)S(1)} collective-permute-done((bf16[128,1536]{1,0:T(8,128)(2,1)S(1)}, bf16[128,1536]{1,0:T(8,128)(2,1)S(1)}, u32[]{:S(2)}, u32[]{:S(2)}) %collective-permute-start.5) | collective-permute-done | bytes 393248 | tf_op jit(solution)/shard_map/ppermute | solution.py:31
  79.4 7.2 %collective-permute-done.6.x3 = bf16[128,1536]{1,0:T(8,128)(2,1)} collective-permute-done((bf16[128,1536]{1,0:T(8,128)(2,1)S(1)}, bf16[128,1536]{1,0:T(8,128)(2,1)}, u32[]{:S(2)}, u32[]{:S(2)}) %collective-permute-start.6) | collective-permute-done | bytes 393248 | tf_op jit(solution)/shard_map/ppermute | solution.py:31
  86.6 3.4 %project.1 = bf16[8,144,384]{2,1,0:T(8,128)(2,1)S(1)} custom-call(s32[4]{0:T(128)S(1)} %pad_add_fusion.s_ref, bf16[128,1536]{1,0:T(8,128)(2,1)S(1)} %constant_dynamic-update-slice_fusion.x0, bf16[128,1536]{1,0:T(8,128)(2,1)S(1)} %collective-permute-done.4.x1, bf16[128,1536]{1,0:T(8,128)(2,1)S(1)} %collective-permute-done.5.x2, ...), custom_call_target="tpu_custom_call" | custom-call | flops 1207959552 | bytes 6291456 | tf_op jit(solution)/shard_map/project/pallas_call | solution.py:163
  90.0 0.0 copy-start
  90.0 0.0 copy-start.1
  90.1 17.9 %all_to_all.10.r_ref = bf16[8,144,384]{2,1,0:T(8,128)(2,1)S(1)} all-to-all(bf16[8,144,384]{2,1,0:T(8,128)(2,1)S(1)} %project.1), channel_id=1, replica_groups=mesh['y'=4,'zh'=4,'core'=2,'x'=4,'zl'=4] {'core','x'}, dimensions={0} | all-to-all | bytes 1769472 | tf_op jit(solution)/shard_map/all_to_all | solution.py:168
  108.0 0.0 copy-done.1
  108.0 1.4 norm.1
  109.4 3.8 %collective-permute-start.11 = (bf16[256,128]{1,0:T(8,128)(2,1)S(1)}, bf16[256,128]{1,0:T(8,128)(2,1)S(1)}, u32[]{:S(2)}, u32[]{:S(2)}) collective-permute-start(bf16[256,128]{1,0:T(8,128)(2,1)S(1)} %get-tuple-element.11.q0), channel_id=1, source_target_pairs={{0,1},{1,2},{2,3},{3,0},{4,5},{5,6},{6,7},{7,4},{8,9},{9,10},{10,1... | collective-permute-start | bytes 196616 | tf_op jit(solution)/shard_map/ppermute | solution.py:31
  113.2 2.7 %collective-permute-start.14 = (bf16[256,256]{1,0:T(8,128)(2,1)S(1)}, bf16[256,256]{1,0:T(8,128)(2,1)S(1)}, u32[]{:S(2)}, u32[]{:S(2)}) collective-permute-start(bf16[256,256]{1,0:T(8,128)(2,1)S(1)} %get-tuple-element.12.c0), channel_id=1, source_target_pairs={{0,4},{4,8},{8,12},{12,0},{1,5},{5,9},{9,13},{13,1},{2,6},{6,10},{... | collective-permute-start | bytes 393224 | tf_op jit(solution)/shard_map/ppermute | solution.py:31
  115.9 4.1 %collective-permute-start.15 = (bf16[256,256]{1,0:T(8,128)(2,1)S(1)}, bf16[256,256]{1,0:T(8,128)(2,1)S(1)}, u32[]{:S(2)}, u32[]{:S(2)}) collective-permute-start(bf16[256,256]{1,0:T(8,128)(2,1)S(1)} %get-tuple-element.12.c0), channel_id=1, source_target_pairs={{0,8},{4,12},{8,0},{12,4},{1,9},{5,13},{9,1},{13,5},{2,10},{6,14},... | collective-permute-start | bytes 393224 | tf_op jit(solution)/shard_map/ppermute | solution.py:31
  120.1 2.7 %collective-permute-start.16 = (bf16[256,256]{1,0:T(8,128)(2,1)S(1)}, bf16[256,256]{1,0:T(8,128)(2,1)S(1)}, u32[]{:S(2)}, u32[]{:S(2)}) collective-permute-start(bf16[256,256]{1,0:T(8,128)(2,1)S(1)} %get-tuple-element.12.c0), channel_id=1, source_target_pairs={{0,12},{4,0},{8,4},{12,8},{1,13},{5,1},{9,5},{13,9},{2,14},{6,2},{... | collective-permute-start | bytes 393224 | tf_op jit(solution)/shard_map/ppermute | solution.py:31
  122.8 16.2 %collective-permute-start.12 = (bf16[256,128]{1,0:T(8,128)(2,1)S(1)}, bf16[256,128]{1,0:T(8,128)(2,1)S(1)}, u32[]{:S(2)}, u32[]{:S(2)}) collective-permute-start(bf16[256,128]{1,0:T(8,128)(2,1)S(1)} %get-tuple-element.11.q0), channel_id=1, source_target_pairs={{0,2},{1,3},{2,0},{3,1},{4,6},{5,7},{6,4},{7,5},{8,10},{9,11},{10,... | collective-permute-start | bytes 196616 | tf_op jit(solution)/shard_map/ppermute | solution.py:31
  139.0 0.0 collective-permute-done.11.q1
  139.0 1.9 %collective-permute-start.13 = (bf16[256,128]{1,0:T(8,128)(2,1)S(1)}, bf16[256,128]{1,0:T(8,128)(2,1)S(1)}, u32[]{:S(2)}, u32[]{:S(2)}) collective-permute-start(bf16[256,128]{1,0:T(8,128)(2,1)S(1)} %get-tuple-element.11.q0), channel_id=1, source_target_pairs={{0,3},{1,0},{2,1},{3,2},{4,7},{5,4},{6,5},{7,6},{8,11},{9,8},{10,9... | collective-permute-start | bytes 196616 | tf_op jit(solution)/shard_map/ppermute | solution.py:31
  140.9 0.5 collective-permute-done.12.q2
  141.5 3.7 %collective-permute-done.13.q3 = bf16[256,128]{1,0:T(8,128)(2,1)S(1)} collective-permute-done((bf16[256,128]{1,0:T(8,128)(2,1)S(1)}, bf16[256,128]{1,0:T(8,128)(2,1)S(1)}, u32[]{:S(2)}, u32[]{:S(2)}) %collective-permute-start.13) | collective-permute-done | bytes 65568 | tf_op jit(solution)/shard_map/ppermute | solution.py:31
  145.2 0.0 collective-permute-done.14.c1
  145.2 0.0 collective-permute-done.15.c2
  145.2 0.0 collective-permute-done.16.c3
  145.2 2.0 %attend.1 = bf16[4,144,256]{2,1,0:T(8,128)(2,1)S(1)} custom-call(s32[4]{0:T(128)S(1)} %pad_add_fusion.s_ref, bf16[256,128]{1,0:T(8,128)(2,1)S(1)} %get-tuple-element.11.q0, bf16[256,128]{1,0:T(8,128)(2,1)S(1)} %collective-permute-done.11.q1, bf16[256,128]{1,0:T(8,128)(2,1)S(1)} %collective-permute-done.12.q2, ...), custom_call_target="tpu_custom_call" | custom-call | flops 536870912 | bytes 2097152 | tf_op jit(solution)/shard_map/attend/pallas_call | solution.py:177
  147.2 11.1 %all_to_all.11.r_ref = bf16[4,144,256]{2,1,0:T(8,128)(2,1)S(1)} all-to-all(bf16[4,144,256]{2,1,0:T(8,128)(2,1)S(1)} %attend.1), channel_id=1, replica_groups=mesh['y'=4,'zh'=4,'core'=2,'x'=4,'zl'=4] {'zl'}, dimensions={0} | all-to-all | bytes 589824 | tf_op jit(solution)/shard_map/all_to_all | solution.py:182
  158.3 1.3 combine.1
  (7 shorter events, 0.1 us)
Async XLA Ops:
  1.1 14.5 %collective-permute-start.7 = (bf16[384,384]{1,0:T(8,128)(2,1)S(1)}, bf16[384,384]{1,0:T(8,128)(2,1)S(1)}, u32[]{:S(2)}, u32[]{:S(2)}) collective-permute-start(bf16[384,384]{1,0:T(8,128)(2,1)S(1)} %fusion.3), channel_id=1, source_target_pairs={{0,1},{1,2},{2,3},{3,0},{4,5},{5,6},{6,7},{7,4},{8,9},{9,10},{10,1... | collective-permute-start | bytes 884744 | tf_op jit(solution)/shard_map/ppermute | solution.py:31
  4.9 22.4 %collective-permute-start.8 = (bf16[384,384]{1,0:T(8,128)(2,1)S(1)}, bf16[384,384]{1,0:T(8,128)(2,1)S(1)}, u32[]{:S(2)}, u32[]{:S(2)}) collective-permute-start(bf16[384,384]{1,0:T(8,128)(2,1)S(1)} %fusion.3), channel_id=1, source_target_pairs={{0,2},{1,3},{2,0},{3,1},{4,6},{5,7},{6,4},{7,5},{8,10},{9,11},{10,... | collective-permute-start | bytes 884744 | tf_op jit(solution)/shard_map/ppermute | solution.py:31
  10.1 17.2 %collective-permute-start.9 = (bf16[384,384]{1,0:T(8,128)(2,1)S(1)}, bf16[384,384]{1,0:T(8,128)(2,1)S(1)}, u32[]{:S(2)}, u32[]{:S(2)}) collective-permute-start(bf16[384,384]{1,0:T(8,128)(2,1)S(1)} %fusion.3), channel_id=1, source_target_pairs={{0,3},{1,0},{2,1},{3,2},{4,7},{5,4},{6,5},{7,6},{8,11},{9,8},{10,9... | collective-permute-start | bytes 884744 | tf_op jit(solution)/shard_map/ppermute | solution.py:31
  27.4 2.1 %copy-start.2 = (bf16[128,384]{1,0:T(8,128)(2,1)S(1)}, bf16[128,384]{1,0:T(8,128)(2,1)}, u32[]{:S(2)}) copy-start(bf16[128,384]{1,0:T(8,128)(2,1)} %param.5) | copy-start | bytes 294916
  27.5 43.6 %collective-permute-start.10 = (bf16[4,384,384]{2,1,0:T(8,128)(2,1)S(1)}, bf16[4,384,384]{2,1,0:T(8,128)(2,1)S(1)}, u32[]{:S(2)}, u32[]{:S(2)}) collective-permute-start(bf16[4,384,384]{2,1,0:T(8,128)(2,1)S(1)} %pad_maximum_fusion.own_ref), channel_id=1, source_target_pairs={{0,16},{16,0},{1,17},{17,1},{2,18},{18,2},{3,19},{19,3},{4,20},{20... | collective-permute-start | bytes 3538952 | tf_op jit(solution)/shard_map/ppermute | solution.py:154
  29.5 24.0 %collective-permute-start = (bf16[128,384]{1,0:T(8,128)(2,1)S(1)}, bf16[128,384]{1,0:T(8,128)(2,1)S(1)}, u32[]{:S(2)}, u32[]{:S(2)}) collective-permute-start(bf16[128,384]{1,0:T(8,128)(2,1)S(1)} %copy-done.2), channel_id=1, source_target_pairs={{0,0},{1,32},{2,64},{3,96},{32,1},{33,33},{34,65},{35,97},{64,2},{... | collective-permute-start | bytes 294920 | tf_op jit(solution)/shard_map/ppermute | solution.py:149
  35.5 18.1 %collective-permute-start.1 = (bf16[128,384]{1,0:T(8,128)(2,1)S(1)}, bf16[128,384]{1,0:T(8,128)(2,1)S(1)}, u32[]{:S(2)}, u32[]{:S(2)}) collective-permute-start(bf16[128,384]{1,0:T(8,128)(2,1)S(1)} %copy-done.2), channel_id=1, source_target_pairs={{0,32},{1,64},{2,96},{3,0},{32,33},{33,65},{34,97},{35,1},{64,34},... | collective-permute-start | bytes 294920 | tf_op jit(solution)/shard_map/ppermute | solution.py:149
  38.9 14.7 %collective-permute-start.2 = (bf16[128,384]{1,0:T(8,128)(2,1)S(1)}, bf16[128,384]{1,0:T(8,128)(2,1)S(1)}, u32[]{:S(2)}, u32[]{:S(2)}) collective-permute-start(bf16[128,384]{1,0:T(8,128)(2,1)S(1)} %copy-done.2), channel_id=1, source_target_pairs={{0,64},{1,96},{2,0},{3,32},{32,65},{33,97},{34,1},{35,33},{64,66},... | collective-permute-start | bytes 294920 | tf_op jit(solution)/shard_map/ppermute | solution.py:149
  47.6 12.8 %collective-permute-start.3 = (bf16[128,384]{1,0:T(8,128)(2,1)S(1)}, bf16[128,384]{1,0:T(8,128)(2,1)S(1)}, u32[]{:S(2)}, u32[]{:S(2)}) collective-permute-start(bf16[128,384]{1,0:T(8,128)(2,1)S(1)} %copy-done.2), channel_id=1, source_target_pairs={{0,96},{1,0},{2,32},{3,64},{32,97},{33,1},{34,33},{35,65},{64,98},... | collective-permute-start | bytes 294920 | tf_op jit(solution)/shard_map/ppermute | solution.py:149
  60.4 13.9 %collective-permute-start.4 = (bf16[128,1536]{1,0:T(8,128)(2,1)S(1)}, bf16[128,1536]{1,0:T(8,128)(2,1)S(1)}, u32[]{:S(2)}, u32[]{:S(2)}) collective-permute-start(bf16[128,1536]{1,0:T(8,128)(2,1)S(1)} %constant_dynamic-update-slice_fusion.x0), channel_id=1, source_target_pairs={{0,128},{128,256},{256,384},{384,0},{1,129},{129,257},{257,385},{3... | collective-permute-start | bytes 1179656 | tf_op jit(solution)/shard_map/ppermute | solution.py:31
  63.9 15.5 %collective-permute-start.5 = (bf16[128,1536]{1,0:T(8,128)(2,1)S(1)}, bf16[128,1536]{1,0:T(8,128)(2,1)S(1)}, u32[]{:S(2)}, u32[]{:S(2)}) collective-permute-start(bf16[128,1536]{1,0:T(8,128)(2,1)S(1)} %constant_dynamic-update-slice_fusion.x0), channel_id=1, source_target_pairs={{0,256},{128,384},{256,0},{384,128},{1,257},{129,385},{257,1},{385... | collective-permute-start | bytes 1179656 | tf_op jit(solution)/shard_map/ppermute | solution.py:31
  66.7 19.9 %collective-permute-start.6 = (bf16[128,1536]{1,0:T(8,128)(2,1)S(1)}, bf16[128,1536]{1,0:T(8,128)(2,1)}, u32[]{:S(2)}, u32[]{:S(2)}) collective-permute-start(bf16[128,1536]{1,0:T(8,128)(2,1)S(1)} %constant_dynamic-update-slice_fusion.x0), channel_id=1, source_target_pairs={{0,384},{128,0},{256,128},{384,256},{1,385},{129,1},{257,129},{385... | collective-permute-start | bytes 1179656 | tf_op jit(solution)/shard_map/ppermute | solution.py:31
  90.0 17.9 %copy-start = (f32[1,128]{1,0:T(1,128)S(1)}, f32[1,128]{1,0:T(1,128)}, u32[]{:S(2)}) copy-start(f32[1,128]{1,0:T(1,128)} %qg_ref.1) | copy-start | bytes 1540
  90.0 17.9 %copy-start.1 = (f32[1,128]{1,0:T(1,128)S(1)}, f32[1,128]{1,0:T(1,128)}, u32[]{:S(2)}) copy-start(f32[1,128]{1,0:T(1,128)} %kg_ref.1) | copy-start | bytes 1540
  109.4 29.6 %collective-permute-start.11 = (bf16[256,128]{1,0:T(8,128)(2,1)S(1)}, bf16[256,128]{1,0:T(8,128)(2,1)S(1)}, u32[]{:S(2)}, u32[]{:S(2)}) collective-permute-start(bf16[256,128]{1,0:T(8,128)(2,1)S(1)} %get-tuple-element.11.q0), channel_id=1, source_target_pairs={{0,1},{1,2},{2,3},{3,0},{4,5},{5,6},{6,7},{7,4},{8,9},{9,10},{10,1... | collective-permute-start | bytes 196616 | tf_op jit(solution)/shard_map/ppermute | solution.py:31
  113.2 32.0 %collective-permute-start.14 = (bf16[256,256]{1,0:T(8,128)(2,1)S(1)}, bf16[256,256]{1,0:T(8,128)(2,1)S(1)}, u32[]{:S(2)}, u32[]{:S(2)}) collective-permute-start(bf16[256,256]{1,0:T(8,128)(2,1)S(1)} %get-tuple-element.12.c0), channel_id=1, source_target_pairs={{0,4},{4,8},{8,12},{12,0},{1,5},{5,9},{9,13},{13,1},{2,6},{6,10},{... | collective-permute-start | bytes 393224 | tf_op jit(solution)/shard_map/ppermute | solution.py:31
  115.9 29.2 %collective-permute-start.15 = (bf16[256,256]{1,0:T(8,128)(2,1)S(1)}, bf16[256,256]{1,0:T(8,128)(2,1)S(1)}, u32[]{:S(2)}, u32[]{:S(2)}) collective-permute-start(bf16[256,256]{1,0:T(8,128)(2,1)S(1)} %get-tuple-element.12.c0), channel_id=1, source_target_pairs={{0,8},{4,12},{8,0},{12,4},{1,9},{5,13},{9,1},{13,5},{2,10},{6,14},... | collective-permute-start | bytes 393224 | tf_op jit(solution)/shard_map/ppermute | solution.py:31
  120.1 25.1 %collective-permute-start.16 = (bf16[256,256]{1,0:T(8,128)(2,1)S(1)}, bf16[256,256]{1,0:T(8,128)(2,1)S(1)}, u32[]{:S(2)}, u32[]{:S(2)}) collective-permute-start(bf16[256,256]{1,0:T(8,128)(2,1)S(1)} %get-tuple-element.12.c0), channel_id=1, source_target_pairs={{0,12},{4,0},{8,4},{12,8},{1,13},{5,1},{9,5},{13,9},{2,14},{6,2},{... | collective-permute-start | bytes 393224 | tf_op jit(solution)/shard_map/ppermute | solution.py:31
  122.8 18.7 %collective-permute-start.12 = (bf16[256,128]{1,0:T(8,128)(2,1)S(1)}, bf16[256,128]{1,0:T(8,128)(2,1)S(1)}, u32[]{:S(2)}, u32[]{:S(2)}) collective-permute-start(bf16[256,128]{1,0:T(8,128)(2,1)S(1)} %get-tuple-element.11.q0), channel_id=1, source_target_pairs={{0,2},{1,3},{2,0},{3,1},{4,6},{5,7},{6,4},{7,5},{8,10},{9,11},{10,... | collective-permute-start | bytes 196616 | tf_op jit(solution)/shard_map/ppermute | solution.py:31
  139.0 6.2 %collective-permute-start.13 = (bf16[256,128]{1,0:T(8,128)(2,1)S(1)}, bf16[256,128]{1,0:T(8,128)(2,1)S(1)}, u32[]{:S(2)}, u32[]{:S(2)}) collective-permute-start(bf16[256,128]{1,0:T(8,128)(2,1)S(1)} %get-tuple-element.11.q0), channel_id=1, source_target_pairs={{0,3},{1,0},{2,1},{3,2},{4,7},{5,4},{6,5},{7,6},{8,11},{9,8},{10,9... | collective-permute-start | bytes 196616 | tf_op jit(solution)/shard_map/ppermute | solution.py:31

commit v2 on v1

--- a/solution.py
+++ b/solution.py
@@ -10,6 +10,7 @@
 FB = 384
 FD = 4 * FB
 TB = 128
+QT = 32
 EXTRA = 16
 EPS = 1e-06
 
@@ -17,6 +18,8 @@
 f32 = jnp.float32
 
 AXES = ("y", "zh", "core", "x", "zl")
+GATHER = ("x",)
+REDUCE = ("zl",)
 
 
 def pieces(v):
@@ -31,11 +34,16 @@
     return lax.ppermute(x, axis, [(i, (i + k) % 4) for i in range(4)])
 
 
-def call(kernel, out_shape, n_vmem, limit, flops, nbytes, trans=0, name=None):
+def swap(x, axis, k=1, n=2):
+    return lax.ppermute(x, axis, [(i, i ^ k) for i in range(n)])
+
+
+def call(kernel, out_shape, n_vmem, limit, flops, nbytes, trans=0, name=None, scratch=()):
     return pl.pallas_call(
         kernel,
         out_shape=out_shape,
         in_specs=[pl.BlockSpec(memory_space=pltpu.SMEM)] + [pl.BlockSpec(memory_space=pltpu.VMEM)] * n_vmem,
+        scratch_shapes=scratch,
         out_specs=jax.tree.map(lambda _: pl.BlockSpec(memory_space=pltpu.VMEM), out_shape),
         compiler_params=pltpu.CompilerParams(vmem_limit_bytes=limit << 20),
         cost_estimate=pl.CostEstimate(flops=flops, bytes_accessed=nbytes, transcendentals=trans),
@@ -44,22 +52,27 @@
 
 
 def prep_kernel(s_ref, own_ref, oth_ref, w_ref, sums_ref):
-    turn, core = s_ref[0], s_ref[1]
-    for k in range(4):
-        j = lax.rem(k + turn, 4)
+    core = s_ref[0]
+    for b in range(4):
+        j = s_ref[4 + b]
         own, oth = own_ref[j], oth_ref[j]
-        w_ref[k * FB : (k + 1) * FB, 0:FB] = jnp.where(core == 0, own, oth)
-        w_ref[k * FB : (k + 1) * FB, FB : 2 * FB] = jnp.where(core == 0, oth, own)
+        w_ref[b * FB : (b + 1) * FB, 0:FB] = jnp.where(core == 0, own, oth)
+        w_ref[b * FB : (b + 1) * FB, FB : 2 * FB] = jnp.where(core == 0, oth, own)
     sums_ref[...] = jnp.dot(jnp.ones((8, FD), bf16), w_ref[...], preferred_element_type=f32)
 
 
-def project_kernel(s_ref, x0, x1, x2, x3, w_ref, sums_ref, out_ref):
-    y = s_ref[2]
+def project_kernel(s_ref, x0, x2, x1, x3, w_ref, sums_ref, out_ref, xs_ref):
+    for k, x_ref in ((0, x0), (2, x2), (1, x1), (3, x3)):
+        block = lax.rem(s_ref[1] - k + 4, 4)
+        to = pl.multiple_of(block * QT, QT)
+        for a in range(4):
+            for b in range(4):
+                xs_ref[a, pl.ds(to, QT), b * FB : (b + 1) * FB] = x_ref[a * 4 + b]
     ones = jnp.ones((8, 128), f32)
     colsum = sums_ref[0:1, :]
     col_rows = jnp.concatenate(pieces(colsum), axis=0)
-    for k, x_ref in enumerate((x0, x1, x2, x3)):
-        x = x_ref[...]
+    for at in range(4):
+        x = xs_ref[at]
         total = jnp.zeros((TB, 128), f32)
         squares = jnp.zeros((TB, 128), f32)
         for i in range(FD // 128):
@@ -73,7 +86,6 @@
         stats = jnp.concatenate(pieces(s1[0:1]) + pieces(s2[0:1]), axis=0)
         stats = jnp.concatenate([stats, jnp.zeros((6, FB - TB), f32)], axis=1)
         prod = jnp.dot(x, w_ref[...], preferred_element_type=f32) - mean * colsum
-        at = lax.rem(y - k + 4, 4)
         for h in range(2):
             out_ref[h * 4 + at, 0:TB, :] = prod[:, h * FB : (h + 1) * FB].astype(bf16)
             out_ref[h * 4 + at, TB : TB + EXTRA, :] = jnp.concatenate(
@@ -106,27 +118,33 @@
 
         at = slice(half * TB, (half + 1) * TB)
         q_ref[at, :] = head_norm(proj[:, 0:HS], qg_ref[...]).astype(bf16)
-        kv_ref[at, 0:HS] = head_norm(proj[:, HS : 2 * HS], kg_ref[...]).astype(bf16)
-        kv_ref[at, HS : 2 * HS] = proj[:, 2 * HS : 3 * HS].astype(bf16)
-
-
-def attend_kernel(s_ref, q0, q1, q2, q3, c0, c1, c2, c3, out_ref):
-    zl = s_ref[3]
-    kvs = (c0, c1, c2, c3)
-    vts = [c[:, HS : 2 * HS].T for c in kvs]
-    for j, q_ref in enumerate((q0, q1, q2, q3)):
-        q = q_ref[...]
+        keys = head_norm(proj[:, HS : 2 * HS], kg_ref[...]).astype(bf16)
+        values = proj[:, 2 * HS : 3 * HS].astype(bf16)
+        for x in range(4):
+            kv_ref[x, at, 0:HS] = keys
+            kv_ref[x, at, HS : 2 * HS] = values
+
+
+def attend_kernel(s_ref, q0, q1, q2, q3, kv_ref, out_ref, qs_ref):
+    for k, q_ref in enumerate((q0, q1, q2, q3)):
+        quarter = s_ref[4 + k]
+        for a in range(4):
+            for half in range(2):
+                to = pl.multiple_of(half * TB + quarter * QT, QT)
+                qs_ref[a, pl.ds(to, QT), :] = q_ref[half * TB + a * QT : half * TB + (a + 1) * QT, :]
+    vts = [kv_ref[c, :, HS : 2 * HS].T for c in range(4)]
+    for a in range(4):
+        q = qs_ref[a]
         n = q.shape[0]
         total = jnp.zeros((HS, n), f32)
         denom = jnp.zeros((1, n), f32)
-        for c, vt in zip(kvs, vts):
-            s = lax.dot_general(c[:, 0:HS], q, (((1,), (1,)), ((), ())), preferred_element_type=f32)
+        for c in range(4):
+            s = lax.dot_general(kv_ref[c, :, 0:HS], q, (((1,), (1,)), ((), ())), preferred_element_type=f32)
             p = jnp.exp(s * (HS ** -0.5))
             denom = denom + jnp.sum(p, axis=0, keepdims=True)
-            total = total + jnp.dot(vt, p.astype(bf16), preferred_element_type=f32)
-        at = lax.rem(zl - j + 4, 4)
-        out_ref[at, 0:HS, :] = total.astype(bf16)
-        out_ref[at, HS : HS + EXTRA, :] = jnp.concatenate(
+            total = total + jnp.dot(vts[c], p.astype(bf16), preferred_element_type=f32)
+        out_ref[a, 0:HS, :] = total.astype(bf16)
+        out_ref[a, HS : HS + EXTRA, :] = jnp.concatenate(
             pieces(denom) + (jnp.zeros((EXTRA - 3, n), f32),), axis=0
         ).astype(bf16)
 
@@ -142,44 +160,46 @@
 
 
 def body(tokens, ln_gain, qkv_weight, q_gain, k_gain):
-    y, zh, core, zl = (lax.axis_index(a).astype(jnp.int32) for a in ("y", "zh", "core", "zl"))
-    where = jnp.stack([lax.rem(zl - zh + 4, 4), core, y, zl])
-
-    parts = [
-        lax.ppermute(tokens, ("zh", "zl"), [(a * 4 + b, ((b + k) % 4) * 4 + a) for a in range(4) for b in range(4)])
-        for k in range(4)
-    ]
+    y, core, x = (lax.axis_index(a).astype(jnp.int32) for a in ("y", "core", "x"))
+    where = jnp.stack([core, y, x, x] + [jnp.bitwise_xor(x, k) for k in range(4)])
+
+    x0 = lax.all_to_all(
+        jnp.concatenate([tokens] * 4, axis=0).reshape(16, QT, FB),
+        ("zh",) + GATHER, split_axis=0, concat_axis=0, tiled=True,
+    )
     w = (ln_gain[:, None] * qkv_weight.reshape(FB, 3 * HS).astype(f32)).astype(bf16)
-    own = jnp.stack([w] + [shift(w, "zl", k) for k in (1, 2, 3)])
-    other = lax.ppermute(own, "core", [(0, 1), (1, 0)])
+    own = jnp.stack([w] + [swap(w, "x", k, 4) for k in (1, 2, 3)])
+
+    far = shift(x0, "y", 2)
+    xs = [x0, far, shift(x0, "y", 1), shift(x0, "y", 3)]
+
     weights, sums = call(
         prep_kernel,
         (jax.ShapeDtypeStruct((FD, 2 * FB), bf16), jax.ShapeDtypeStruct((8, 2 * FB), f32)),
         2, 24, 2 * 8 * FD * 2 * FB, 4 * FD * 2 * FB, name="prep",
-    )(where, own, other)
-
-    x0 = jnp.concatenate(parts, axis=1)
-    xs = [x0] + [shift(x0, "y", k) for k in (1, 2, 3)]
+    )(where, own, swap(own, "core"))
     products = call(
         project_kernel,
         jax.ShapeDtypeStruct((8, TB + EXTRA, FB), bf16),
         6, 40, 2 * 4 * TB * FD * 2 * FB, 6 << 20, name="project",
+        scratch=(pltpu.VMEM((4, TB, FD), bf16),),
     )(where, *xs, weights, sums)
-    received = lax.all_to_all(products, ("core", "x"), split_axis=0, concat_axis=0, tiled=True)
+    received = lax.all_to_all(products, ("core",) + REDUCE, split_axis=0, concat_axis=0, tiled=True)
     q, kv = call(
         norm_kernel,
-        (jax.ShapeDtypeStruct((2 * TB, HS), bf16), jax.ShapeDtypeStruct((2 * TB, 2 * HS), bf16)),
+        (jax.ShapeDtypeStruct((2 * TB, HS), bf16), jax.ShapeDtypeStruct((4, 2 * TB, 2 * HS), bf16)),
         3, 24, 10 * 8 * TB * FB, 2 << 20, name="norm",
     )(where, received, q_gain, k_gain)
 
-    qs = [q] + [shift(q, "zl", k) for k in (1, 2, 3)]
-    kvs = [kv] + [shift(kv, "x", k) for k in (1, 2, 3)]
+    qs = [q] + [swap(q, GATHER, k, 4) for k in (1, 2, 3)]
+    kvs = lax.all_to_all(kv, REDUCE, split_axis=0, concat_axis=0, tiled=True)
     partial = call(
         attend_kernel,
         jax.ShapeDtypeStruct((4, HS + EXTRA, 2 * TB), bf16),
-        8, 40, 4 * 1024 * 1024 * HS, 2 << 20, 1 << 20, name="attend",
-    )(where, *qs, *kvs)
-    gathered = lax.all_to_all(partial, "zl", split_axis=0, concat_axis=0, tiled=True)
+        5, 40, 4 * 1024 * 1024 * HS, 2 << 20, 1 << 20, name="attend",
+        scratch=(pltpu.VMEM((4, 2 * TB, HS), bf16),),
+    )(where, *qs, kvs)
+    gathered = lax.all_to_all(partial, GATHER, split_axis=0, concat_axis=0, tiled=True)
     out = call(
         combine_kernel,
         jax.ShapeDtypeStruct((2 * TB, HS), f32),

time: 160 us -> 133 us (0.83)
  the two profiles are of different devices: /device:TPU:136 before, /device:TPU:24 now
where the time goes in v2:
time: 133 us; the launch traced here: 132 us
  starting transfers between devices  53 us (40%)
  blocking collectives  38 us (29%)
  waiting for transfers between devices  28.4 us (21%)
  Pallas kernels  10.2 us (8%)
  other arithmetic  2.28 us (2%)
    all_to_all x1, blocking collectives, body(): lax.all_to_all(products, ('core',) + REDUCE, split_axis=0, concat_axis=0,...  28 us
    ppermute x7, starting transfers between devices, swap(): return lax.ppermute(x, axis, [(i, i ^ k) for i in range(n)])  22.7 us
    all_to_all x1, starting transfers between devices, body(): lax.all_to_all(jnp.concatenate([tokens] * 4, axis=0).reshape(16, QT, FB),...  17.7 us
    ppermute x7, waiting for transfers between devices, swap(): return lax.ppermute(x, axis, [(i, i ^ k) for i in range(n)])  15.1 us
    ppermute x3, waiting for transfers between devices, shift(): return lax.ppermute(x, axis, [(i, (i + k) % 4) for i in range(4)])  13.1 us
    all_to_all x1, blocking collectives, body(): lax.all_to_all(partial, GATHER, split_axis=0, concat_axis=0, tiled=True)  10.1 us
    ppermute x3, starting transfers between devices, shift(): return lax.ppermute(x, axis, [(i, (i + k) % 4) for i in range(4)])  9.15 us
    pallas_call x1, Pallas kernels, body(): call(project_kernel, jax.ShapeDtypeStruct((8, TB + EXTRA, FB), bf16), 6,...  3.67 us
  transfers between devices with their start and end apart: 12, of which 8 were waited for; matrix products, arithmetic and copies ran while one was open for 0% of the time, Pallas kernels for 1%

profile of v2, /device:TPU:24, one launch (start us, length us, event | category | flops | bytes accessed | tf_op | source)
XLA Modules:
  0.0 132.2 jit_solution(17744370742408704243)
XLA Ops:
  0.0 0.0 copy-start.3
  0.0 0.0 copy-start.2
  0.0 1.9 %pad_maximum_fusion.1 = bf16[512,384]{1,0:T(8,128)(2,1)} fusion(bf16[128,384]{1,0:T(8,128)(2,1)} %param.5), kind=kLoop, calls=%fused_computation.7 | loop fusion | flops 1572864 | bytes 491520 | tf_op jit(solution)/shard_map/concatenate | solution.py:167
  1.9 17.7 %all-to-all-start = ((bf16[16,32,384]{2,1,0:T(8,128)(2,1)}), bf16[16,32,384]{2,1,0:T(8,128)(2,1)S(1)}, u32[]{:S(2)}, u32[]{:S(2)}) async-start(bf16[16,32,384]{2,1,0:T(8,128)(2,1)} %bitcast.6), calls=%async_computation | async-start | bytes 786432 | tf_op jit(solution)/shard_map/all_to_all | solution.py:166
  19.5 0.0 copy-done.3
  19.5 0.0 copy-done.2
  19.6 0.1 fusion.3
  19.7 5.3 %collective-permute-start.4 = (bf16[384,384]{1,0:T(8,128)(2,1)S(1)}, bf16[384,384]{1,0:T(8,128)(2,1)S(1)}, u32[]{:S(2)}, u32[]{:S(2)}) collective-permute-start(bf16[384,384]{1,0:T(8,128)(2,1)S(1)} %fusion.3), channel_id=1, source_target_pairs={{0,8},{4,12},{8,0},{12,4},{1,9},{5,13},{9,1},{13,5},{2,10},{6,14},... | collective-permute-start | bytes 884744 | tf_op jit(solution)/shard_map/ppermute | solution.py:38
  25.0 3.1 %collective-permute-start.5 = (bf16[384,384]{1,0:T(8,128)(2,1)S(1)}, bf16[384,384]{1,0:T(8,128)(2,1)S(1)}, u32[]{:S(2)}, u32[]{:S(2)}) collective-permute-start(bf16[384,384]{1,0:T(8,128)(2,1)S(1)} %fusion.3), channel_id=1, source_target_pairs={{0,12},{4,8},{8,4},{12,0},{1,13},{5,9},{9,5},{13,1},{2,14},{6,10},... | collective-permute-start | bytes 884744 | tf_op jit(solution)/shard_map/ppermute | solution.py:38
  28.1 1.9 %collective-permute-start.3 = (bf16[384,384]{1,0:T(8,128)(2,1)S(1)}, bf16[384,384]{1,0:T(8,128)(2,1)S(1)}, u32[]{:S(2)}, u32[]{:S(2)}) collective-permute-start(bf16[384,384]{1,0:T(8,128)(2,1)S(1)} %fusion.3), channel_id=1, source_target_pairs={{0,4},{4,0},{8,12},{12,8},{1,5},{5,1},{9,13},{13,9},{2,6},{6,2},{1... | collective-permute-start | bytes 884744 | tf_op jit(solution)/shard_map/ppermute | solution.py:38
  30.0 0.1 fusion.1
  30.2 4.4 %collective-permute-done.4 = bf16[384,384]{1,0:T(8,128)(2,1)S(1)} collective-permute-done((bf16[384,384]{1,0:T(8,128)(2,1)S(1)}, bf16[384,384]{1,0:T(8,128)(2,1)S(1)}, u32[]{:S(2)}, u32[]{:S(2)}) %collective-permute-start.4) | collective-permute-done | bytes 294944 | tf_op jit(solution)/shard_map/ppermute | solution.py:38
  34.5 6.2 %collective-permute-done.5 = bf16[384,384]{1,0:T(8,128)(2,1)S(1)} collective-permute-done((bf16[384,384]{1,0:T(8,128)(2,1)S(1)}, bf16[384,384]{1,0:T(8,128)(2,1)S(1)}, u32[]{:S(2)}, u32[]{:S(2)}) %collective-permute-start.5) | collective-permute-done | bytes 294944 | tf_op jit(solution)/shard_map/ppermute | solution.py:38
  40.8 0.2 collective-permute-done.3
  41.0 0.2 pad_maximum_fusion.own_ref
  41.1 1.9 %collective-permute-start.6 = (bf16[4,384,384]{2,1,0:T(8,128)(2,1)S(1)}, bf16[4,384,384]{2,1,0:T(8,128)(2,1)S(1)}, u32[]{:S(2)}, u32[]{:S(2)}) collective-permute-start(bf16[4,384,384]{2,1,0:T(8,128)(2,1)S(1)} %pad_maximum_fusion.own_ref), channel_id=1, source_target_pairs={{0,16},{16,0},{1,17},{17,1},{2,18},{18,2},{3,19},{19,3},{4,20},{20... | collective-permute-start | bytes 3538952 | tf_op jit(solution)/shard_map/ppermute | solution.py:38
  43.1 0.0 all-to-all-done.x0
  43.1 3.1 %collective-permute-start = (bf16[16,32,384]{2,1,0:T(8,128)(2,1)S(1)}, bf16[16,32,384]{2,1,0:T(8,128)(2,1)S(1)}, u32[]{:S(2)}, u32[]{:S(2)}) collective-permute-start(bf16[16,32,384]{2,1,0:T(8,128)(2,1)S(1)} %all-to-all-done.x0), channel_id=1, source_target_pairs={{0,256},{128,384},{256,0},{384,128},{1,257},{129,385},{257,1},{385... | collective-permute-start | bytes 1179656 | tf_op jit(solution)/shard_map/ppermute | solution.py:34
  46.2 4.1 %collective-permute-start.1 = (bf16[16,32,384]{2,1,0:T(8,128)(2,1)S(1)}, bf16[16,32,384]{2,1,0:T(8,128)(2,1)S(1)}, u32[]{:S(2)}, u32[]{:S(2)}) collective-permute-start(bf16[16,32,384]{2,1,0:T(8,128)(2,1)S(1)} %all-to-all-done.x0), channel_id=1, source_target_pairs={{0,128},{128,256},{256,384},{384,0},{1,129},{129,257},{257,385},{3... | collective-permute-start | bytes 1179656 | tf_op jit(solution)/shard_map/ppermute | solution.py:34
  50.3 1.9 %collective-permute-start.2 = (bf16[16,32,384]{2,1,0:T(8,128)(2,1)S(1)}, bf16[16,32,384]{2,1,0:T(8,128)(2,1)}, u32[]{:S(2)}, u32[]{:S(2)}) collective-permute-start(bf16[16,32,384]{2,1,0:T(8,128)(2,1)S(1)} %all-to-all-done.x0), channel_id=1, source_target_pairs={{0,384},{128,0},{256,128},{384,256},{1,385},{129,1},{257,129},{385... | collective-permute-start | bytes 1179656 | tf_op jit(solution)/shard_map/ppermute | solution.py:34
  52.3 0.1 stack.42.s_ref
  52.4 0.0 collective-permute-done.6.oth_ref
  52.4 1.1 prep.1
  53.4 5.0 %collective-permute-done.x2 = bf16[16,32,384]{2,1,0:T(8,128)(2,1)S(1)} collective-permute-done((bf16[16,32,384]{2,1,0:T(8,128)(2,1)S(1)}, bf16[16,32,384]{2,1,0:T(8,128)(2,1)S(1)}, u32[]{:S(2)}, u32[]{:S(2)}) %collective-permute-start) | collective-permute-done | bytes 393248 | tf_op jit(solution)/shard_map/ppermute | solution.py:34
  58.4 5.6 %collective-permute-done.1.x1 = bf16[16,32,384]{2,1,0:T(8,128)(2,1)S(1)} collective-permute-done((bf16[16,32,384]{2,1,0:T(8,128)(2,1)S(1)}, bf16[16,32,384]{2,1,0:T(8,128)(2,1)S(1)}, u32[]{:S(2)}, u32[]{:S(2)}) %collective-permute-start.1) | collective-permute-done | bytes 393248 | tf_op jit(solution)/shard_map/ppermute | solution.py:34
  64.0 2.5 %collective-permute-done.2.x3 = bf16[16,32,384]{2,1,0:T(8,128)(2,1)} collective-permute-done((bf16[16,32,384]{2,1,0:T(8,128)(2,1)S(1)}, bf16[16,32,384]{2,1,0:T(8,128)(2,1)}, u32[]{:S(2)}, u32[]{:S(2)}) %collective-permute-start.2) | collective-permute-done | bytes 393248 | tf_op jit(solution)/shard_map/ppermute | solution.py:34
  66.5 3.7 %project.1 = bf16[8,144,384]{2,1,0:T(8,128)(2,1)S(1)} custom-call(s32[8]{0:T(128)S(1)} %stack.42.s_ref, bf16[16,32,384]{2,1,0:T(8,128)(2,1)S(1)} %all-to-all-done.x0, bf16[16,32,384]{2,1,0:T(8,128)(2,1)S(1)} %collective-permute-done.x2, bf16[16,32,384]{2,1,0:T(8,128)(2,1)S(1)} %collective-permute-done.1.x1, bf16[16,32,384]{2,1,0:T(8,128)(2,1)} %collective-permute-done.2.x3, ...), custom_call_target="tpu_custom_call" | custom-call | flops 1207959552 | bytes 6291456 | tf_op jit(solution)/shard_map/project/pallas_call | solution.py:181
  70.2 0.0 copy-start
  70.2 0.0 copy-start.1
  70.2 28.0 %all_to_all.20.r_ref = bf16[8,144,384]{2,1,0:T(8,128)(2,1)S(1)} all-to-all(bf16[8,144,384]{2,1,0:T(8,128)(2,1)S(1)} %project.1), channel_id=1, replica_groups=mesh['y'=4,'zh'=4,'core'=2,'x'=4,'zl'=4] {'core','zl'}, dimensions={0} | all-to-all | bytes 1769472 | tf_op jit(solution)/shard_map/all_to_all | solution.py:187
  98.2 0.0 copy-done
  98.2 0.0 copy-done.1
  98.2 2.2 %norm.1 = (bf16[256,128]{1,0:T(8,128)(2,1)S(1)}, bf16[4,256,256]{2,1,0:T(8,128)(2,1)}) custom-call(s32[8]{0:T(128)S(1)} %stack.42.s_ref, bf16[8,144,384]{2,1,0:T(8,128)(2,1)S(1)} %all_to_all.20.r_ref, f32[1,128]{1,0:T(1,128)S(1)} %copy-done, f32[1,128]{1,0:T(1,128)S(1)} %copy-done.1), custom_call_target="tpu_custom_call" | custom-call | flops 3932160 | bytes 2097152 | tf_op jit(solution)/shard_map/norm/pallas_call | solution.py:188
  100.4 3.5 %all-to-all-start.2 = ((bf16[4,256,256]{2,1,0:T(8,128)(2,1)}), bf16[4,256,256]{2,1,0:T(8,128)(2,1)S(1)}, u32[]{:S(2)}, u32[]{:S(2)}) async-start(bf16[4,256,256]{2,1,0:T(8,128)(2,1)} %get-tuple-element.12), calls=%async_computation.2 | async-start | bytes 1048576 | tf_op jit(solution)/shard_map/all_to_all | solution.py:195
  103.9 2.2 %collective-permute-start.7 = (bf16[256,128]{1,0:T(8,128)(2,1)S(1)}, bf16[256,128]{1,0:T(8,128)(2,1)S(1)}, u32[]{:S(2)}, u32[]{:S(2)}) collective-permute-start(bf16[256,128]{1,0:T(8,128)(2,1)S(1)} %get-tuple-element.11.q0), channel_id=1, source_target_pairs={{0,4},{4,0},{8,12},{12,8},{1,5},{5,1},{9,13},{13,9},{2,6},{6,2},{1... | collective-permute-start | bytes 196616 | tf_op jit(solution)/shard_map/ppermute | solution.py:38
  106.0 5.2 %collective-permute-start.8 = (bf16[256,128]{1,0:T(8,128)(2,1)S(1)}, bf16[256,128]{1,0:T(8,128)(2,1)S(1)}, u32[]{:S(2)}, u32[]{:S(2)}) collective-permute-start(bf16[256,128]{1,0:T(8,128)(2,1)S(1)} %get-tuple-element.11.q0), channel_id=1, source_target_pairs={{0,8},{4,12},{8,0},{12,4},{1,9},{5,13},{9,1},{13,5},{2,10},{6,14},... | collective-permute-start | bytes 196616 | tf_op jit(solution)/shard_map/ppermute | solution.py:38
  111.3 3.0 %collective-permute-start.9 = (bf16[256,128]{1,0:T(8,128)(2,1)S(1)}, bf16[256,128]{1,0:T(8,128)(2,1)S(1)}, u32[]{:S(2)}, u32[]{:S(2)}) collective-permute-start(bf16[256,128]{1,0:T(8,128)(2,1)S(1)} %get-tuple-element.11.q0), channel_id=1, source_target_pairs={{0,12},{4,8},{8,4},{12,0},{1,13},{5,9},{9,5},{13,1},{2,14},{6,10},... | collective-permute-start | bytes 196616 | tf_op jit(solution)/shard_map/ppermute | solution.py:38
  114.3 0.0 collective-permute-done.7.q1
  114.3 0.0 collective-permute-done.8.q2
  114.3 4.3 %collective-permute-done.9.q3 = bf16[256,128]{1,0:T(8,128)(2,1)S(1)} collective-permute-done((bf16[256,128]{1,0:T(8,128)(2,1)S(1)}, bf16[256,128]{1,0:T(8,128)(2,1)S(1)}, u32[]{:S(2)}, u32[]{:S(2)}) %collective-permute-start.9) | collective-permute-done | bytes 65568 | tf_op jit(solution)/shard_map/ppermute | solution.py:38
  118.6 0.2 all-to-all-done.2.kv_ref
  118.9 2.0 %attend.1 = bf16[4,144,256]{2,1,0:T(8,128)(2,1)S(1)} custom-call(s32[8]{0:T(128)S(1)} %stack.42.s_ref, bf16[256,128]{1,0:T(8,128)(2,1)S(1)} %get-tuple-element.11.q0, bf16[256,128]{1,0:T(8,128)(2,1)S(1)} %collective-permute-done.7.q1, bf16[256,128]{1,0:T(8,128)(2,1)S(1)} %collective-permute-done.8.q2, bf16[256,128]{1,0:T(8,128)(2,1)S(1)} %collective-permute-done.9.q3, ...), custom_call_target="tpu_custom_call" | custom-call | flops 536870912 | bytes 2097152 | tf_op jit(solution)/shard_map/attend/pallas_call | solution.py:196
  120.9 10.1 %all_to_all.21.r_ref = bf16[4,144,256]{2,1,0:T(8,128)(2,1)S(1)} all-to-all(bf16[4,144,256]{2,1,0:T(8,128)(2,1)S(1)} %attend.1), channel_id=1, replica_groups=mesh['y'=4,'zh'=4,'core'=2,'x'=4,'zl'=4] {'x'}, dimensions={0} | all-to-all | bytes 589824 | tf_op jit(solution)/shard_map/all_to_all | solution.py:202
  130.9 1.3 combine.1
Async XLA Ops:
  0.0 19.5 %copy-start.3 = (f32[384]{0:T(512)S(1)}, f32[384]{0:T(512)}, u32[]{:S(2)}) copy-start(f32[384]{0:T(512)} %param.6) | copy-start | bytes 4612
  0.0 19.5 %copy-start.2 = (bf16[384,1,384]{2,0,1:T(8,128)(2,1)S(1)}, bf16[384,1,384]{2,0,1:T(8,128)(2,1)}, u32[]{:S(2)}) copy-start(bf16[384,1,384]{2,0,1:T(8,128)(2,1)} %param.7) | copy-start | bytes 884740
  1.9 41.2 %all-to-all-start = ((bf16[16,32,384]{2,1,0:T(8,128)(2,1)}), bf16[16,32,384]{2,1,0:T(8,128)(2,1)S(1)}, u32[]{:S(2)}, u32[]{:S(2)}) async-start(bf16[16,32,384]{2,1,0:T(8,128)(2,1)} %bitcast.6), calls=%async_computation | async-start | bytes 786432 | tf_op jit(solution)/shard_map/all_to_all | solution.py:166
  19.7 14.9 %collective-permute-start.4 = (bf16[384,384]{1,0:T(8,128)(2,1)S(1)}, bf16[384,384]{1,0:T(8,128)(2,1)S(1)}, u32[]{:S(2)}, u32[]{:S(2)}) collective-permute-start(bf16[384,384]{1,0:T(8,128)(2,1)S(1)} %fusion.3), channel_id=1, source_target_pairs={{0,8},{4,12},{8,0},{12,4},{1,9},{5,13},{9,1},{13,5},{2,10},{6,14},... | collective-permute-start | bytes 884744 | tf_op jit(solution)/shard_map/ppermute | solution.py:38
  25.0 15.7 %collective-permute-start.5 = (bf16[384,384]{1,0:T(8,128)(2,1)S(1)}, bf16[384,384]{1,0:T(8,128)(2,1)S(1)}, u32[]{:S(2)}, u32[]{:S(2)}) collective-permute-start(bf16[384,384]{1,0:T(8,128)(2,1)S(1)} %fusion.3), channel_id=1, source_target_pairs={{0,12},{4,8},{8,4},{12,0},{1,13},{5,9},{9,5},{13,1},{2,14},{6,10},... | collective-permute-start | bytes 884744 | tf_op jit(solution)/shard_map/ppermute | solution.py:38
  28.1 12.9 %collective-permute-start.3 = (bf16[384,384]{1,0:T(8,128)(2,1)S(1)}, bf16[384,384]{1,0:T(8,128)(2,1)S(1)}, u32[]{:S(2)}, u32[]{:S(2)}) collective-permute-start(bf16[384,384]{1,0:T(8,128)(2,1)S(1)} %fusion.3), channel_id=1, source_target_pairs={{0,4},{4,0},{8,12},{12,8},{1,5},{5,1},{9,13},{13,9},{2,6},{6,2},{1... | collective-permute-start | bytes 884744 | tf_op jit(solution)/shard_map/ppermute | solution.py:38
  41.1 11.2 %collective-permute-start.6 = (bf16[4,384,384]{2,1,0:T(8,128)(2,1)S(1)}, bf16[4,384,384]{2,1,0:T(8,128)(2,1)S(1)}, u32[]{:S(2)}, u32[]{:S(2)}) collective-permute-start(bf16[4,384,384]{2,1,0:T(8,128)(2,1)S(1)} %pad_maximum_fusion.own_ref), channel_id=1, source_target_pairs={{0,16},{16,0},{1,17},{17,1},{2,18},{18,2},{3,19},{19,3},{4,20},{20... | collective-permute-start | bytes 3538952 | tf_op jit(solution)/shard_map/ppermute | solution.py:38
  43.1 15.3 %collective-permute-start = (bf16[16,32,384]{2,1,0:T(8,128)(2,1)S(1)}, bf16[16,32,384]{2,1,0:T(8,128)(2,1)S(1)}, u32[]{:S(2)}, u32[]{:S(2)}) collective-permute-start(bf16[16,32,384]{2,1,0:T(8,128)(2,1)S(1)} %all-to-all-done.x0), channel_id=1, source_target_pairs={{0,256},{128,384},{256,0},{384,128},{1,257},{129,385},{257,1},{385... | collective-permute-start | bytes 1179656 | tf_op jit(solution)/shard_map/ppermute | solution.py:34
  46.2 17.8 %collective-permute-start.1 = (bf16[16,32,384]{2,1,0:T(8,128)(2,1)S(1)}, bf16[16,32,384]{2,1,0:T(8,128)(2,1)S(1)}, u32[]{:S(2)}, u32[]{:S(2)}) collective-permute-start(bf16[16,32,384]{2,1,0:T(8,128)(2,1)S(1)} %all-to-all-done.x0), channel_id=1, source_target_pairs={{0,128},{128,256},{256,384},{384,0},{1,129},{129,257},{257,385},{3... | collective-permute-start | bytes 1179656 | tf_op jit(solution)/shard_map/ppermute | solution.py:34
  50.3 16.2 %collective-permute-start.2 = (bf16[16,32,384]{2,1,0:T(8,128)(2,1)S(1)}, bf16[16,32,384]{2,1,0:T(8,128)(2,1)}, u32[]{:S(2)}, u32[]{:S(2)}) collective-permute-start(bf16[16,32,384]{2,1,0:T(8,128)(2,1)S(1)} %all-to-all-done.x0), channel_id=1, source_target_pairs={{0,384},{128,0},{256,128},{384,256},{1,385},{129,1},{257,129},{385... | collective-permute-start | bytes 1179656 | tf_op jit(solution)/shard_map/ppermute | solution.py:34
  70.2 28.0 %copy-start = (f32[1,128]{1,0:T(1,128)S(1)}, f32[1,128]{1,0:T(1,128)}, u32[]{:S(2)}) copy-start(f32[1,128]{1,0:T(1,128)} %qg_ref.1) | copy-start | bytes 1540
  70.2 28.0 %copy-start.1 = (f32[1,128]{1,0:T(1,128)S(1)}, f32[1,128]{1,0:T(1,128)}, u32[]{:S(2)}) copy-start(f32[1,128]{1,0:T(1,128)} %kg_ref.1) | copy-start | bytes 1540
  100.4 18.5 %all-to-all-start.2 = ((bf16[4,256,256]{2,1,0:T(8,128)(2,1)}), bf16[4,256,256]{2,1,0:T(8,128)(2,1)S(1)}, u32[]{:S(2)}, u32[]{:S(2)}) async-start(bf16[4,256,256]{2,1,0:T(8,128)(2,1)} %get-tuple-element.12), calls=%async_computation.2 | async-start | bytes 1048576 | tf_op jit(solution)/shard_map/all_to_all | solution.py:195
  103.9 10.4 %collective-permute-start.7 = (bf16[256,128]{1,0:T(8,128)(2,1)S(1)}, bf16[256,128]{1,0:T(8,128)(2,1)S(1)}, u32[]{:S(2)}, u32[]{:S(2)}) collective-permute-start(bf16[256,128]{1,0:T(8,128)(2,1)S(1)} %get-tuple-element.11.q0), channel_id=1, source_target_pairs={{0,4},{4,0},{8,12},{12,8},{1,5},{5,1},{9,13},{13,9},{2,6},{6,2},{1... | collective-permute-start | bytes 196616 | tf_op jit(solution)/shard_map/ppermute | solution.py:38
  106.0 8.3 %collective-permute-start.8 = (bf16[256,128]{1,0:T(8,128)(2,1)S(1)}, bf16[256,128]{1,0:T(8,128)(2,1)S(1)}, u32[]{:S(2)}, u32[]{:S(2)}) collective-permute-start(bf16[256,128]{1,0:T(8,128)(2,1)S(1)} %get-tuple-element.11.q0), channel_id=1, source_target_pairs={{0,8},{4,12},{8,0},{12,4},{1,9},{5,13},{9,1},{13,5},{2,10},{6,14},... | collective-permute-start | bytes 196616 | tf_op jit(solution)/shard_map/ppermute | solution.py:38
  111.3 7.4 %collective-permute-start.9 = (bf16[256,128]{1,0:T(8,128)(2,1)S(1)}, bf16[256,128]{1,0:T(8,128)(2,1)S(1)}, u32[]{:S(2)}, u32[]{:S(2)}) collective-permute-start(bf16[256,128]{1,0:T(8,128)(2,1)S(1)} %get-tuple-element.11.q0), channel_id=1, source_target_pairs={{0,12},{4,8},{8,4},{12,0},{1,13},{5,9},{9,5},{13,1},{2,14},{6,10},... | collective-permute-start | bytes 196616 | tf_op jit(solution)/shard_map/ppermute | solution.py:38

commit v3 on v2

--- a/solution.py
+++ b/solution.py
@@ -17,9 +17,9 @@
 bf16 = jnp.bfloat16
 f32 = jnp.float32
 
-AXES = ("y", "zh", "core", "x", "zl")
-GATHER = ("x",)
-REDUCE = ("zl",)
+AXES = ("y", "zh", "core", "xa", "xb", "zg", "zr")
+GATHER = ("xb", "zg")
+REDUCE = ("xa", "zr")
 
 
 def pieces(v):
@@ -51,6 +51,11 @@
     )
 
 
+def pair_kernel(s_ref, a_ref, b_ref, out_ref):
+    out_ref[0] = a_ref[...]
+    out_ref[1] = b_ref[...]
+
+
 def prep_kernel(s_ref, own_ref, oth_ref, w_ref, sums_ref):
     core = s_ref[0]
     for b in range(4):
@@ -61,46 +66,57 @@
     sums_ref[...] = jnp.dot(jnp.ones((8, FD), bf16), w_ref[...], preferred_element_type=f32)
 
 
-def project_kernel(s_ref, x0, x2, x1, x3, w_ref, sums_ref, out_ref, xs_ref):
-    for k, x_ref in ((0, x0), (2, x2), (1, x1), (3, x3)):
-        block = lax.rem(s_ref[1] - k + 4, 4)
-        to = pl.multiple_of(block * QT, QT)
+def project_kernel(s_ref, xa_ref, xb_ref, w_ref, sums_ref, *refs):
+    *before, out_ref, stats_ref, xs_ref = refs
+    first = 1 if before else 0
+    for k, x_ref in ((first, xa_ref), (first + 2, xb_ref)):
+        high = lax.rem(s_ref[1] - k + 4, 4) // 2
         for a in range(4):
+            to = pl.multiple_of(high * (4 * QT) + a % 2 * (2 * QT) + a // 2 * QT, QT)
             for b in range(4):
-                xs_ref[a, pl.ds(to, QT), b * FB : (b + 1) * FB] = x_ref[a * 4 + b]
+                xs_ref[pl.ds(to, QT), b * FB : (b + 1) * FB] = x_ref[a * 4 + b]
+    x = xs_ref[...]
+    n = x.shape[0]
+    total = jnp.zeros((n, 128), f32)
+    squares = jnp.zeros((n, 128), f32)
+    for i in range(FD // 128):
+        t = x[:, i * 128 : (i + 1) * 128].astype(f32)
+        total = total + t
+        squares = squares + t * t
     ones = jnp.ones((8, 128), f32)
+    nt = (((1,), (1,)), ((), ()))
+    s1 = lax.dot_general(ones, total, nt, precision=lax.Precision.HIGHEST, preferred_element_type=f32)
+    s2 = lax.dot_general(ones, squares, nt, precision=lax.Precision.HIGHEST, preferred_element_type=f32)
+    stats = jnp.concatenate([s1[0:1], s2[0:1], jnp.zeros((6, n), f32)], axis=0)
+    stats_ref[...] = stats
+    mean = jnp.sum(total, axis=1, keepdims=True) * (1.0 / FD)
     colsum = sums_ref[0:1, :]
-    col_rows = jnp.concatenate(pieces(colsum), axis=0)
-    for at in range(4):
-        x = xs_ref[at]
-        total = jnp.zeros((TB, 128), f32)
-        squares = jnp.zeros((TB, 128), f32)
-        for i in range(FD // 128):
-            t = x[:, i * 128 : (i + 1) * 128].astype(f32)
-            total = total + t
-            squares = squares + t * t
-        mean = jnp.sum(total, axis=1, keepdims=True) * (1.0 / FD)
-        nt = (((1,), (1,)), ((), ()))
-        s1 = lax.dot_general(ones, total, nt, precision=lax.Precision.HIGHEST, preferred_element_type=f32)
-        s2 = lax.dot_general(ones, squares, nt, precision=lax.Precision.HIGHEST, preferred_element_type=f32)
-        stats = jnp.concatenate(pieces(s1[0:1]) + pieces(s2[0:1]), axis=0)
-        stats = jnp.concatenate([stats, jnp.zeros((6, FB - TB), f32)], axis=1)
-        prod = jnp.dot(x, w_ref[...], preferred_element_type=f32) - mean * colsum
+    prod = (jnp.dot(x, w_ref[...], preferred_element_type=f32) - mean * colsum).astype(bf16)
+    rows = 2 * QT
+    for a in range(4):
         for h in range(2):
-            out_ref[h * 4 + at, 0:TB, :] = prod[:, h * FB : (h + 1) * FB].astype(bf16)
-            out_ref[h * 4 + at, TB : TB + EXTRA, :] = jnp.concatenate(
-                [stats, col_rows[:, h * FB : (h + 1) * FB], jnp.zeros((EXTRA - 9, FB), f32)], axis=0
-            ).astype(bf16)
-
-
-def norm_kernel(s_ref, r_ref, qg_ref, kg_ref, q_ref, kv_ref):
+            out_ref[h * 4 + a, 0:rows, :] = prod[a * rows : (a + 1) * rows, h * FB : (h + 1) * FB]
+    if before:
+        col_rows = jnp.concatenate(pieces(colsum), axis=0)
+        for a in range(4):
+            at = slice(a * rows, (a + 1) * rows)
+            both = jnp.concatenate([before[0][:, at], stats[:, at]], axis=1)
+            rest = jnp.concatenate(pieces(both[0:1]) + pieces(both[1:2]), axis=0)
+            rest = jnp.concatenate([rest, jnp.zeros((6, FB - TB), f32)], axis=1)
+            for h in range(2):
+                out_ref[h * 4 + a, rows : rows + EXTRA, :] = jnp.concatenate(
+                    [rest, col_rows[:, h * FB : (h + 1) * FB], jnp.zeros((EXTRA - 9, FB), f32)], axis=0
+                ).astype(bf16)
+
+
+def norm_kernel(s_ref, ra_ref, rb_ref, qg_ref, kg_ref, q_ref, kv_ref):
     for half in range(2):
         s1, s2, cs = [], [], []
         acc = jnp.zeros((TB, 3 * HS), f32)
         for x in range(4):
             blk = half * 4 + x
-            acc = acc + r_ref[blk, 0:TB, :].astype(f32)
-            e = r_ref[blk, TB : TB + EXTRA, :].astype(f32)
+            acc = acc + jnp.concatenate([ra_ref[blk], rb_ref[blk, 0 : 2 * QT, :]], axis=0).astype(f32)
+            e = rb_ref[blk, 2 * QT : 2 * QT + EXTRA, :].astype(f32)
             s1.append(e[0:1, 0:TB] + e[1:2, 0:TB] + e[2:3, 0:TB])
             s2.append(e[3:4, 0:TB] + e[4:5, 0:TB] + e[5:6, 0:TB])
             cs.append(e[6:7] + e[7:8] + e[8:9])
@@ -143,8 +159,9 @@
             p = jnp.exp(s * (HS ** -0.5))
             denom = denom + jnp.sum(p, axis=0, keepdims=True)
             total = total + jnp.dot(vts[c], p.astype(bf16), preferred_element_type=f32)
-        out_ref[a, 0:HS, :] = total.astype(bf16)
-        out_ref[a, HS : HS + EXTRA, :] = jnp.concatenate(
+        to = lax.rem(s_ref[1] + a // 2, 2) * 2 + a % 2
+        out_ref[to, 0:HS, :] = total.astype(bf16)
+        out_ref[to, HS : HS + EXTRA, :] = jnp.concatenate(
             pieces(denom) + (jnp.zeros((EXTRA - 3, n), f32),), axis=0
         ).astype(bf16)
 
@@ -156,40 +173,51 @@
         total = total + r_ref[j, 0:HS, :].astype(f32)
         e = r_ref[j, HS : HS + EXTRA, :].astype(f32)
         denom = denom + (e[0:1] + e[1:2] + e[2:3])
-    out_ref[...] = (total / denom).T
+    out_ref[...] = (total * (1.0 / denom)).T
 
 
 def body(tokens, ln_gain, qkv_weight, q_gain, k_gain):
-    y, core, x = (lax.axis_index(a).astype(jnp.int32) for a in ("y", "core", "x"))
-    where = jnp.stack([core, y, x, x] + [jnp.bitwise_xor(x, k) for k in range(4)])
+    y, core, xb, zg = (lax.axis_index(a).astype(jnp.int32) for a in ("y", "core", "xb", "zg"))
+    here = xb * 2 + zg
+    where = jnp.stack([core, y, xb, zg] + [jnp.bitwise_xor(here, k) for k in range(4)])
 
     x0 = lax.all_to_all(
-        jnp.concatenate([tokens] * 4, axis=0).reshape(16, QT, FB),
+        jnp.broadcast_to(tokens.reshape(1, 4, QT, FB), (4, 4, QT, FB)).reshape(16, QT, FB),
         ("zh",) + GATHER, split_axis=0, concat_axis=0, tiled=True,
     )
     w = (ln_gain[:, None] * qkv_weight.reshape(FB, 3 * HS).astype(f32)).astype(bf16)
-    own = jnp.stack([w] + [swap(w, "x", k, 4) for k in (1, 2, 3)])
+    pair = call(
+        pair_kernel, jax.ShapeDtypeStruct((2, FB, 3 * HS), bf16), 2, 16, 10**11, 0, name="pair"
+    )(where, w, swap(w, "zg"))
+    own = jnp.concatenate([pair, swap(pair, "xb")], axis=0)
 
     far = shift(x0, "y", 2)
     xs = [x0, far, shift(x0, "y", 1), shift(x0, "y", 3)]
 
+    own, _ = lax.optimization_barrier((own, x0))
     weights, sums = call(
         prep_kernel,
         (jax.ShapeDtypeStruct((FD, 2 * FB), bf16), jax.ShapeDtypeStruct((8, 2 * FB), f32)),
-        2, 24, 2 * 8 * FD * 2 * FB, 4 * FD * 2 * FB, name="prep",
+        2, 24, 0, 0, name="prep",
     )(where, own, swap(own, "core"))
-    products = call(
-        project_kernel,
-        jax.ShapeDtypeStruct((8, TB + EXTRA, FB), bf16),
-        6, 40, 2 * 4 * TB * FD * 2 * FB, 6 << 20, name="project",
-        scratch=(pltpu.VMEM((4, TB, FD), bf16),),
-    )(where, *xs, weights, sums)
-    received = lax.all_to_all(products, ("core",) + REDUCE, split_axis=0, concat_axis=0, tiled=True)
+    def project(xa, xb, extra, *before):
+        return call(
+            project_kernel,
+            (jax.ShapeDtypeStruct((8, 2 * QT + extra, FB), bf16), jax.ShapeDtypeStruct((8, 8 * QT), f32)),
+            4 + len(before), 40, 10**11 if before else 0, 0, name="project",
+            scratch=(pltpu.VMEM((8 * QT, FD), bf16),),
+        )(where, xa, xb, weights, sums, *before)
+
+    first, stats = project(xs[0], xs[1], 0)
+    second, _ = project(xs[2], xs[3], EXTRA, stats)
+    received = [
+        lax.all_to_all(p, ("core",) + REDUCE, split_axis=0, concat_axis=0, tiled=True) for p in (first, second)
+    ]
     q, kv = call(
         norm_kernel,
         (jax.ShapeDtypeStruct((2 * TB, HS), bf16), jax.ShapeDtypeStruct((4, 2 * TB, 2 * HS), bf16)),
-        3, 24, 10 * 8 * TB * FB, 2 << 20, name="norm",
-    )(where, received, q_gain, k_gain)
+        4, 24, 10 * 8 * TB * FB, 2 << 20, name="norm",
+    )(where, *received, q_gain, k_gain)
 
     qs = [q] + [swap(q, GATHER, k, 4) for k in (1, 2, 3)]
     kvs = lax.all_to_all(kv, REDUCE, split_axis=0, concat_axis=0, tiled=True)
@@ -209,8 +237,8 @@
 
 
 def solution(mesh):
-    split = Mesh(mesh.devices.reshape(4, 4, 2, 4, 4), AXES)
-    row, col = ("y", "zh", "core"), ("x", "zl")
+    split = Mesh(mesh.devices.reshape(4, 4, 2, 2, 2, 2, 2), AXES)
+    row, col = ("y", "zh", "core"), ("xa", "xb", "zg", "zr")
     return jax.shard_map(
         body,
         mesh=split,

time: 133 us -> 132 us (level)
  blocking collectives: 38 us -> 24.7 us
  waiting for transfers between devices: 28.4 us -> 33.7 us
  starting transfers between devices: 53 us -> 55.7 us
  Pallas kernels: 10.2 us -> 12.6 us
  local copies, waits for them, and re-layouts: 0.11 us -> 2.51 us
    all_to_all x1, blocking collectives: 28 us -> 13 us  [body(): lax.all_to_all(p, ('core',) + REDUCE, split_axis=0, concat_axis=0, tiled=...]
    ppermute x3, waiting for transfers between devices: 13.1 us -> 5.23 us  [shift(): return lax.ppermute(x, axis, [(i, (i + k) % 4) for i in range(4)])]
    ppermute x7 -> x6, waiting for transfers between devices: 15.1 us -> 21.9 us  [swap(): return lax.ppermute(x, axis, [(i, i ^ k) for i in range(n)])]
    all_to_all x1 -> x2, waiting for transfers between devices: 0.01 us -> 6.55 us  [the longest x1 6.18 us: body(): lax.all_to_all(p, ('core',) + REDUCE, split_axis=0, concat_axis=0, tiled=...]
    all_to_all x1 -> x2, starting transfers between devices: 17.7 us -> 20.9 us  [the longest x1 14.4 us: body(): lax.all_to_all(jnp.broadcast_to(tokens.reshape(1, 4, QT, FB), (4, 4, QT,...]
    pallas_call x1 -> x3, Pallas kernels: 3.67 us -> 6.03 us  [the longest x2 5.43 us: project(): call(project_kernel, (jax.ShapeDtypeStruct((8, 2 * QT + extra, FB), bf16)...]
    concatenate x1, other arithmetic: 1.86 us -> 0.13 us  [body(): own = jnp.concatenate([pair, swap(pair, 'xb')], axis=0)]
    broadcast_in_dim x0 -> x1, local copies, waits for them, and re-layouts: none -> 1.68 us  [body(): jnp.broadcast_to(tokens.reshape(1, 4, QT, FB), (4, 4, QT, FB))]
  transfers between devices with their start and end apart: 12 -> 12, of which waited for: 8 -> 6; matrix products, arithmetic and copies ran while one was open for 0% -> 1% of each run, Pallas kernels for 1% -> 5%
where the time goes in v3:
time: 132 us; the launch traced here: 131 us
  starting transfers between devices  55.7 us (42%)
  waiting for transfers between devices  33.7 us (26%)
  blocking collectives  24.7 us (19%)
  Pallas kernels  12.6 us (10%)
  local copies, waits for them, and re-layouts  2.51 us (2%)
    ppermute x6, starting transfers between devices, swap(): return lax.ppermute(x, axis, [(i, i ^ k) for i in range(n)])  22.1 us
    ppermute x6, waiting for transfers between devices, swap(): return lax.ppermute(x, axis, [(i, i ^ k) for i in range(n)])  21.9 us
    all_to_all x1, starting transfers between devices, body(): lax.all_to_all(jnp.broadcast_to(tokens.reshape(1, 4, QT, FB), (4, 4, QT,...  14.4 us
    all_to_all x1, blocking collectives, body(): lax.all_to_all(p, ('core',) + REDUCE, split_axis=0, concat_axis=0, tiled=...  13 us
    all_to_all x1, blocking collectives, body(): lax.all_to_all(partial, GATHER, split_axis=0, concat_axis=0, tiled=True)  11.7 us
    ppermute x3, starting transfers between devices, shift(): return lax.ppermute(x, axis, [(i, (i + k) % 4) for i in range(4)])  9.16 us
    all_to_all x1, starting transfers between devices, body(): lax.all_to_all(p, ('core',) + REDUCE, split_axis=0, concat_axis=0, tiled=...  6.53 us
    all_to_all x1, waiting for transfers between devices, body(): lax.all_to_all(p, ('core',) + REDUCE, split_axis=0, concat_axis=0, tiled=...  6.18 us
  transfers between devices with their start and end apart: 12, of which 6 were waited for; matrix products, arithmetic and copies ran while one was open for 1% of the time, Pallas kernels for 5%

profile of v3, /device:TPU:24, one launch (start us, length us, event | category | flops | bytes accessed | tf_op | source)
XLA Modules:
  0.0 130.5 jit_solution(14102519574893066118)
XLA Ops:
  0.0 1.1 fusion.a_ref
  1.1 5.2 %collective-permute-start.1 = (bf16[384,384]{1,0:T(8,128)(2,1)S(1)}, bf16[384,384]{1,0:T(8,128)(2,1)S(1)}, u32[]{:S(2)}, u32[]{:S(2)}) collective-permute-start(bf16[384,384]{1,0:T(8,128)(2,1)S(1)} %fusion.a_ref), channel_id=1, source_target_pairs={{0,2},{2,0},{1,3},{3,1},{4,6},{6,4},{5,7},{7,5},{8,10},{10,8},{9,1... | collective-permute-start | bytes 884744 | tf_op jit(solution)/shard_map/ppermute | solution.py:38
  6.3 1.7 %broadcast_in_dim.9 = bf16[4,4,32,384]{3,2,1,0:T(8,128)(2,1)} broadcast(bf16[4,32,384]{2,1,0:T(8,128)(2,1)} %bitcast.16), dimensions={1,2,3} | broadcast | bytes 491520 | tf_op jit(solution)/shard_map/broadcast_in_dim | solution.py:185
  8.0 14.4 %all-to-all-start = ((bf16[16,32,384]{2,1,0:T(8,128)(2,1)}), bf16[16,32,384]{2,1,0:T(8,128)(2,1)}, u32[]{:S(2)}, u32[]{:S(2)}) async-start(bf16[16,32,384]{2,1,0:T(8,128)(2,1)} %bitcast.9), calls=%async_computation | async-start | bytes 786432 | tf_op jit(solution)/shard_map/all_to_all | solution.py:184
  22.3 0.1 stack.35.s_ref
  22.4 0.0 collective-permute-done.1.b_ref
  22.4 0.6 pair.1
  23.0 3.8 %collective-permute-start.2 = (bf16[2,384,384]{2,1,0:T(8,128)(2,1)S(1)}, bf16[2,384,384]{2,1,0:T(8,128)(2,1)S(1)}, u32[]{:S(2)}, u32[]{:S(2)}) collective-permute-start(bf16[2,384,384]{2,1,0:T(8,128)(2,1)S(1)} %pair.1), channel_id=1, source_target_pairs={{0,4},{4,0},{1,5},{5,1},{2,6},{6,2},{3,7},{7,3},{8,12},{12,8},{9,1... | collective-permute-start | bytes 1769480 | tf_op jit(solution)/shard_map/ppermute | solution.py:38
  26.8 16.0 %collective-permute-done.2 = bf16[2,384,384]{2,1,0:T(8,128)(2,1)S(1)} collective-permute-done((bf16[2,384,384]{2,1,0:T(8,128)(2,1)S(1)}, bf16[2,384,384]{2,1,0:T(8,128)(2,1)S(1)}, u32[]{:S(2)}, u32[]{:S(2)}) %collective-permute-start.2) | collective-permute-done | bytes 589856 | tf_op jit(solution)/shard_map/ppermute | solution.py:38
  42.8 0.1 pad_maximum_fusion.own_ref
  42.9 0.4 all-to-all-done.xa_ref
  43.3 1.9 %collective-permute-start.3 = (bf16[4,384,384]{2,1,0:T(8,128)(2,1)S(1)}, bf16[4,384,384]{2,1,0:T(8,128)(2,1)S(1)}, u32[]{:S(2)}, u32[]{:S(2)}) collective-permute-start(bf16[4,384,384]{2,1,0:T(8,128)(2,1)S(1)} %pad_maximum_fusion.own_ref), channel_id=1, source_target_pairs={{0,16},{16,0},{1,17},{17,1},{2,18},{18,2},{3,19},{19,3},{4,20},{20... | collective-permute-start | bytes 3538952 | tf_op jit(solution)/shard_map/ppermute | solution.py:38
  45.2 3.1 %collective-permute-start = (bf16[16,32,384]{2,1,0:T(8,128)(2,1)}, bf16[16,32,384]{2,1,0:T(8,128)(2,1)S(1)}, u32[]{:S(2)}, u32[]{:S(2)}) collective-permute-start(bf16[16,32,384]{2,1,0:T(8,128)(2,1)} %all-to-all-done.xa_ref), channel_id=1, source_target_pairs={{0,256},{128,384},{256,0},{384,128},{1,257},{129,385},{257,1},{385... | collective-permute-start | bytes 1179656 | tf_op jit(solution)/shard_map/ppermute | solution.py:34
  48.4 4.1 %collective-permute-start.4 = (bf16[16,32,384]{2,1,0:T(8,128)(2,1)}, bf16[16,32,384]{2,1,0:T(8,128)(2,1)}, u32[]{:S(2)}, u32[]{:S(2)}) collective-permute-start(bf16[16,32,384]{2,1,0:T(8,128)(2,1)} %all-to-all-done.xa_ref), channel_id=1, source_target_pairs={{0,128},{128,256},{256,384},{384,0},{1,129},{129,257},{257,385},{3... | collective-permute-start | bytes 1179656 | tf_op jit(solution)/shard_map/ppermute | solution.py:34
  52.5 1.9 %collective-permute-start.5 = (bf16[16,32,384]{2,1,0:T(8,128)(2,1)}, bf16[16,32,384]{2,1,0:T(8,128)(2,1)}, u32[]{:S(2)}, u32[]{:S(2)}) collective-permute-start(bf16[16,32,384]{2,1,0:T(8,128)(2,1)} %all-to-all-done.xa_ref), channel_id=1, source_target_pairs={{0,384},{128,0},{256,128},{384,256},{1,385},{129,1},{257,129},{385... | collective-permute-start | bytes 1179656 | tf_op jit(solution)/shard_map/ppermute | solution.py:34
  54.4 0.0 collective-permute-done.3.oth_ref
  54.4 1.1 prep.1
  55.5 0.0 copy-start
  55.5 5.2 %collective-permute-done.xb_ref = bf16[16,32,384]{2,1,0:T(8,128)(2,1)S(1)} collective-permute-done((bf16[16,32,384]{2,1,0:T(8,128)(2,1)}, bf16[16,32,384]{2,1,0:T(8,128)(2,1)S(1)}, u32[]{:S(2)}, u32[]{:S(2)}) %collective-permute-start) | collective-permute-done | bytes 393248 | tf_op jit(solution)/shard_map/ppermute | solution.py:34
  60.8 3.0 %project.2 = (bf16[8,64,384]{2,1,0:T(8,128)(2,1)}, f32[8,256]{1,0:T(8,128)S(1)}) custom-call(s32[8]{0:T(128)S(1)} %stack.35.s_ref, bf16[16,32,384]{2,1,0:T(8,128)(2,1)} %all-to-all-done.xa_ref, bf16[16,32,384]{2,1,0:T(8,128)(2,1)S(1)} %collective-permute-done.xb_ref, bf16[1536,768]{1,0:T(8,128)(2,1)S(1)} %get-tuple-element.14.w_ref, ...), custom_call_target="tpu_custom_call" | custom-call | tf_op jit(solution)/shard_map/project/pallas_call | solution.py:204
  63.8 0.0 copy-done
  63.8 6.5 %all-to-all-start.1 = ((bf16[8,64,384]{2,1,0:T(8,128)(2,1)}), bf16[8,64,384]{2,1,0:T(8,128)(2,1)S(1)}, u32[]{:S(2)}, u32[]{:S(2)}) async-start(bf16[8,64,384]{2,1,0:T(8,128)(2,1)} %get-tuple-element.16), calls=%async_computation.1 | async-start | bytes 786432 | tf_op jit(solution)/shard_map/all_to_all | solution.py:214
  70.3 0.0 collective-permute-done.4.xa_ref
  70.3 0.0 collective-permute-done.5.xb_ref
  70.3 0.0 copy-start.1
  70.3 0.7 copy-done.1
  71.1 0.0 copy-start.2
  71.1 0.0 copy-start.3
  71.1 2.4 %project.3 = (bf16[8,80,384]{2,1,0:T(8,128)(2,1)S(1)}, f32[8,256]{1,0:T(8,128)}) custom-call(s32[8]{0:T(128)S(1)} %stack.35.s_ref, bf16[16,32,384]{2,1,0:T(8,128)(2,1)} %collective-permute-done.4.xa_ref, bf16[16,32,384]{2,1,0:T(8,128)(2,1)} %collective-permute-done.5.xb_ref, bf16[1536,768]{1,0:T(8,128)(2,1)S(1)} %get-tuple-element.14.w_ref, ...), custom_call_target="tpu_custom_call" | custom-call | flops 99999997952 | tf_op jit(solution)/shard_map/project/pallas_call | solution.py:204
  73.5 6.2 %all-to-all-done.1.ra_ref = bf16[8,64,384]{2,1,0:T(8,128)(2,1)S(1)} async-done(((bf16[8,64,384]{2,1,0:T(8,128)(2,1)}), bf16[8,64,384]{2,1,0:T(8,128)(2,1)S(1)}, u32[]{:S(2)}, u32[]{:S(2)}) %all-to-all-start.1) | async-done | bytes 393248 | tf_op jit(solution)/shard_map/all_to_all | solution.py:214
  79.7 13.0 %all_to_all.25.rb_ref = bf16[8,80,384]{2,1,0:T(8,128)(2,1)S(1)} all-to-all(bf16[8,80,384]{2,1,0:T(8,128)(2,1)S(1)} %get-tuple-element.18), channel_id=1, replica_groups=mesh['y'=4,'zh'=4,'core'=2,'xa'=2,'xb'=2,'zg'=2,'zr'=2] {'core','xa','zr'}, dimensions={0} | all-to-all | bytes 983040 | tf_op jit(solution)/shard_map/all_to_all | solution.py:214
  92.7 0.0 copy-done.2
  92.7 0.0 copy-done.3
  92.7 2.2 %norm.1 = (bf16[256,128]{1,0:T(8,128)(2,1)S(1)}, bf16[4,256,256]{2,1,0:T(8,128)(2,1)}) custom-call(s32[8]{0:T(128)S(1)} %stack.35.s_ref, bf16[8,64,384]{2,1,0:T(8,128)(2,1)S(1)} %all-to-all-done.1.ra_ref, bf16[8,80,384]{2,1,0:T(8,128)(2,1)S(1)} %all_to_all.25.rb_ref, f32[1,128]{1,0:T(1,128)S(1)} %copy-done.2, f32[1,128]{1,0:T(1,128)S(1)} %copy-done.3), custom_call_target="tpu_custom_call" | custom-call | flops 3932160 | bytes 2097152 | tf_op jit(solution)/shard_map/norm/pallas_call | solution.py:216
  94.8 3.5 %all-to-all-start.3 = ((bf16[4,256,256]{2,1,0:T(8,128)(2,1)}), bf16[4,256,256]{2,1,0:T(8,128)(2,1)S(1)}, u32[]{:S(2)}, u32[]{:S(2)}) async-start(bf16[4,256,256]{2,1,0:T(8,128)(2,1)} %get-tuple-element.20), calls=%async_computation.3 | async-start | bytes 1048576 | tf_op jit(solution)/shard_map/all_to_all | solution.py:223
  98.3 6.0 %collective-permute-start.6 = (bf16[256,128]{1,0:T(8,128)(2,1)S(1)}, bf16[256,128]{1,0:T(8,128)(2,1)S(1)}, u32[]{:S(2)}, u32[]{:S(2)}) collective-permute-start(bf16[256,128]{1,0:T(8,128)(2,1)S(1)} %get-tuple-element.19.q0), channel_id=1, source_target_pairs={{0,2},{2,0},{4,6},{6,4},{1,3},{3,1},{5,7},{7,5},{8,10},{10,8},{12,... | collective-permute-start | bytes 196616 | tf_op jit(solution)/shard_map/ppermute | solution.py:38
  104.3 2.8 %collective-permute-start.7 = (bf16[256,128]{1,0:T(8,128)(2,1)S(1)}, bf16[256,128]{1,0:T(8,128)(2,1)S(1)}, u32[]{:S(2)}, u32[]{:S(2)}) collective-permute-start(bf16[256,128]{1,0:T(8,128)(2,1)S(1)} %get-tuple-element.19.q0), channel_id=1, source_target_pairs={{0,4},{2,6},{4,0},{6,2},{1,5},{3,7},{5,1},{7,3},{8,12},{10,14},{12... | collective-permute-start | bytes 196616 | tf_op jit(solution)/shard_map/ppermute | solution.py:38
  107.2 2.5 %collective-permute-start.8 = (bf16[256,128]{1,0:T(8,128)(2,1)S(1)}, bf16[256,128]{1,0:T(8,128)(2,1)S(1)}, u32[]{:S(2)}, u32[]{:S(2)}) collective-permute-start(bf16[256,128]{1,0:T(8,128)(2,1)S(1)} %get-tuple-element.19.q0), channel_id=1, source_target_pairs={{0,6},{2,4},{4,2},{6,0},{1,7},{3,5},{5,3},{7,1},{8,14},{10,12},{12... | collective-permute-start | bytes 196616 | tf_op jit(solution)/shard_map/ppermute | solution.py:38
  109.6 0.0 collective-permute-done.6.q1
  109.6 0.8 collective-permute-done.7.q2
  110.5 5.1 %collective-permute-done.8.q3 = bf16[256,128]{1,0:T(8,128)(2,1)S(1)} collective-permute-done((bf16[256,128]{1,0:T(8,128)(2,1)S(1)}, bf16[256,128]{1,0:T(8,128)(2,1)S(1)}, u32[]{:S(2)}, u32[]{:S(2)}) %collective-permute-start.8) | collective-permute-done | bytes 65568 | tf_op jit(solution)/shard_map/ppermute | solution.py:38
  115.5 0.0 all-to-all-done.3.kv_ref
  115.5 2.0 %attend.1 = bf16[4,144,256]{2,1,0:T(8,128)(2,1)S(1)} custom-call(s32[8]{0:T(128)S(1)} %stack.35.s_ref, bf16[256,128]{1,0:T(8,128)(2,1)S(1)} %get-tuple-element.19.q0, bf16[256,128]{1,0:T(8,128)(2,1)S(1)} %collective-permute-done.6.q1, bf16[256,128]{1,0:T(8,128)(2,1)S(1)} %collective-permute-done.7.q2, bf16[256,128]{1,0:T(8,128)(2,1)S(1)} %collective-permute-done.8.q3, ...), custom_call_target="tpu_custom_call" | custom-call | flops 536870912 | bytes 2097152 | tf_op jit(solution)/shard_map/attend/pallas_call | solution.py:224
  117.5 11.7 %all_to_all.26.r_ref = bf16[4,144,256]{2,1,0:T(8,128)(2,1)S(1)} all-to-all(bf16[4,144,256]{2,1,0:T(8,128)(2,1)S(1)} %attend.1), channel_id=1, replica_groups=mesh['y'=4,'zh'=4,'core'=2,'xa'=2,'xb'=2,'zg'=2,'zr'=2] {'xb','zg'}, dimensions={0} | all-to-all | bytes 589824 | tf_op jit(solution)/shard_map/all_to_all | solution.py:230
  129.2 1.3 %combine.1 = f32[256,128]{1,0:T(8,128)} custom-call(s32[8]{0:T(128)S(1)} %stack.35.s_ref, bf16[4,144,256]{2,1,0:T(8,128)(2,1)S(1)} %all_to_all.26.r_ref), custom_call_target="tpu_custom_call" | custom-call | flops 262144 | bytes 1048576 | tf_op jit(solution)/shard_map/combine/pallas_call | solution.py:231
Async XLA Ops:
  1.1 21.3 %collective-permute-start.1 = (bf16[384,384]{1,0:T(8,128)(2,1)S(1)}, bf16[384,384]{1,0:T(8,128)(2,1)S(1)}, u32[]{:S(2)}, u32[]{:S(2)}) collective-permute-start(bf16[384,384]{1,0:T(8,128)(2,1)S(1)} %fusion.a_ref), channel_id=1, source_target_pairs={{0,2},{2,0},{1,3},{3,1},{4,6},{6,4},{5,7},{7,5},{8,10},{10,8},{9,1... | collective-permute-start | bytes 884744 | tf_op jit(solution)/shard_map/ppermute | solution.py:38
  8.0 35.3 %all-to-all-start = ((bf16[16,32,384]{2,1,0:T(8,128)(2,1)}), bf16[16,32,384]{2,1,0:T(8,128)(2,1)}, u32[]{:S(2)}, u32[]{:S(2)}) async-start(bf16[16,32,384]{2,1,0:T(8,128)(2,1)} %bitcast.9), calls=%async_computation | async-start | bytes 786432 | tf_op jit(solution)/shard_map/all_to_all | solution.py:184
  23.0 19.8 %collective-permute-start.2 = (bf16[2,384,384]{2,1,0:T(8,128)(2,1)S(1)}, bf16[2,384,384]{2,1,0:T(8,128)(2,1)S(1)}, u32[]{:S(2)}, u32[]{:S(2)}) collective-permute-start(bf16[2,384,384]{2,1,0:T(8,128)(2,1)S(1)} %pair.1), channel_id=1, source_target_pairs={{0,4},{4,0},{1,5},{5,1},{2,6},{6,2},{3,7},{7,3},{8,12},{12,8},{9,1... | collective-permute-start | bytes 1769480 | tf_op jit(solution)/shard_map/ppermute | solution.py:38
  43.3 11.1 %collective-permute-start.3 = (bf16[4,384,384]{2,1,0:T(8,128)(2,1)S(1)}, bf16[4,384,384]{2,1,0:T(8,128)(2,1)S(1)}, u32[]{:S(2)}, u32[]{:S(2)}) collective-permute-start(bf16[4,384,384]{2,1,0:T(8,128)(2,1)S(1)} %pad_maximum_fusion.own_ref), channel_id=1, source_target_pairs={{0,16},{16,0},{1,17},{17,1},{2,18},{18,2},{3,19},{19,3},{4,20},{20... | collective-permute-start | bytes 3538952 | tf_op jit(solution)/shard_map/ppermute | solution.py:38
  45.2 15.5 %collective-permute-start = (bf16[16,32,384]{2,1,0:T(8,128)(2,1)}, bf16[16,32,384]{2,1,0:T(8,128)(2,1)S(1)}, u32[]{:S(2)}, u32[]{:S(2)}) collective-permute-start(bf16[16,32,384]{2,1,0:T(8,128)(2,1)} %all-to-all-done.xa_ref), channel_id=1, source_target_pairs={{0,256},{128,384},{256,0},{384,128},{1,257},{129,385},{257,1},{385... | collective-permute-start | bytes 1179656 | tf_op jit(solution)/shard_map/ppermute | solution.py:34
  48.4 21.9 %collective-permute-start.4 = (bf16[16,32,384]{2,1,0:T(8,128)(2,1)}, bf16[16,32,384]{2,1,0:T(8,128)(2,1)}, u32[]{:S(2)}, u32[]{:S(2)}) collective-permute-start(bf16[16,32,384]{2,1,0:T(8,128)(2,1)} %all-to-all-done.xa_ref), channel_id=1, source_target_pairs={{0,128},{128,256},{256,384},{384,0},{1,129},{129,257},{257,385},{3... | collective-permute-start | bytes 1179656 | tf_op jit(solution)/shard_map/ppermute | solution.py:34
  52.5 17.9 %collective-permute-start.5 = (bf16[16,32,384]{2,1,0:T(8,128)(2,1)}, bf16[16,32,384]{2,1,0:T(8,128)(2,1)}, u32[]{:S(2)}, u32[]{:S(2)}) collective-permute-start(bf16[16,32,384]{2,1,0:T(8,128)(2,1)} %all-to-all-done.xa_ref), channel_id=1, source_target_pairs={{0,384},{128,0},{256,128},{384,256},{1,385},{129,1},{257,129},{385... | collective-permute-start | bytes 1179656 | tf_op jit(solution)/shard_map/ppermute | solution.py:34
  55.5 8.2 %copy-start = (f32[8,768]{1,0:T(8,128)}, f32[8,768]{1,0:T(8,128)S(1)}, u32[]{:S(2)}) copy-start(f32[8,768]{1,0:T(8,128)S(1)} %get-tuple-element.15.sums_ref) | copy-start | bytes 73732
  63.8 15.9 %all-to-all-start.1 = ((bf16[8,64,384]{2,1,0:T(8,128)(2,1)}), bf16[8,64,384]{2,1,0:T(8,128)(2,1)S(1)}, u32[]{:S(2)}, u32[]{:S(2)}) async-start(bf16[8,64,384]{2,1,0:T(8,128)(2,1)} %get-tuple-element.16), calls=%async_computation.1 | async-start | bytes 786432 | tf_op jit(solution)/shard_map/all_to_all | solution.py:214
  70.3 0.7 copy-start.1
  71.1 21.6 %copy-start.2 = (f32[1,128]{1,0:T(1,128)S(1)}, f32[1,128]{1,0:T(1,128)}, u32[]{:S(2)}) copy-start(f32[1,128]{1,0:T(1,128)} %qg_ref.1) | copy-start | bytes 1540
  71.1 21.6 %copy-start.3 = (f32[1,128]{1,0:T(1,128)S(1)}, f32[1,128]{1,0:T(1,128)}, u32[]{:S(2)}) copy-start(f32[1,128]{1,0:T(1,128)} %kg_ref.1) | copy-start | bytes 1540
  94.8 20.7 %all-to-all-start.3 = ((bf16[4,256,256]{2,1,0:T(8,128)(2,1)}), bf16[4,256,256]{2,1,0:T(8,128)(2,1)S(1)}, u32[]{:S(2)}, u32[]{:S(2)}) async-start(bf16[4,256,256]{2,1,0:T(8,128)(2,1)} %get-tuple-element.20), calls=%async_computation.3 | async-start | bytes 1048576 | tf_op jit(solution)/shard_map/all_to_all | solution.py:223
  98.3 11.3 %collective-permute-start.6 = (bf16[256,128]{1,0:T(8,128)(2,1)S(1)}, bf16[256,128]{1,0:T(8,128)(2,1)S(1)}, u32[]{:S(2)}, u32[]{:S(2)}) collective-permute-start(bf16[256,128]{1,0:T(8,128)(2,1)S(1)} %get-tuple-element.19.q0), channel_id=1, source_target_pairs={{0,2},{2,0},{4,6},{6,4},{1,3},{3,1},{5,7},{7,5},{8,10},{10,8},{12,... | collective-permute-start | bytes 196616 | tf_op jit(solution)/shard_map/ppermute | solution.py:38
  104.3 6.2 %collective-permute-start.7 = (bf16[256,128]{1,0:T(8,128)(2,1)S(1)}, bf16[256,128]{1,0:T(8,128)(2,1)S(1)}, u32[]{:S(2)}, u32[]{:S(2)}) collective-permute-start(bf16[256,128]{1,0:T(8,128)(2,1)S(1)} %get-tuple-element.19.q0), channel_id=1, source_target_pairs={{0,4},{2,6},{4,0},{6,2},{1,5},{3,7},{5,1},{7,3},{8,12},{10,14},{12... | collective-permute-start | bytes 196616 | tf_op jit(solution)/shard_map/ppermute | solution.py:38
  107.2 8.4 %collective-permute-start.8 = (bf16[256,128]{1,0:T(8,128)(2,1)S(1)}, bf16[256,128]{1,0:T(8,128)(2,1)S(1)}, u32[]{:S(2)}, u32[]{:S(2)}) collective-permute-start(bf16[256,128]{1,0:T(8,128)(2,1)S(1)} %get-tuple-element.19.q0), channel_id=1, source_target_pairs={{0,6},{2,4},{4,2},{6,0},{1,7},{3,5},{5,3},{7,1},{8,14},{10,12},{12... | collective-permute-start | bytes 196616 | tf_op jit(solution)/shard_map/ppermute | solution.py:38

commit v4 on v3

--- a/solution.py
+++ b/solution.py
@@ -13,6 +13,7 @@
 QT = 32
 EXTRA = 16
 EPS = 1e-06
+LOG2E = 1.4426950408889634
 
 bf16 = jnp.bfloat16
 f32 = jnp.float32
@@ -51,18 +52,18 @@
     )
 
 
-def pair_kernel(s_ref, a_ref, b_ref, out_ref):
-    out_ref[0] = a_ref[...]
-    out_ref[1] = b_ref[...]
-
-
-def prep_kernel(s_ref, own_ref, oth_ref, w_ref, sums_ref):
+def copy_kernel(s_ref, x_ref, out_ref):
+    out_ref[...] = x_ref[...]
+
+
+def prep_kernel(s_ref, *refs):
+    own_refs, other_refs, (w_ref, sums_ref) = refs[:4], refs[4:8], refs[8:]
     core = s_ref[0]
-    for b in range(4):
-        j = s_ref[4 + b]
-        own, oth = own_ref[j], oth_ref[j]
-        w_ref[b * FB : (b + 1) * FB, 0:FB] = jnp.where(core == 0, own, oth)
-        w_ref[b * FB : (b + 1) * FB, FB : 2 * FB] = jnp.where(core == 0, oth, own)
+    for j in range(4):
+        to = pl.multiple_of(s_ref[4 + j] * FB, FB)
+        own, oth = own_refs[j][...], other_refs[j][...]
+        w_ref[pl.ds(to, FB), 0:FB] = jnp.where(core == 0, own, oth)
+        w_ref[pl.ds(to, FB), FB : 2 * FB] = jnp.where(core == 0, oth, own)
     sums_ref[...] = jnp.dot(jnp.ones((8, FD), bf16), w_ref[...], preferred_element_type=f32)
 
 
@@ -85,18 +86,22 @@
         squares = squares + t * t
     ones = jnp.ones((8, 128), f32)
     nt = (((1,), (1,)), ((), ()))
-    s1 = lax.dot_general(ones, total, nt, precision=lax.Precision.HIGHEST, preferred_element_type=f32)
-    s2 = lax.dot_general(ones, squares, nt, precision=lax.Precision.HIGHEST, preferred_element_type=f32)
-    stats = jnp.concatenate([s1[0:1], s2[0:1], jnp.zeros((6, n), f32)], axis=0)
+    sums = lax.dot_general(
+        ones, jnp.concatenate([total, squares], axis=0), nt, precision=lax.Precision.HIGHEST, preferred_element_type=f32
+    )
+    stats = jnp.concatenate([sums[0:1, 0:n], sums[0:1, n:], jnp.zeros((6, n), f32)], axis=0)
     stats_ref[...] = stats
     mean = jnp.sum(total, axis=1, keepdims=True) * (1.0 / FD)
     colsum = sums_ref[0:1, :]
     prod = (jnp.dot(x, w_ref[...], preferred_element_type=f32) - mean * colsum).astype(bf16)
     rows = 2 * QT
+    at0 = first * rows
     for a in range(4):
         for h in range(2):
-            out_ref[h * 4 + a, 0:rows, :] = prod[a * rows : (a + 1) * rows, h * FB : (h + 1) * FB]
+            out_ref[h * 4 + a, at0 : at0 + rows, :] = prod[a * rows : (a + 1) * rows, h * FB : (h + 1) * FB]
     if before:
+        for blk in range(8):
+            out_ref[blk, 0:rows, :] = before[1][blk]
         col_rows = jnp.concatenate(pieces(colsum), axis=0)
         for a in range(4):
             at = slice(a * rows, (a + 1) * rows)
@@ -104,19 +109,19 @@
             rest = jnp.concatenate(pieces(both[0:1]) + pieces(both[1:2]), axis=0)
             rest = jnp.concatenate([rest, jnp.zeros((6, FB - TB), f32)], axis=1)
             for h in range(2):
-                out_ref[h * 4 + a, rows : rows + EXTRA, :] = jnp.concatenate(
+                out_ref[h * 4 + a, 2 * rows : 2 * rows + EXTRA, :] = jnp.concatenate(
                     [rest, col_rows[:, h * FB : (h + 1) * FB], jnp.zeros((EXTRA - 9, FB), f32)], axis=0
                 ).astype(bf16)
 
 
-def norm_kernel(s_ref, ra_ref, rb_ref, qg_ref, kg_ref, q_ref, kv_ref):
+def norm_kernel(s_ref, r_ref, qg_ref, kg_ref, q_ref, kv_ref):
     for half in range(2):
         s1, s2, cs = [], [], []
         acc = jnp.zeros((TB, 3 * HS), f32)
         for x in range(4):
             blk = half * 4 + x
-            acc = acc + jnp.concatenate([ra_ref[blk], rb_ref[blk, 0 : 2 * QT, :]], axis=0).astype(f32)
-            e = rb_ref[blk, 2 * QT : 2 * QT + EXTRA, :].astype(f32)
+            acc = acc + r_ref[blk, 0:TB, :].astype(f32)
+            e = r_ref[blk, TB : TB + EXTRA, :].astype(f32)
             s1.append(e[0:1, 0:TB] + e[1:2, 0:TB] + e[2:3, 0:TB])
             s2.append(e[3:4, 0:TB] + e[4:5, 0:TB] + e[5:6, 0:TB])
             cs.append(e[6:7] + e[7:8] + e[8:9])
@@ -156,7 +161,7 @@
         denom = jnp.zeros((1, n), f32)
         for c in range(4):
             s = lax.dot_general(kv_ref[c, :, 0:HS], q, (((1,), (1,)), ((), ())), preferred_element_type=f32)
-            p = jnp.exp(s * (HS ** -0.5))
+            p = jnp.exp2(s * (HS ** -0.5 * LOG2E))
             denom = denom + jnp.sum(p, axis=0, keepdims=True)
             total = total + jnp.dot(vts[c], p.astype(bf16), preferred_element_type=f32)
         to = lax.rem(s_ref[1] + a // 2, 2) * 2 + a % 2
@@ -186,38 +191,37 @@
         ("zh",) + GATHER, split_axis=0, concat_axis=0, tiled=True,
     )
     w = (ln_gain[:, None] * qkv_weight.reshape(FB, 3 * HS).astype(f32)).astype(bf16)
-    pair = call(
-        pair_kernel, jax.ShapeDtypeStruct((2, FB, 3 * HS), bf16), 2, 16, 10**11, 0, name="pair"
-    )(where, w, swap(w, "zg"))
-    own = jnp.concatenate([pair, swap(pair, "xb")], axis=0)
+    near = call(
+        copy_kernel, jax.ShapeDtypeStruct((FB, 3 * HS), bf16), 1, 16, 10**11, 0, name="copy"
+    )(where, swap(w, "zg"))
+    w, near = lax.optimization_barrier((w, near))
+    own = [w, near, swap(w, "xb"), swap(near, "xb")]
 
     far = shift(x0, "y", 2)
     xs = [x0, far, shift(x0, "y", 1), shift(x0, "y", 3)]
 
-    own, _ = lax.optimization_barrier((own, x0))
     weights, sums = call(
         prep_kernel,
         (jax.ShapeDtypeStruct((FD, 2 * FB), bf16), jax.ShapeDtypeStruct((8, 2 * FB), f32)),
-        2, 24, 0, 0, name="prep",
-    )(where, own, swap(own, "core"))
-    def project(xa, xb, extra, *before):
+        8, 24, 0, 0, name="prep",
+    )(where, *own, *[swap(v, "core") for v in own])
+
+    def project(xa, xb, rows, *before):
         return call(
             project_kernel,
-            (jax.ShapeDtypeStruct((8, 2 * QT + extra, FB), bf16), jax.ShapeDtypeStruct((8, 8 * QT), f32)),
-            4 + len(before), 40, 10**11 if before else 0, 0, name="project",
+            (jax.ShapeDtypeStruct((8, rows, FB), bf16), jax.ShapeDtypeStruct((8, 8 * QT), f32)),
+            4 + len(before), 40, 0, 0, name="project",
             scratch=(pltpu.VMEM((8 * QT, FD), bf16),),
         )(where, xa, xb, weights, sums, *before)
 
-    first, stats = project(xs[0], xs[1], 0)
-    second, _ = project(xs[2], xs[3], EXTRA, stats)
-    received = [
-        lax.all_to_all(p, ("core",) + REDUCE, split_axis=0, concat_axis=0, tiled=True) for p in (first, second)
-    ]
+    first, stats = project(xs[0], xs[1], 2 * QT)
+    second, _ = project(xs[2], xs[3], TB + EXTRA, stats, first)
+    received = lax.all_to_all(second, ("core",) + REDUCE, split_axis=0, concat_axis=0, tiled=True)
     q, kv = call(
         norm_kernel,
         (jax.ShapeDtypeStruct((2 * TB, HS), bf16), jax.ShapeDtypeStruct((4, 2 * TB, 2 * HS), bf16)),
-        4, 24, 10 * 8 * TB * FB, 2 << 20, name="norm",
-    )(where, *received, q_gain, k_gain)
+        3, 24, 10 * 8 * TB * FB, 2 << 20, name="norm",
+    )(where, received, q_gain, k_gain)
 
     qs = [q] + [swap(q, GATHER, k, 4) for k in (1, 2, 3)]
     kvs = lax.all_to_all(kv, REDUCE, split_axis=0, concat_axis=0, tiled=True)

time: 132 us -> 126 us (0.955)
  waiting for transfers between devices: 33.7 us -> 18.1 us
  blocking collectives: 24.7 us -> 33.2 us
  starting transfers between devices: 55.7 us -> 59.5 us
  Pallas kernels: 12.6 us -> 11 us
    ppermute x6 -> x10, waiting for transfers between devices: 21.9 us -> 6.46 us  [swap(): return lax.ppermute(x, axis, [(i, i ^ k) for i in range(n)])]
    all_to_all x1, waiting for transfers between devices: 0.37 us -> 10.2 us  [body(): lax.all_to_all(jnp.broadcast_to(tokens.reshape(1, 4, QT, FB), (4, 4, QT,...]
    ppermute x6 -> x10, starting transfers between devices: 22.1 us -> 31.5 us  [swap(): return lax.ppermute(x, axis, [(i, i ^ k) for i in range(n)])]
    all_to_all x1, blocking collectives: 13 us -> 20.9 us  [body(): lax.all_to_all(second, ('core',) + REDUCE, split_axis=0, concat_axis=0, t...]
    all_to_all x1 -> x0, starting transfers between devices: 6.53 us -> none  [body(): lax.all_to_all(p, ('core',) + REDUCE, split_axis=0, concat_axis=0, tiled=...]
    all_to_all x1 -> x0, waiting for transfers between devices: 6.18 us -> none  [body(): lax.all_to_all(p, ('core',) + REDUCE, split_axis=0, concat_axis=0, tiled=...]
    ppermute x3, waiting for transfers between devices: 5.23 us -> 1.43 us  [shift(): return lax.ppermute(x, axis, [(i, (i + k) % 4) for i in range(4)])]
    pallas_call x3, Pallas kernels: 6.03 us -> 4.23 us  [the longest x2 3.66 us: project(): call(project_kernel, (jax.ShapeDtypeStruct((8, rows, FB), bf16), jax.Shap...]
  transfers between devices with their start and end apart: 12 -> 15, of which waited for: 6 -> 5; matrix products, arithmetic and copies ran while one was open for 1% -> 1% of each run, Pallas kernels for 5% -> 3%
where the time goes in v4:
time: 126 us; the launch traced here: 125 us
  starting transfers between devices  59.5 us (47%)
  blocking collectives  33.2 us (26%)
  waiting for transfers between devices  18.1 us (14%)
  Pallas kernels  11 us (9%)
  local copies, waits for them, and re-layouts  1.78 us (1%)
    ppermute x10, starting transfers between devices, swap(): return lax.ppermute(x, axis, [(i, i ^ k) for i in range(n)])  31.5 us
    all_to_all x1, blocking collectives, body(): lax.all_to_all(second, ('core',) + REDUCE, split_axis=0, concat_axis=0, t...  20.9 us
    all_to_all x1, starting transfers between devices, body(): lax.all_to_all(jnp.broadcast_to(tokens.reshape(1, 4, QT, FB), (4, 4, QT,...  14.3 us
    all_to_all x1, blocking collectives, body(): lax.all_to_all(partial, GATHER, split_axis=0, concat_axis=0, tiled=True)  12.3 us
    all_to_all x1, waiting for transfers between devices, body(): lax.all_to_all(jnp.broadcast_to(tokens.reshape(1, 4, QT, FB), (4, 4, QT,...  10.2 us
    ppermute x3, starting transfers between devices, shift(): return lax.ppermute(x, axis, [(i, (i + k) % 4) for i in range(4)])  10.2 us
    ppermute x10, waiting for transfers between devices, swap(): return lax.ppermute(x, axis, [(i, i ^ k) for i in range(n)])  6.46 us
    pallas_call x2, Pallas kernels, project(): call(project_kernel, (jax.ShapeDtypeStruct((8, rows, FB), bf16), jax.Shap...  3.66 us
  transfers between devices with their start and end apart: 15, of which 5 were waited for; matrix products, arithmetic and copies ran while one was open for 1% of the time, Pallas kernels for 3%

profile of v4, /device:TPU:24, one launch (start us, length us, event | category | flops | bytes accessed | tf_op | source)
XLA Modules:
  0.0 124.8 jit_solution(15317008178916509038)
XLA Ops:
  0.0 1.1 fusion.refs_0_
  1.1 5.2 %collective-permute-start.2 = (bf16[384,384]{1,0:T(8,128)(2,1)S(1)}, bf16[384,384]{1,0:T(8,128)(2,1)S(1)}, u32[]{:S(2)}, u32[]{:S(2)}) collective-permute-start(bf16[384,384]{1,0:T(8,128)(2,1)S(1)} %fusion.refs_0_), channel_id=1, source_target_pairs={{0,2},{2,0},{1,3},{3,1},{4,6},{6,4},{5,7},{7,5},{8,10},{10,8},{9,1... | collective-permute-start | bytes 884744 | tf_op jit(solution)/shard_map/ppermute | solution.py:39
  6.3 1.7 %broadcast_in_dim.9 = bf16[4,4,32,384]{3,2,1,0:T(8,128)(2,1)} broadcast(bf16[4,32,384]{2,1,0:T(8,128)(2,1)} %bitcast.16), dimensions={1,2,3} | broadcast | bytes 491520 | tf_op jit(solution)/shard_map/broadcast_in_dim | solution.py:190
  8.0 14.3 %all-to-all-start = ((bf16[16,32,384]{2,1,0:T(8,128)(2,1)}), bf16[16,32,384]{2,1,0:T(8,128)(2,1)S(1)}, u32[]{:S(2)}, u32[]{:S(2)}) async-start(bf16[16,32,384]{2,1,0:T(8,128)(2,1)} %bitcast.9), calls=%async_computation | async-start | bytes 786432 | tf_op jit(solution)/shard_map/all_to_all | solution.py:189
  22.3 0.1 stack.35.s_ref
  22.4 0.0 collective-permute-done.2.x_ref
  22.4 0.6 copy.8.refs_1_
  23.0 1.9 %collective-permute-start.5 = (bf16[384,384]{1,0:T(8,128)(2,1)S(1)}, bf16[384,384]{1,0:T(8,128)(2,1)S(1)}, u32[]{:S(2)}, u32[]{:S(2)}) collective-permute-start(bf16[384,384]{1,0:T(8,128)(2,1)S(1)} %fusion.refs_0_), channel_id=1, source_target_pairs={{0,16},{16,0},{1,17},{17,1},{2,18},{18,2},{3,19},{19,3},{4,20},{20... | collective-permute-start | bytes 884744 | tf_op jit(solution)/shard_map/ppermute | solution.py:39
  24.9 3.8 %collective-permute-start.3 = (bf16[384,384]{1,0:T(8,128)(2,1)S(1)}, bf16[384,384]{1,0:T(8,128)(2,1)S(1)}, u32[]{:S(2)}, u32[]{:S(2)}) collective-permute-start(bf16[384,384]{1,0:T(8,128)(2,1)S(1)} %fusion.refs_0_), channel_id=1, source_target_pairs={{0,4},{4,0},{1,5},{5,1},{2,6},{6,2},{3,7},{7,3},{8,12},{12,8},{9,1... | collective-permute-start | bytes 884744 | tf_op jit(solution)/shard_map/ppermute | solution.py:39
  28.7 2.1 %collective-permute-start.6 = (bf16[384,384]{1,0:T(8,128)(2,1)S(1)}, bf16[384,384]{1,0:T(8,128)(2,1)S(1)}, u32[]{:S(2)}, u32[]{:S(2)}) collective-permute-start(bf16[384,384]{1,0:T(8,128)(2,1)S(1)} %copy.8.refs_1_), channel_id=1, source_target_pairs={{0,16},{16,0},{1,17},{17,1},{2,18},{18,2},{3,19},{19,3},{4,20},{20... | collective-permute-start | bytes 884744 | tf_op jit(solution)/shard_map/ppermute | solution.py:39
  30.9 2.2 %collective-permute-start.4 = (bf16[384,384]{1,0:T(8,128)(2,1)S(1)}, bf16[384,384]{1,0:T(8,128)(2,1)S(1)}, u32[]{:S(2)}, u32[]{:S(2)}) collective-permute-start(bf16[384,384]{1,0:T(8,128)(2,1)S(1)} %copy.8.refs_1_), channel_id=1, source_target_pairs={{0,4},{4,0},{1,5},{5,1},{2,6},{6,2},{3,7},{7,3},{8,12},{12,8},{9,1... | collective-permute-start | bytes 884744 | tf_op jit(solution)/shard_map/ppermute | solution.py:39
  33.1 10.2 %all-to-all-done.xa_ref = bf16[16,32,384]{2,1,0:T(8,128)(2,1)S(1)} async-done(((bf16[16,32,384]{2,1,0:T(8,128)(2,1)}), bf16[16,32,384]{2,1,0:T(8,128)(2,1)S(1)}, u32[]{:S(2)}, u32[]{:S(2)}) %all-to-all-start) | async-done | bytes 393248 | tf_op jit(solution)/shard_map/all_to_all | solution.py:189
  43.3 3.1 %collective-permute-start.9 = (bf16[16,32,384]{2,1,0:T(8,128)(2,1)S(1)}, bf16[16,32,384]{2,1,0:T(8,128)(2,1)S(1)}, u32[]{:S(2)}, u32[]{:S(2)}) collective-permute-start(bf16[16,32,384]{2,1,0:T(8,128)(2,1)S(1)} %all-to-all-done.xa_ref), channel_id=1, source_target_pairs={{0,256},{128,384},{256,0},{384,128},{1,257},{129,385},{257,1},{385... | collective-permute-start | bytes 1179656 | tf_op jit(solution)/shard_map/ppermute | solution.py:35
  46.4 0.0 collective-permute-done.5.refs_4_
  46.4 1.9 %collective-permute-start.1 = (bf16[16,32,384]{2,1,0:T(8,128)(2,1)S(1)}, bf16[16,32,384]{2,1,0:T(8,128)(2,1)S(1)}, u32[]{:S(2)}, u32[]{:S(2)}) collective-permute-start(bf16[16,32,384]{2,1,0:T(8,128)(2,1)S(1)} %all-to-all-done.xa_ref), channel_id=1, source_target_pairs={{0,384},{128,0},{256,128},{384,256},{1,385},{129,1},{257,129},{385... | collective-permute-start | bytes 1179656 | tf_op jit(solution)/shard_map/ppermute | solution.py:35
  48.3 0.0 collective-permute-done.3.refs_2_
  48.4 5.1 %collective-permute-start = (bf16[16,32,384]{2,1,0:T(8,128)(2,1)S(1)}, bf16[16,32,384]{2,1,0:T(8,128)(2,1)S(1)}, u32[]{:S(2)}, u32[]{:S(2)}) collective-permute-start(bf16[16,32,384]{2,1,0:T(8,128)(2,1)S(1)} %all-to-all-done.xa_ref), channel_id=1, source_target_pairs={{0,128},{128,256},{256,384},{384,0},{1,129},{129,257},{257,385},{3... | collective-permute-start | bytes 1179656 | tf_op jit(solution)/shard_map/ppermute | solution.py:35
  53.5 0.0 collective-permute-done.6.refs_5_
  53.5 1.9 %collective-permute-start.7 = (bf16[384,384]{1,0:T(8,128)(2,1)S(1)}, bf16[384,384]{1,0:T(8,128)(2,1)S(1)}, u32[]{:S(2)}, u32[]{:S(2)}) collective-permute-start(bf16[384,384]{1,0:T(8,128)(2,1)S(1)} %collective-permute-done.3.refs_2_), channel_id=1, source_target_pairs={{0,16},{16,0},{1,17},{17,1},{2,18},{18,2},{3,19},{19,3},{4,20},{20... | collective-permute-start | bytes 884744 | tf_op jit(solution)/shard_map/ppermute | solution.py:39
  55.4 0.0 collective-permute-done.4.refs_3_
  55.4 2.4 %collective-permute-start.8 = (bf16[384,384]{1,0:T(8,128)(2,1)S(1)}, bf16[384,384]{1,0:T(8,128)(2,1)S(1)}, u32[]{:S(2)}, u32[]{:S(2)}) collective-permute-start(bf16[384,384]{1,0:T(8,128)(2,1)S(1)} %collective-permute-done.4.refs_3_), channel_id=1, source_target_pairs={{0,16},{16,0},{1,17},{17,1},{2,18},{18,2},{3,19},{19,3},{4,20},{20... | collective-permute-start | bytes 884744 | tf_op jit(solution)/shard_map/ppermute | solution.py:39
  57.9 0.0 collective-permute-done.7.refs_6_
  57.9 1.2 collective-permute-done.8.refs_7_
  59.1 1.3 %prep.1 = (bf16[1536,768]{1,0:T(8,128)(2,1)S(1)}, f32[8,768]{1,0:T(8,128)S(1)}) custom-call(s32[8]{0:T(128)S(1)} %stack.35.s_ref, bf16[384,384]{1,0:T(8,128)(2,1)S(1)} %fusion.refs_0_, bf16[384,384]{1,0:T(8,128)(2,1)S(1)} %copy.8.refs_1_, bf16[384,384]{1,0:T(8,128)(2,1)S(1)} %collective-permute-done.3.refs_2_, ...), custom_call_target="tpu_custom_call" | custom-call | tf_op jit(solution)/shard_map/prep/pallas_call | solution.py:203
  60.3 0.0 collective-permute-done.9.xb_ref
  60.3 1.8 %project.2 = (bf16[8,64,384]{2,1,0:T(8,128)(2,1)S(1)}, f32[8,256]{1,0:T(8,128)S(1)}) custom-call(s32[8]{0:T(128)S(1)} %stack.35.s_ref, bf16[16,32,384]{2,1,0:T(8,128)(2,1)S(1)} %all-to-all-done.xa_ref, bf16[16,32,384]{2,1,0:T(8,128)(2,1)S(1)} %collective-permute-done.9.xb_ref, bf16[1536,768]{1,0:T(8,128)(2,1)S(1)} %get-tuple-element.16.w_ref, ...), custom_call_target="tpu_custom_call" | custom-call | tf_op jit(solution)/shard_map/project/pallas_call | solution.py:210
  62.2 1.4 %collective-permute-done.1.xb_ref = bf16[16,32,384]{2,1,0:T(8,128)(2,1)S(1)} collective-permute-done((bf16[16,32,384]{2,1,0:T(8,128)(2,1)S(1)}, bf16[16,32,384]{2,1,0:T(8,128)(2,1)S(1)}, u32[]{:S(2)}, u32[]{:S(2)}) %collective-permute-start.1) | collective-permute-done | bytes 393248 | tf_op jit(solution)/shard_map/ppermute | solution.py:35
  63.6 0.0 collective-permute-done.xa_ref
  63.6 0.0 copy-start
  63.6 0.0 copy-start.1
  63.6 1.8 %project.3 = (bf16[8,144,384]{2,1,0:T(8,128)(2,1)S(1)}, f32[8,256]{1,0:T(8,128)}) custom-call(s32[8]{0:T(128)S(1)} %stack.35.s_ref, bf16[16,32,384]{2,1,0:T(8,128)(2,1)S(1)} %collective-permute-done.xa_ref, bf16[16,32,384]{2,1,0:T(8,128)(2,1)S(1)} %collective-permute-done.1.xb_ref, bf16[1536,768]{1,0:T(8,128)(2,1)S(1)} %get-tuple-element.16.w_ref, ...), custom_call_target="tpu_custom_call" | custom-call | tf_op jit(solution)/shard_map/project/pallas_call | solution.py:210
  65.4 20.9 %all_to_all.20.r_ref = bf16[8,144,384]{2,1,0:T(8,128)(2,1)S(1)} all-to-all(bf16[8,144,384]{2,1,0:T(8,128)(2,1)S(1)} %get-tuple-element.20), channel_id=1, replica_groups=mesh['y'=4,'zh'=4,'core'=2,'xa'=2,'xb'=2,'zg'=2,'zr'=2] {'core','xa','zr'}, dimensions={0} | all-to-all | bytes 1769472 | tf_op jit(solution)/shard_map/all_to_all | solution.py:219
  86.3 0.0 copy-done
  86.3 0.0 copy-done.1
  86.3 2.2 %norm.1 = (bf16[256,128]{1,0:T(8,128)(2,1)S(1)}, bf16[4,256,256]{2,1,0:T(8,128)(2,1)}) custom-call(s32[8]{0:T(128)S(1)} %stack.35.s_ref, bf16[8,144,384]{2,1,0:T(8,128)(2,1)S(1)} %all_to_all.20.r_ref, f32[1,128]{1,0:T(1,128)S(1)} %copy-done, f32[1,128]{1,0:T(1,128)S(1)} %copy-done.1), custom_call_target="tpu_custom_call" | custom-call | flops 3932160 | bytes 2097152 | tf_op jit(solution)/shard_map/norm/pallas_call | solution.py:220
  88.5 3.5 %all-to-all-start.2 = ((bf16[4,256,256]{2,1,0:T(8,128)(2,1)}), bf16[4,256,256]{2,1,0:T(8,128)(2,1)S(1)}, u32[]{:S(2)}, u32[]{:S(2)}) async-start(bf16[4,256,256]{2,1,0:T(8,128)(2,1)} %get-tuple-element.22), calls=%async_computation.2 | async-start | bytes 1048576 | tf_op jit(solution)/shard_map/all_to_all | solution.py:227
  92.0 7.6 %collective-permute-start.12 = (bf16[256,128]{1,0:T(8,128)(2,1)S(1)}, bf16[256,128]{1,0:T(8,128)(2,1)S(1)}, u32[]{:S(2)}, u32[]{:S(2)}) collective-permute-start(bf16[256,128]{1,0:T(8,128)(2,1)S(1)} %get-tuple-element.21.q0), channel_id=1, source_target_pairs={{0,6},{2,4},{4,2},{6,0},{1,7},{3,5},{5,3},{7,1},{8,14},{10,12},{12... | collective-permute-start | bytes 196616 | tf_op jit(solution)/shard_map/ppermute | solution.py:39
  99.5 2.1 %collective-permute-start.11 = (bf16[256,128]{1,0:T(8,128)(2,1)S(1)}, bf16[256,128]{1,0:T(8,128)(2,1)S(1)}, u32[]{:S(2)}, u32[]{:S(2)}) collective-permute-start(bf16[256,128]{1,0:T(8,128)(2,1)S(1)} %get-tuple-element.21.q0), channel_id=1, source_target_pairs={{0,4},{2,6},{4,0},{6,2},{1,5},{3,7},{5,1},{7,3},{8,12},{10,14},{12... | collective-permute-start | bytes 196616 | tf_op jit(solution)/shard_map/ppermute | solution.py:39
  101.6 2.3 %collective-permute-start.10 = (bf16[256,128]{1,0:T(8,128)(2,1)S(1)}, bf16[256,128]{1,0:T(8,128)(2,1)S(1)}, u32[]{:S(2)}, u32[]{:S(2)}) collective-permute-start(bf16[256,128]{1,0:T(8,128)(2,1)S(1)} %get-tuple-element.21.q0), channel_id=1, source_target_pairs={{0,2},{2,0},{4,6},{6,4},{1,3},{3,1},{5,7},{7,5},{8,10},{10,8},{12,... | collective-permute-start | bytes 196616 | tf_op jit(solution)/shard_map/ppermute | solution.py:39
  103.9 0.0 collective-permute-done.12.q3
  103.9 1.7 %collective-permute-done.11.q2 = bf16[256,128]{1,0:T(8,128)(2,1)S(1)} collective-permute-done((bf16[256,128]{1,0:T(8,128)(2,1)S(1)}, bf16[256,128]{1,0:T(8,128)(2,1)S(1)}, u32[]{:S(2)}, u32[]{:S(2)}) %collective-permute-start.11) | collective-permute-done | bytes 65568 | tf_op jit(solution)/shard_map/ppermute | solution.py:39
  105.7 3.5 %collective-permute-done.10.q1 = bf16[256,128]{1,0:T(8,128)(2,1)S(1)} collective-permute-done((bf16[256,128]{1,0:T(8,128)(2,1)S(1)}, bf16[256,128]{1,0:T(8,128)(2,1)S(1)}, u32[]{:S(2)}, u32[]{:S(2)}) %collective-permute-start.10) | collective-permute-done | bytes 65568 | tf_op jit(solution)/shard_map/ppermute | solution.py:39
  109.2 0.0 all-to-all-done.2.kv_ref
  109.2 2.0 %attend.1 = bf16[4,144,256]{2,1,0:T(8,128)(2,1)S(1)} custom-call(s32[8]{0:T(128)S(1)} %stack.35.s_ref, bf16[256,128]{1,0:T(8,128)(2,1)S(1)} %get-tuple-element.21.q0, bf16[256,128]{1,0:T(8,128)(2,1)S(1)} %collective-permute-done.10.q1, bf16[256,128]{1,0:T(8,128)(2,1)S(1)} %collective-permute-done.11.q2, bf16[256,128]{1,0:T(8,128)(2,1)S(1)} %collective-permute-done.12.q3, ...), custom_call_target="tpu_custom_call" | custom-call | flops 536870912 | bytes 2097152 | tf_op jit(solution)/shard_map/attend/pallas_call | solution.py:228
  111.2 12.3 %all_to_all.21.r_ref = bf16[4,144,256]{2,1,0:T(8,128)(2,1)S(1)} all-to-all(bf16[4,144,256]{2,1,0:T(8,128)(2,1)S(1)} %attend.1), channel_id=1, replica_groups=mesh['y'=4,'zh'=4,'core'=2,'xa'=2,'xb'=2,'zg'=2,'zr'=2] {'xb','zg'}, dimensions={0} | all-to-all | bytes 589824 | tf_op jit(solution)/shard_map/all_to_all | solution.py:234
  123.5 1.3 %combine.1 = f32[256,128]{1,0:T(8,128)} custom-call(s32[8]{0:T(128)S(1)} %stack.35.s_ref, bf16[4,144,256]{2,1,0:T(8,128)(2,1)S(1)} %all_to_all.21.r_ref), custom_call_target="tpu_custom_call" | custom-call | flops 262144 | bytes 1048576 | tf_op jit(solution)/shard_map/combine/pallas_call | solution.py:235
Async XLA Ops:
  1.1 21.3 %collective-permute-start.2 = (bf16[384,384]{1,0:T(8,128)(2,1)S(1)}, bf16[384,384]{1,0:T(8,128)(2,1)S(1)}, u32[]{:S(2)}, u32[]{:S(2)}) collective-permute-start(bf16[384,384]{1,0:T(8,128)(2,1)S(1)} %fusion.refs_0_), channel_id=1, source_target_pairs={{0,2},{2,0},{1,3},{3,1},{4,6},{6,4},{5,7},{7,5},{8,10},{10,8},{9,1... | collective-permute-start | bytes 884744 | tf_op jit(solution)/shard_map/ppermute | solution.py:39
  8.0 35.3 %all-to-all-start = ((bf16[16,32,384]{2,1,0:T(8,128)(2,1)}), bf16[16,32,384]{2,1,0:T(8,128)(2,1)S(1)}, u32[]{:S(2)}, u32[]{:S(2)}) async-start(bf16[16,32,384]{2,1,0:T(8,128)(2,1)} %bitcast.9), calls=%async_computation | async-start | bytes 786432 | tf_op jit(solution)/shard_map/all_to_all | solution.py:189
  23.0 23.4 %collective-permute-start.5 = (bf16[384,384]{1,0:T(8,128)(2,1)S(1)}, bf16[384,384]{1,0:T(8,128)(2,1)S(1)}, u32[]{:S(2)}, u32[]{:S(2)}) collective-permute-start(bf16[384,384]{1,0:T(8,128)(2,1)S(1)} %fusion.refs_0_), channel_id=1, source_target_pairs={{0,16},{16,0},{1,17},{17,1},{2,18},{18,2},{3,19},{19,3},{4,20},{20... | collective-permute-start | bytes 884744 | tf_op jit(solution)/shard_map/ppermute | solution.py:39
  24.9 23.5 %collective-permute-start.3 = (bf16[384,384]{1,0:T(8,128)(2,1)S(1)}, bf16[384,384]{1,0:T(8,128)(2,1)S(1)}, u32[]{:S(2)}, u32[]{:S(2)}) collective-permute-start(bf16[384,384]{1,0:T(8,128)(2,1)S(1)} %fusion.refs_0_), channel_id=1, source_target_pairs={{0,4},{4,0},{1,5},{5,1},{2,6},{6,2},{3,7},{7,3},{8,12},{12,8},{9,1... | collective-permute-start | bytes 884744 | tf_op jit(solution)/shard_map/ppermute | solution.py:39
  28.7 24.8 %collective-permute-start.6 = (bf16[384,384]{1,0:T(8,128)(2,1)S(1)}, bf16[384,384]{1,0:T(8,128)(2,1)S(1)}, u32[]{:S(2)}, u32[]{:S(2)}) collective-permute-start(bf16[384,384]{1,0:T(8,128)(2,1)S(1)} %copy.8.refs_1_), channel_id=1, source_target_pairs={{0,16},{16,0},{1,17},{17,1},{2,18},{18,2},{3,19},{19,3},{4,20},{20... | collective-permute-start | bytes 884744 | tf_op jit(solution)/shard_map/ppermute | solution.py:39
  30.9 24.6 %collective-permute-start.4 = (bf16[384,384]{1,0:T(8,128)(2,1)S(1)}, bf16[384,384]{1,0:T(8,128)(2,1)S(1)}, u32[]{:S(2)}, u32[]{:S(2)}) collective-permute-start(bf16[384,384]{1,0:T(8,128)(2,1)S(1)} %copy.8.refs_1_), channel_id=1, source_target_pairs={{0,4},{4,0},{1,5},{5,1},{2,6},{6,2},{3,7},{7,3},{8,12},{12,8},{9,1... | collective-permute-start | bytes 884744 | tf_op jit(solution)/shard_map/ppermute | solution.py:39
  43.3 17.1 %collective-permute-start.9 = (bf16[16,32,384]{2,1,0:T(8,128)(2,1)S(1)}, bf16[16,32,384]{2,1,0:T(8,128)(2,1)S(1)}, u32[]{:S(2)}, u32[]{:S(2)}) collective-permute-start(bf16[16,32,384]{2,1,0:T(8,128)(2,1)S(1)} %all-to-all-done.xa_ref), channel_id=1, source_target_pairs={{0,256},{128,384},{256,0},{384,128},{1,257},{129,385},{257,1},{385... | collective-permute-start | bytes 1179656 | tf_op jit(solution)/shard_map/ppermute | solution.py:35
  46.4 17.2 %collective-permute-start.1 = (bf16[16,32,384]{2,1,0:T(8,128)(2,1)S(1)}, bf16[16,32,384]{2,1,0:T(8,128)(2,1)S(1)}, u32[]{:S(2)}, u32[]{:S(2)}) collective-permute-start(bf16[16,32,384]{2,1,0:T(8,128)(2,1)S(1)} %all-to-all-done.xa_ref), channel_id=1, source_target_pairs={{0,384},{128,0},{256,128},{384,256},{1,385},{129,1},{257,129},{385... | collective-permute-start | bytes 1179656 | tf_op jit(solution)/shard_map/ppermute | solution.py:35
  48.4 15.2 %collective-permute-start = (bf16[16,32,384]{2,1,0:T(8,128)(2,1)S(1)}, bf16[16,32,384]{2,1,0:T(8,128)(2,1)S(1)}, u32[]{:S(2)}, u32[]{:S(2)}) collective-permute-start(bf16[16,32,384]{2,1,0:T(8,128)(2,1)S(1)} %all-to-all-done.xa_ref), channel_id=1, source_target_pairs={{0,128},{128,256},{256,384},{384,0},{1,129},{129,257},{257,385},{3... | collective-permute-start | bytes 1179656 | tf_op jit(solution)/shard_map/ppermute | solution.py:35
  53.5 4.4 %collective-permute-start.7 = (bf16[384,384]{1,0:T(8,128)(2,1)S(1)}, bf16[384,384]{1,0:T(8,128)(2,1)S(1)}, u32[]{:S(2)}, u32[]{:S(2)}) collective-permute-start(bf16[384,384]{1,0:T(8,128)(2,1)S(1)} %collective-permute-done.3.refs_2_), channel_id=1, source_target_pairs={{0,16},{16,0},{1,17},{17,1},{2,18},{18,2},{3,19},{19,3},{4,20},{20... | collective-permute-start | bytes 884744 | tf_op jit(solution)/shard_map/ppermute | solution.py:39
  55.4 3.6 %collective-permute-start.8 = (bf16[384,384]{1,0:T(8,128)(2,1)S(1)}, bf16[384,384]{1,0:T(8,128)(2,1)S(1)}, u32[]{:S(2)}, u32[]{:S(2)}) collective-permute-start(bf16[384,384]{1,0:T(8,128)(2,1)S(1)} %collective-permute-done.4.refs_3_), channel_id=1, source_target_pairs={{0,16},{16,0},{1,17},{17,1},{2,18},{18,2},{3,19},{19,3},{4,20},{20... | collective-permute-start | bytes 884744 | tf_op jit(solution)/shard_map/ppermute | solution.py:39
  63.6 22.7 %copy-start = (f32[1,128]{1,0:T(1,128)S(1)}, f32[1,128]{1,0:T(1,128)}, u32[]{:S(2)}) copy-start(f32[1,128]{1,0:T(1,128)} %qg_ref.1) | copy-start | bytes 1540
  63.6 22.7 %copy-start.1 = (f32[1,128]{1,0:T(1,128)S(1)}, f32[1,128]{1,0:T(1,128)}, u32[]{:S(2)}) copy-start(f32[1,128]{1,0:T(1,128)} %kg_ref.1) | copy-start | bytes 1540
  88.5 20.7 %all-to-all-start.2 = ((bf16[4,256,256]{2,1,0:T(8,128)(2,1)}), bf16[4,256,256]{2,1,0:T(8,128)(2,1)S(1)}, u32[]{:S(2)}, u32[]{:S(2)}) async-start(bf16[4,256,256]{2,1,0:T(8,128)(2,1)} %get-tuple-element.22), calls=%async_computation.2 | async-start | bytes 1048576 | tf_op jit(solution)/shard_map/all_to_all | solution.py:227
  92.0 12.0 %collective-permute-start.12 = (bf16[256,128]{1,0:T(8,128)(2,1)S(1)}, bf16[256,128]{1,0:T(8,128)(2,1)S(1)}, u32[]{:S(2)}, u32[]{:S(2)}) collective-permute-start(bf16[256,128]{1,0:T(8,128)(2,1)S(1)} %get-tuple-element.21.q0), channel_id=1, source_target_pairs={{0,6},{2,4},{4,2},{6,0},{1,7},{3,5},{5,3},{7,1},{8,14},{10,12},{12... | collective-permute-start | bytes 196616 | tf_op jit(solution)/shard_map/ppermute | solution.py:39
  99.5 6.2 %collective-permute-start.11 = (bf16[256,128]{1,0:T(8,128)(2,1)S(1)}, bf16[256,128]{1,0:T(8,128)(2,1)S(1)}, u32[]{:S(2)}, u32[]{:S(2)}) collective-permute-start(bf16[256,128]{1,0:T(8,128)(2,1)S(1)} %get-tuple-element.21.q0), channel_id=1, source_target_pairs={{0,4},{2,6},{4,0},{6,2},{1,5},{3,7},{5,1},{7,3},{8,12},{10,14},{12... | collective-permute-start | bytes 196616 | tf_op jit(solution)/shard_map/ppermute | solution.py:39
  101.6 7.6 %collective-permute-start.10 = (bf16[256,128]{1,0:T(8,128)(2,1)S(1)}, bf16[256,128]{1,0:T(8,128)(2,1)S(1)}, u32[]{:S(2)}, u32[]{:S(2)}) collective-permute-start(bf16[256,128]{1,0:T(8,128)(2,1)S(1)} %get-tuple-element.21.q0), channel_id=1, source_target_pairs={{0,2},{2,0},{4,6},{6,4},{1,3},{3,1},{5,7},{7,5},{8,10},{10,8},{12,... | collective-permute-start | bytes 196616 | tf_op jit(solution)/shard_map/ppermute | solution.py:39

commit v5 on v4

--- a/solution.py
+++ b/solution.py
@@ -115,35 +115,33 @@
 
 
 def norm_kernel(s_ref, r_ref, qg_ref, kg_ref, q_ref, kv_ref):
-    for half in range(2):
-        s1, s2, cs = [], [], []
-        acc = jnp.zeros((TB, 3 * HS), f32)
-        for x in range(4):
-            blk = half * 4 + x
-            acc = acc + r_ref[blk, 0:TB, :].astype(f32)
-            e = r_ref[blk, TB : TB + EXTRA, :].astype(f32)
-            s1.append(e[0:1, 0:TB] + e[1:2, 0:TB] + e[2:3, 0:TB])
-            s2.append(e[3:4, 0:TB] + e[4:5, 0:TB] + e[5:6, 0:TB])
-            cs.append(e[6:7] + e[7:8] + e[8:9])
-        mean = (s1[0] + s1[1] + s1[2] + s1[3]) * (1.0 / D)
-        var = (s2[0] + s2[1] + s2[2] + s2[3]) * (1.0 / D) - mean * mean
-        rows = [s * (1.0 / FD) - mean for s in s1] + [lax.rsqrt(var + EPS)]
-        cols = jnp.concatenate(rows + [jnp.zeros((TB - 5, TB), f32)], axis=0).T
-        for x in range(4):
-            acc = acc + cols[:, x : x + 1] * cs[x]
-        proj = acc * cols[:, 4:5]
-
-        def head_norm(v, gain):
-            c = v - jnp.mean(v, axis=1, keepdims=True)
-            return c * lax.rsqrt(jnp.mean(c * c, axis=1, keepdims=True) + EPS) * gain
-
-        at = slice(half * TB, (half + 1) * TB)
-        q_ref[at, :] = head_norm(proj[:, 0:HS], qg_ref[...]).astype(bf16)
-        keys = head_norm(proj[:, HS : 2 * HS], kg_ref[...]).astype(bf16)
-        values = proj[:, 2 * HS : 3 * HS].astype(bf16)
-        for x in range(4):
-            kv_ref[x, at, 0:HS] = keys
-            kv_ref[x, at, HS : 2 * HS] = values
+    s1, s2, cs = [], [], []
+    acc = jnp.zeros((2 * TB, 3 * HS), f32)
+    for x in range(4):
+        acc = acc + jnp.concatenate([r_ref[x, 0:TB, :], r_ref[4 + x, 0:TB, :]], axis=0).astype(f32)
+        e0, e1 = (r_ref[b, TB : TB + EXTRA, :].astype(f32) for b in (x, 4 + x))
+        e = jnp.concatenate([e0[:, 0:TB], e1[:, 0:TB]], axis=1)
+        s1.append(e[0:1] + e[1:2] + e[2:3])
+        s2.append(e[3:4] + e[4:5] + e[5:6])
+        cs.append(e0[6:7] + e0[7:8] + e0[8:9])
+    mean = (s1[0] + s1[1] + s1[2] + s1[3]) * (1.0 / D)
+    var = (s2[0] + s2[1] + s2[2] + s2[3]) * (1.0 / D) - mean * mean
+    rows = [s * (1.0 / FD) - mean for s in s1] + [lax.rsqrt(var + EPS)]
+    cols = jnp.concatenate(rows + [jnp.zeros((TB - 5, 2 * TB), f32)], axis=0).T
+    for x in range(4):
+        acc = acc + cols[:, x : x + 1] * cs[x]
+    proj = acc * cols[:, 4:5]
+
+    def head_norm(v, gain):
+        c = v - jnp.mean(v, axis=1, keepdims=True)
+        return c * lax.rsqrt(jnp.mean(c * c, axis=1, keepdims=True) + EPS) * gain
+
+    q_ref[...] = head_norm(proj[:, 0:HS], qg_ref[...]).astype(bf16)
+    keys = head_norm(proj[:, HS : 2 * HS], kg_ref[...]).astype(bf16)
+    values = proj[:, 2 * HS : 3 * HS].astype(bf16)
+    for x in range(4):
+        kv_ref[x, :, 0:HS] = keys
+        kv_ref[x, :, HS : 2 * HS] = values
 
 
 def attend_kernel(s_ref, q0, q1, q2, q3, kv_ref, out_ref, qs_ref):

time: 126 us -> 126 us (level)
  no operation moved by 1% of the time
where the time goes in v5:
time: 126 us; the launch traced here: 125 us
  starting transfers between devices  59.5 us (47%)
  blocking collectives  33.2 us (26%)
  waiting for transfers between devices  18.1 us (14%)
  Pallas kernels  10.9 us (9%)
  local copies, waits for them, and re-layouts  1.78 us (1%)
    ppermute x10, starting transfers between devices, swap(): return lax.ppermute(x, axis, [(i, i ^ k) for i in range(n)])  31.5 us
    all_to_all x1, blocking collectives, body(): lax.all_to_all(second, ('core',) + REDUCE, split_axis=0, concat_axis=0, t...  20.9 us
    all_to_all x1, starting transfers between devices, body(): lax.all_to_all(jnp.broadcast_to(tokens.reshape(1, 4, QT, FB), (4, 4, QT,...  14.3 us
    all_to_all x1, blocking collectives, body(): lax.all_to_all(partial, GATHER, split_axis=0, concat_axis=0, tiled=True)  12.3 us
    all_to_all x1, waiting for transfers between devices, body(): lax.all_to_all(jnp.broadcast_to(tokens.reshape(1, 4, QT, FB), (4, 4, QT,...  10.2 us
    ppermute x3, starting transfers between devices, shift(): return lax.ppermute(x, axis, [(i, (i + k) % 4) for i in range(4)])  10.2 us
    ppermute x10, waiting for transfers between devices, swap(): return lax.ppermute(x, axis, [(i, i ^ k) for i in range(n)])  6.46 us
    pallas_call x2, Pallas kernels, project(): call(project_kernel, (jax.ShapeDtypeStruct((8, rows, FB), bf16), jax.Shap...  3.66 us
  transfers between devices with their start and end apart: 15, of which 5 were waited for; matrix products, arithmetic and copies ran while one was open for 1% of the time, Pallas kernels for 3%

profile of v5, /device:TPU:24, one launch (start us, length us, event | category | flops | bytes accessed | tf_op | source)
XLA Modules:
  0.0 124.7 jit_solution(5623427916579785268)
XLA Ops:
  0.0 1.1 fusion.refs_0_
  1.1 5.2 %collective-permute-start.2 = (bf16[384,384]{1,0:T(8,128)(2,1)S(1)}, bf16[384,384]{1,0:T(8,128)(2,1)S(1)}, u32[]{:S(2)}, u32[]{:S(2)}) collective-permute-start(bf16[384,384]{1,0:T(8,128)(2,1)S(1)} %fusion.refs_0_), channel_id=1, source_target_pairs={{0,2},{2,0},{1,3},{3,1},{4,6},{6,4},{5,7},{7,5},{8,10},{10,8},{9,1... | collective-permute-start | bytes 884744 | tf_op jit(solution)/shard_map/ppermute | solution.py:39
  6.3 1.7 %broadcast_in_dim.9 = bf16[4,4,32,384]{3,2,1,0:T(8,128)(2,1)} broadcast(bf16[4,32,384]{2,1,0:T(8,128)(2,1)} %bitcast.16), dimensions={1,2,3} | broadcast | bytes 491520 | tf_op jit(solution)/shard_map/broadcast_in_dim | solution.py:188
  8.0 14.3 %all-to-all-start = ((bf16[16,32,384]{2,1,0:T(8,128)(2,1)}), bf16[16,32,384]{2,1,0:T(8,128)(2,1)S(1)}, u32[]{:S(2)}, u32[]{:S(2)}) async-start(bf16[16,32,384]{2,1,0:T(8,128)(2,1)} %bitcast.9), calls=%async_computation | async-start | bytes 786432 | tf_op jit(solution)/shard_map/all_to_all | solution.py:187
  22.3 0.1 stack.35.s_ref
  22.4 0.0 collective-permute-done.2.x_ref
  22.4 0.6 copy.8.refs_1_
  23.0 1.9 %collective-permute-start.5 = (bf16[384,384]{1,0:T(8,128)(2,1)S(1)}, bf16[384,384]{1,0:T(8,128)(2,1)S(1)}, u32[]{:S(2)}, u32[]{:S(2)}) collective-permute-start(bf16[384,384]{1,0:T(8,128)(2,1)S(1)} %fusion.refs_0_), channel_id=1, source_target_pairs={{0,16},{16,0},{1,17},{17,1},{2,18},{18,2},{3,19},{19,3},{4,20},{20... | collective-permute-start | bytes 884744 | tf_op jit(solution)/shard_map/ppermute | solution.py:39
  24.9 3.8 %collective-permute-start.3 = (bf16[384,384]{1,0:T(8,128)(2,1)S(1)}, bf16[384,384]{1,0:T(8,128)(2,1)S(1)}, u32[]{:S(2)}, u32[]{:S(2)}) collective-permute-start(bf16[384,384]{1,0:T(8,128)(2,1)S(1)} %fusion.refs_0_), channel_id=1, source_target_pairs={{0,4},{4,0},{1,5},{5,1},{2,6},{6,2},{3,7},{7,3},{8,12},{12,8},{9,1... | collective-permute-start | bytes 884744 | tf_op jit(solution)/shard_map/ppermute | solution.py:39
  28.7 2.1 %collective-permute-start.6 = (bf16[384,384]{1,0:T(8,128)(2,1)S(1)}, bf16[384,384]{1,0:T(8,128)(2,1)S(1)}, u32[]{:S(2)}, u32[]{:S(2)}) collective-permute-start(bf16[384,384]{1,0:T(8,128)(2,1)S(1)} %copy.8.refs_1_), channel_id=1, source_target_pairs={{0,16},{16,0},{1,17},{17,1},{2,18},{18,2},{3,19},{19,3},{4,20},{20... | collective-permute-start | bytes 884744 | tf_op jit(solution)/shard_map/ppermute | solution.py:39
  30.9 2.2 %collective-permute-start.4 = (bf16[384,384]{1,0:T(8,128)(2,1)S(1)}, bf16[384,384]{1,0:T(8,128)(2,1)S(1)}, u32[]{:S(2)}, u32[]{:S(2)}) collective-permute-start(bf16[384,384]{1,0:T(8,128)(2,1)S(1)} %copy.8.refs_1_), channel_id=1, source_target_pairs={{0,4},{4,0},{1,5},{5,1},{2,6},{6,2},{3,7},{7,3},{8,12},{12,8},{9,1... | collective-permute-start | bytes 884744 | tf_op jit(solution)/shard_map/ppermute | solution.py:39
  33.1 10.2 %all-to-all-done.xa_ref = bf16[16,32,384]{2,1,0:T(8,128)(2,1)S(1)} async-done(((bf16[16,32,384]{2,1,0:T(8,128)(2,1)}), bf16[16,32,384]{2,1,0:T(8,128)(2,1)S(1)}, u32[]{:S(2)}, u32[]{:S(2)}) %all-to-all-start) | async-done | bytes 393248 | tf_op jit(solution)/shard_map/all_to_all | solution.py:187
  43.3 3.1 %collective-permute-start.9 = (bf16[16,32,384]{2,1,0:T(8,128)(2,1)S(1)}, bf16[16,32,384]{2,1,0:T(8,128)(2,1)S(1)}, u32[]{:S(2)}, u32[]{:S(2)}) collective-permute-start(bf16[16,32,384]{2,1,0:T(8,128)(2,1)S(1)} %all-to-all-done.xa_ref), channel_id=1, source_target_pairs={{0,256},{128,384},{256,0},{384,128},{1,257},{129,385},{257,1},{385... | collective-permute-start | bytes 1179656 | tf_op jit(solution)/shard_map/ppermute | solution.py:35
  46.4 0.0 collective-permute-done.5.refs_4_
  46.4 1.9 %collective-permute-start.1 = (bf16[16,32,384]{2,1,0:T(8,128)(2,1)S(1)}, bf16[16,32,384]{2,1,0:T(8,128)(2,1)S(1)}, u32[]{:S(2)}, u32[]{:S(2)}) collective-permute-start(bf16[16,32,384]{2,1,0:T(8,128)(2,1)S(1)} %all-to-all-done.xa_ref), channel_id=1, source_target_pairs={{0,384},{128,0},{256,128},{384,256},{1,385},{129,1},{257,129},{385... | collective-permute-start | bytes 1179656 | tf_op jit(solution)/shard_map/ppermute | solution.py:35
  48.3 0.0 collective-permute-done.3.refs_2_
  48.4 5.1 %collective-permute-start = (bf16[16,32,384]{2,1,0:T(8,128)(2,1)S(1)}, bf16[16,32,384]{2,1,0:T(8,128)(2,1)S(1)}, u32[]{:S(2)}, u32[]{:S(2)}) collective-permute-start(bf16[16,32,384]{2,1,0:T(8,128)(2,1)S(1)} %all-to-all-done.xa_ref), channel_id=1, source_target_pairs={{0,128},{128,256},{256,384},{384,0},{1,129},{129,257},{257,385},{3... | collective-permute-start | bytes 1179656 | tf_op jit(solution)/shard_map/ppermute | solution.py:35
  53.5 0.0 collective-permute-done.6.refs_5_
  53.5 1.9 %collective-permute-start.7 = (bf16[384,384]{1,0:T(8,128)(2,1)S(1)}, bf16[384,384]{1,0:T(8,128)(2,1)S(1)}, u32[]{:S(2)}, u32[]{:S(2)}) collective-permute-start(bf16[384,384]{1,0:T(8,128)(2,1)S(1)} %collective-permute-done.3.refs_2_), channel_id=1, source_target_pairs={{0,16},{16,0},{1,17},{17,1},{2,18},{18,2},{3,19},{19,3},{4,20},{20... | collective-permute-start | bytes 884744 | tf_op jit(solution)/shard_map/ppermute | solution.py:39
  55.4 0.0 collective-permute-done.4.refs_3_
  55.4 2.4 %collective-permute-start.8 = (bf16[384,384]{1,0:T(8,128)(2,1)S(1)}, bf16[384,384]{1,0:T(8,128)(2,1)S(1)}, u32[]{:S(2)}, u32[]{:S(2)}) collective-permute-start(bf16[384,384]{1,0:T(8,128)(2,1)S(1)} %collective-permute-done.4.refs_3_), channel_id=1, source_target_pairs={{0,16},{16,0},{1,17},{17,1},{2,18},{18,2},{3,19},{19,3},{4,20},{20... | collective-permute-start | bytes 884744 | tf_op jit(solution)/shard_map/ppermute | solution.py:39
  57.9 0.0 collective-permute-done.7.refs_6_
  57.9 1.2 collective-permute-done.8.refs_7_
  59.1 1.3 %prep.1 = (bf16[1536,768]{1,0:T(8,128)(2,1)S(1)}, f32[8,768]{1,0:T(8,128)S(1)}) custom-call(s32[8]{0:T(128)S(1)} %stack.35.s_ref, bf16[384,384]{1,0:T(8,128)(2,1)S(1)} %fusion.refs_0_, bf16[384,384]{1,0:T(8,128)(2,1)S(1)} %copy.8.refs_1_, bf16[384,384]{1,0:T(8,128)(2,1)S(1)} %collective-permute-done.3.refs_2_, ...), custom_call_target="tpu_custom_call" | custom-call | tf_op jit(solution)/shard_map/prep/pallas_call | solution.py:201
  60.3 0.0 collective-permute-done.9.xb_ref
  60.3 1.8 %project.2 = (bf16[8,64,384]{2,1,0:T(8,128)(2,1)S(1)}, f32[8,256]{1,0:T(8,128)S(1)}) custom-call(s32[8]{0:T(128)S(1)} %stack.35.s_ref, bf16[16,32,384]{2,1,0:T(8,128)(2,1)S(1)} %all-to-all-done.xa_ref, bf16[16,32,384]{2,1,0:T(8,128)(2,1)S(1)} %collective-permute-done.9.xb_ref, bf16[1536,768]{1,0:T(8,128)(2,1)S(1)} %get-tuple-element.16.w_ref, ...), custom_call_target="tpu_custom_call" | custom-call | tf_op jit(solution)/shard_map/project/pallas_call | solution.py:208
  62.2 1.4 %collective-permute-done.1.xb_ref = bf16[16,32,384]{2,1,0:T(8,128)(2,1)S(1)} collective-permute-done((bf16[16,32,384]{2,1,0:T(8,128)(2,1)S(1)}, bf16[16,32,384]{2,1,0:T(8,128)(2,1)S(1)}, u32[]{:S(2)}, u32[]{:S(2)}) %collective-permute-start.1) | collective-permute-done | bytes 393248 | tf_op jit(solution)/shard_map/ppermute | solution.py:35
  63.6 0.0 collective-permute-done.xa_ref
  63.6 0.0 copy-start
  63.6 0.0 copy-start.1
  63.6 1.8 %project.3 = (bf16[8,144,384]{2,1,0:T(8,128)(2,1)S(1)}, f32[8,256]{1,0:T(8,128)}) custom-call(s32[8]{0:T(128)S(1)} %stack.35.s_ref, bf16[16,32,384]{2,1,0:T(8,128)(2,1)S(1)} %collective-permute-done.xa_ref, bf16[16,32,384]{2,1,0:T(8,128)(2,1)S(1)} %collective-permute-done.1.xb_ref, bf16[1536,768]{1,0:T(8,128)(2,1)S(1)} %get-tuple-element.16.w_ref, ...), custom_call_target="tpu_custom_call" | custom-call | tf_op jit(solution)/shard_map/project/pallas_call | solution.py:208
  65.4 20.9 %all_to_all.20.r_ref = bf16[8,144,384]{2,1,0:T(8,128)(2,1)S(1)} all-to-all(bf16[8,144,384]{2,1,0:T(8,128)(2,1)S(1)} %get-tuple-element.20), channel_id=1, replica_groups=mesh['y'=4,'zh'=4,'core'=2,'xa'=2,'xb'=2,'zg'=2,'zr'=2] {'core','xa','zr'}, dimensions={0} | all-to-all | bytes 1769472 | tf_op jit(solution)/shard_map/all_to_all | solution.py:217
  86.3 0.0 copy-done
  86.3 0.0 copy-done.1
  86.3 2.1 %norm.1 = (bf16[256,128]{1,0:T(8,128)(2,1)S(1)}, bf16[4,256,256]{2,1,0:T(8,128)(2,1)}) custom-call(s32[8]{0:T(128)S(1)} %stack.35.s_ref, bf16[8,144,384]{2,1,0:T(8,128)(2,1)S(1)} %all_to_all.20.r_ref, f32[1,128]{1,0:T(1,128)S(1)} %copy-done, f32[1,128]{1,0:T(1,128)S(1)} %copy-done.1), custom_call_target="tpu_custom_call" | custom-call | flops 3932160 | bytes 2097152 | tf_op jit(solution)/shard_map/norm/pallas_call | solution.py:218
  88.4 3.5 %all-to-all-start.2 = ((bf16[4,256,256]{2,1,0:T(8,128)(2,1)}), bf16[4,256,256]{2,1,0:T(8,128)(2,1)S(1)}, u32[]{:S(2)}, u32[]{:S(2)}) async-start(bf16[4,256,256]{2,1,0:T(8,128)(2,1)} %get-tuple-element.22), calls=%async_computation.2 | async-start | bytes 1048576 | tf_op jit(solution)/shard_map/all_to_all | solution.py:225
  91.8 7.6 %collective-permute-start.12 = (bf16[256,128]{1,0:T(8,128)(2,1)S(1)}, bf16[256,128]{1,0:T(8,128)(2,1)S(1)}, u32[]{:S(2)}, u32[]{:S(2)}) collective-permute-start(bf16[256,128]{1,0:T(8,128)(2,1)S(1)} %get-tuple-element.21.q0), channel_id=1, source_target_pairs={{0,6},{2,4},{4,2},{6,0},{1,7},{3,5},{5,3},{7,1},{8,14},{10,12},{12... | collective-permute-start | bytes 196616 | tf_op jit(solution)/shard_map/ppermute | solution.py:39
  99.4 2.1 %collective-permute-start.11 = (bf16[256,128]{1,0:T(8,128)(2,1)S(1)}, bf16[256,128]{1,0:T(8,128)(2,1)S(1)}, u32[]{:S(2)}, u32[]{:S(2)}) collective-permute-start(bf16[256,128]{1,0:T(8,128)(2,1)S(1)} %get-tuple-element.21.q0), channel_id=1, source_target_pairs={{0,4},{2,6},{4,0},{6,2},{1,5},{3,7},{5,1},{7,3},{8,12},{10,14},{12... | collective-permute-start | bytes 196616 | tf_op jit(solution)/shard_map/ppermute | solution.py:39
  101.5 2.3 %collective-permute-start.10 = (bf16[256,128]{1,0:T(8,128)(2,1)S(1)}, bf16[256,128]{1,0:T(8,128)(2,1)S(1)}, u32[]{:S(2)}, u32[]{:S(2)}) collective-permute-start(bf16[256,128]{1,0:T(8,128)(2,1)S(1)} %get-tuple-element.21.q0), channel_id=1, source_target_pairs={{0,2},{2,0},{4,6},{6,4},{1,3},{3,1},{5,7},{7,5},{8,10},{10,8},{12,... | collective-permute-start | bytes 196616 | tf_op jit(solution)/shard_map/ppermute | solution.py:39
  103.8 0.0 collective-permute-done.12.q3
  103.8 1.7 %collective-permute-done.11.q2 = bf16[256,128]{1,0:T(8,128)(2,1)S(1)} collective-permute-done((bf16[256,128]{1,0:T(8,128)(2,1)S(1)}, bf16[256,128]{1,0:T(8,128)(2,1)S(1)}, u32[]{:S(2)}, u32[]{:S(2)}) %collective-permute-start.11) | collective-permute-done | bytes 65568 | tf_op jit(solution)/shard_map/ppermute | solution.py:39
  105.6 3.5 %collective-permute-done.10.q1 = bf16[256,128]{1,0:T(8,128)(2,1)S(1)} collective-permute-done((bf16[256,128]{1,0:T(8,128)(2,1)S(1)}, bf16[256,128]{1,0:T(8,128)(2,1)S(1)}, u32[]{:S(2)}, u32[]{:S(2)}) %collective-permute-start.10) | collective-permute-done | bytes 65568 | tf_op jit(solution)/shard_map/ppermute | solution.py:39
  109.1 0.0 all-to-all-done.2.kv_ref
  109.1 2.0 %attend.1 = bf16[4,144,256]{2,1,0:T(8,128)(2,1)S(1)} custom-call(s32[8]{0:T(128)S(1)} %stack.35.s_ref, bf16[256,128]{1,0:T(8,128)(2,1)S(1)} %get-tuple-element.21.q0, bf16[256,128]{1,0:T(8,128)(2,1)S(1)} %collective-permute-done.10.q1, bf16[256,128]{1,0:T(8,128)(2,1)S(1)} %collective-permute-done.11.q2, bf16[256,128]{1,0:T(8,128)(2,1)S(1)} %collective-permute-done.12.q3, ...), custom_call_target="tpu_custom_call" | custom-call | flops 536870912 | bytes 2097152 | tf_op jit(solution)/shard_map/attend/pallas_call | solution.py:226
  111.1 12.3 %all_to_all.21.r_ref = bf16[4,144,256]{2,1,0:T(8,128)(2,1)S(1)} all-to-all(bf16[4,144,256]{2,1,0:T(8,128)(2,1)S(1)} %attend.1), channel_id=1, replica_groups=mesh['y'=4,'zh'=4,'core'=2,'xa'=2,'xb'=2,'zg'=2,'zr'=2] {'xb','zg'}, dimensions={0} | all-to-all | bytes 589824 | tf_op jit(solution)/shard_map/all_to_all | solution.py:232
  123.4 1.3 %combine.1 = f32[256,128]{1,0:T(8,128)} custom-call(s32[8]{0:T(128)S(1)} %stack.35.s_ref, bf16[4,144,256]{2,1,0:T(8,128)(2,1)S(1)} %all_to_all.21.r_ref), custom_call_target="tpu_custom_call" | custom-call | flops 262144 | bytes 1048576 | tf_op jit(solution)/shard_map/combine/pallas_call | solution.py:233
Async XLA Ops:
  1.1 21.3 %collective-permute-start.2 = (bf16[384,384]{1,0:T(8,128)(2,1)S(1)}, bf16[384,384]{1,0:T(8,128)(2,1)S(1)}, u32[]{:S(2)}, u32[]{:S(2)}) collective-permute-start(bf16[384,384]{1,0:T(8,128)(2,1)S(1)} %fusion.refs_0_), channel_id=1, source_target_pairs={{0,2},{2,0},{1,3},{3,1},{4,6},{6,4},{5,7},{7,5},{8,10},{10,8},{9,1... | collective-permute-start | bytes 884744 | tf_op jit(solution)/shard_map/ppermute | solution.py:39
  8.0 35.3 %all-to-all-start = ((bf16[16,32,384]{2,1,0:T(8,128)(2,1)}), bf16[16,32,384]{2,1,0:T(8,128)(2,1)S(1)}, u32[]{:S(2)}, u32[]{:S(2)}) async-start(bf16[16,32,384]{2,1,0:T(8,128)(2,1)} %bitcast.9), calls=%async_computation | async-start | bytes 786432 | tf_op jit(solution)/shard_map/all_to_all | solution.py:187
  23.0 23.4 %collective-permute-start.5 = (bf16[384,384]{1,0:T(8,128)(2,1)S(1)}, bf16[384,384]{1,0:T(8,128)(2,1)S(1)}, u32[]{:S(2)}, u32[]{:S(2)}) collective-permute-start(bf16[384,384]{1,0:T(8,128)(2,1)S(1)} %fusion.refs_0_), channel_id=1, source_target_pairs={{0,16},{16,0},{1,17},{17,1},{2,18},{18,2},{3,19},{19,3},{4,20},{20... | collective-permute-start | bytes 884744 | tf_op jit(solution)/shard_map/ppermute | solution.py:39
  24.9 23.5 %collective-permute-start.3 = (bf16[384,384]{1,0:T(8,128)(2,1)S(1)}, bf16[384,384]{1,0:T(8,128)(2,1)S(1)}, u32[]{:S(2)}, u32[]{:S(2)}) collective-permute-start(bf16[384,384]{1,0:T(8,128)(2,1)S(1)} %fusion.refs_0_), channel_id=1, source_target_pairs={{0,4},{4,0},{1,5},{5,1},{2,6},{6,2},{3,7},{7,3},{8,12},{12,8},{9,1... | collective-permute-start | bytes 884744 | tf_op jit(solution)/shard_map/ppermute | solution.py:39
  28.7 24.8 %collective-permute-start.6 = (bf16[384,384]{1,0:T(8,128)(2,1)S(1)}, bf16[384,384]{1,0:T(8,128)(2,1)S(1)}, u32[]{:S(2)}, u32[]{:S(2)}) collective-permute-start(bf16[384,384]{1,0:T(8,128)(2,1)S(1)} %copy.8.refs_1_), channel_id=1, source_target_pairs={{0,16},{16,0},{1,17},{17,1},{2,18},{18,2},{3,19},{19,3},{4,20},{20... | collective-permute-start | bytes 884744 | tf_op jit(solution)/shard_map/ppermute | solution.py:39
  30.9 24.6 %collective-permute-start.4 = (bf16[384,384]{1,0:T(8,128)(2,1)S(1)}, bf16[384,384]{1,0:T(8,128)(2,1)S(1)}, u32[]{:S(2)}, u32[]{:S(2)}) collective-permute-start(bf16[384,384]{1,0:T(8,128)(2,1)S(1)} %copy.8.refs_1_), channel_id=1, source_target_pairs={{0,4},{4,0},{1,5},{5,1},{2,6},{6,2},{3,7},{7,3},{8,12},{12,8},{9,1... | collective-permute-start | bytes 884744 | tf_op jit(solution)/shard_map/ppermute | solution.py:39
  43.3 17.1 %collective-permute-start.9 = (bf16[16,32,384]{2,1,0:T(8,128)(2,1)S(1)}, bf16[16,32,384]{2,1,0:T(8,128)(2,1)S(1)}, u32[]{:S(2)}, u32[]{:S(2)}) collective-permute-start(bf16[16,32,384]{2,1,0:T(8,128)(2,1)S(1)} %all-to-all-done.xa_ref), channel_id=1, source_target_pairs={{0,256},{128,384},{256,0},{384,128},{1,257},{129,385},{257,1},{385... | collective-permute-start | bytes 1179656 | tf_op jit(solution)/shard_map/ppermute | solution.py:35
  46.4 17.2 %collective-permute-start.1 = (bf16[16,32,384]{2,1,0:T(8,128)(2,1)S(1)}, bf16[16,32,384]{2,1,0:T(8,128)(2,1)S(1)}, u32[]{:S(2)}, u32[]{:S(2)}) collective-permute-start(bf16[16,32,384]{2,1,0:T(8,128)(2,1)S(1)} %all-to-all-done.xa_ref), channel_id=1, source_target_pairs={{0,384},{128,0},{256,128},{384,256},{1,385},{129,1},{257,129},{385... | collective-permute-start | bytes 1179656 | tf_op jit(solution)/shard_map/ppermute | solution.py:35
  48.4 15.2 %collective-permute-start = (bf16[16,32,384]{2,1,0:T(8,128)(2,1)S(1)}, bf16[16,32,384]{2,1,0:T(8,128)(2,1)S(1)}, u32[]{:S(2)}, u32[]{:S(2)}) collective-permute-start(bf16[16,32,384]{2,1,0:T(8,128)(2,1)S(1)} %all-to-all-done.xa_ref), channel_id=1, source_target_pairs={{0,128},{128,256},{256,384},{384,0},{1,129},{129,257},{257,385},{3... | collective-permute-start | bytes 1179656 | tf_op jit(solution)/shard_map/ppermute | solution.py:35
  53.5 4.4 %collective-permute-start.7 = (bf16[384,384]{1,0:T(8,128)(2,1)S(1)}, bf16[384,384]{1,0:T(8,128)(2,1)S(1)}, u32[]{:S(2)}, u32[]{:S(2)}) collective-permute-start(bf16[384,384]{1,0:T(8,128)(2,1)S(1)} %collective-permute-done.3.refs_2_), channel_id=1, source_target_pairs={{0,16},{16,0},{1,17},{17,1},{2,18},{18,2},{3,19},{19,3},{4,20},{20... | collective-permute-start | bytes 884744 | tf_op jit(solution)/shard_map/ppermute | solution.py:39
  55.4 3.6 %collective-permute-start.8 = (bf16[384,384]{1,0:T(8,128)(2,1)S(1)}, bf16[384,384]{1,0:T(8,128)(2,1)S(1)}, u32[]{:S(2)}, u32[]{:S(2)}) collective-permute-start(bf16[384,384]{1,0:T(8,128)(2,1)S(1)} %collective-permute-done.4.refs_3_), channel_id=1, source_target_pairs={{0,16},{16,0},{1,17},{17,1},{2,18},{18,2},{3,19},{19,3},{4,20},{20... | collective-permute-start | bytes 884744 | tf_op jit(solution)/shard_map/ppermute | solution.py:39
  63.6 22.7 %copy-start = (f32[1,128]{1,0:T(1,128)S(1)}, f32[1,128]{1,0:T(1,128)}, u32[]{:S(2)}) copy-start(f32[1,128]{1,0:T(1,128)} %qg_ref.1) | copy-start | bytes 1540
  63.6 22.7 %copy-start.1 = (f32[1,128]{1,0:T(1,128)S(1)}, f32[1,128]{1,0:T(1,128)}, u32[]{:S(2)}) copy-start(f32[1,128]{1,0:T(1,128)} %kg_ref.1) | copy-start | bytes 1540
  88.4 20.7 %all-to-all-start.2 = ((bf16[4,256,256]{2,1,0:T(8,128)(2,1)}), bf16[4,256,256]{2,1,0:T(8,128)(2,1)S(1)}, u32[]{:S(2)}, u32[]{:S(2)}) async-start(bf16[4,256,256]{2,1,0:T(8,128)(2,1)} %get-tuple-element.22), calls=%async_computation.2 | async-start | bytes 1048576 | tf_op jit(solution)/shard_map/all_to_all | solution.py:225
  91.8 12.0 %collective-permute-start.12 = (bf16[256,128]{1,0:T(8,128)(2,1)S(1)}, bf16[256,128]{1,0:T(8,128)(2,1)S(1)}, u32[]{:S(2)}, u32[]{:S(2)}) collective-permute-start(bf16[256,128]{1,0:T(8,128)(2,1)S(1)} %get-tuple-element.21.q0), channel_id=1, source_target_pairs={{0,6},{2,4},{4,2},{6,0},{1,7},{3,5},{5,3},{7,1},{8,14},{10,12},{12... | collective-permute-start | bytes 196616 | tf_op jit(solution)/shard_map/ppermute | solution.py:39
  99.4 6.2 %collective-permute-start.11 = (bf16[256,128]{1,0:T(8,128)(2,1)S(1)}, bf16[256,128]{1,0:T(8,128)(2,1)S(1)}, u32[]{:S(2)}, u32[]{:S(2)}) collective-permute-start(bf16[256,128]{1,0:T(8,128)(2,1)S(1)} %get-tuple-element.21.q0), channel_id=1, source_target_pairs={{0,4},{2,6},{4,0},{6,2},{1,5},{3,7},{5,1},{7,3},{8,12},{10,14},{12... | collective-permute-start | bytes 196616 | tf_op jit(solution)/shard_map/ppermute | solution.py:39
  101.5 7.6 %collective-permute-start.10 = (bf16[256,128]{1,0:T(8,128)(2,1)S(1)}, bf16[256,128]{1,0:T(8,128)(2,1)S(1)}, u32[]{:S(2)}, u32[]{:S(2)}) collective-permute-start(bf16[256,128]{1,0:T(8,128)(2,1)S(1)} %get-tuple-element.21.q0), channel_id=1, source_target_pairs={{0,2},{2,0},{4,6},{6,4},{1,3},{3,1},{5,7},{7,5},{8,10},{10,8},{12,... | collective-permute-start | bytes 196616 | tf_op jit(solution)/shard_map/ppermute | solution.py:39

commit v6 on v5

--- a/solution.py
+++ b/solution.py
@@ -50,6 +50,27 @@
         cost_estimate=pl.CostEstimate(flops=flops, bytes_accessed=nbytes, transcendentals=trans),
         name=name,
     )
+
+
+def repeat_kernel(x_ref, out_ref, sems):
+    copies = [pltpu.make_async_copy(x_ref, out_ref.at[a], sems.at[a]) for a in range(4)]
+    for c in copies:
+        c.start()
+    for c in copies:
+        c.wait()
+
+
+def repeat(x):
+    return pl.pallas_call(
+        repeat_kernel,
+        out_shape=jax.ShapeDtypeStruct((4,) + x.shape, x.dtype),
+        in_specs=[pl.BlockSpec(memory_space=pl.ANY)],
+        out_specs=pl.BlockSpec(memory_space=pl.ANY),
+        scratch_shapes=[pltpu.SemaphoreType.DMA((4,))],
+        compiler_params=pltpu.CompilerParams(vmem_limit_bytes=8 << 20),
+        cost_estimate=pl.CostEstimate(flops=0, bytes_accessed=1 << 19, transcendentals=0),
+        name="repeat",
+    )(x)
 
 
 def copy_kernel(s_ref, x_ref, out_ref):
@@ -185,7 +206,7 @@
     where = jnp.stack([core, y, xb, zg] + [jnp.bitwise_xor(here, k) for k in range(4)])
 
     x0 = lax.all_to_all(
-        jnp.broadcast_to(tokens.reshape(1, 4, QT, FB), (4, 4, QT, FB)).reshape(16, QT, FB),
+        repeat(tokens).reshape(16, QT, FB),
         ("zh",) + GATHER, split_axis=0, concat_axis=0, tiled=True,
     )
     w = (ln_gain[:, None] * qkv_weight.reshape(FB, 3 * HS).astype(f32)).astype(bf16)

time: 126 us -> 126 us (level)
    broadcast_in_dim x1 -> x0, local copies, waits for them, and re-layouts: 1.69 us -> none  [body(): jnp.broadcast_to(tokens.reshape(1, 4, QT, FB), (4, 4, QT, FB))]
  transfers between devices with their start and end apart: 15 -> 15, of which waited for: 5 -> 5; matrix products, arithmetic and copies ran while one was open for 1% -> 0% of each run, Pallas kernels for 3% -> 4%
where the time goes in v6:
time: 126 us; the launch traced here: 125 us
  starting transfers between devices  59.8 us (47%)
  blocking collectives  32.9 us (26%)
  waiting for transfers between devices  18.1 us (14%)
  Pallas kernels  11.6 us (9%)
    ppermute x10, starting transfers between devices, swap(): return lax.ppermute(x, axis, [(i, i ^ k) for i in range(n)])  31.8 us
    all_to_all x1, blocking collectives, body(): lax.all_to_all(second, ('core',) + REDUCE, split_axis=0, concat_axis=0, t...  20.6 us
    all_to_all x1, starting transfers between devices, body(): lax.all_to_all(repeat(tokens).reshape(16, QT, FB), ('zh',) + GATHER, spli...  14.3 us
    all_to_all x1, blocking collectives, body(): lax.all_to_all(partial, GATHER, split_axis=0, concat_axis=0, tiled=True)  12.3 us
    all_to_all x1, waiting for transfers between devices, body(): lax.all_to_all(repeat(tokens).reshape(16, QT, FB), ('zh',) + GATHER, spli...  10.2 us
    ppermute x3, starting transfers between devices, shift(): return lax.ppermute(x, axis, [(i, (i + k) % 4) for i in range(4)])  10.2 us
    ppermute x10, waiting for transfers between devices, swap(): return lax.ppermute(x, axis, [(i, i ^ k) for i in range(n)])  6.46 us
    pallas_call x2, Pallas kernels, project(): call(project_kernel, (jax.ShapeDtypeStruct((8, rows, FB), bf16), jax.Shap...  3.66 us
  transfers between devices with their start and end apart: 15, of which 5 were waited for; matrix products, arithmetic and copies ran while one was open for 0% of the time, Pallas kernels for 4%

profile of v6, /device:TPU:24, one launch (start us, length us, event | category | flops | bytes accessed | tf_op | source)
XLA Modules:
  0.0 124.7 jit_solution(1822667065361388650)
XLA Ops:
  0.0 1.1 fusion.refs_0_
  1.1 5.2 %collective-permute-start.2 = (bf16[384,384]{1,0:T(8,128)(2,1)S(1)}, bf16[384,384]{1,0:T(8,128)(2,1)S(1)}, u32[]{:S(2)}, u32[]{:S(2)}) collective-permute-start(bf16[384,384]{1,0:T(8,128)(2,1)S(1)} %fusion.refs_0_), channel_id=1, source_target_pairs={{0,2},{2,0},{1,3},{3,1},{4,6},{6,4},{5,7},{7,5},{8,10},{10,8},{9,1... | collective-permute-start | bytes 884744 | tf_op jit(solution)/shard_map/ppermute | solution.py:39
  6.3 0.0 copy-start
  6.3 0.9 copy-done
  7.2 0.8 repeat.1
  8.0 14.3 %all-to-all-start = ((bf16[16,32,384]{2,1,0:T(8,128)(2,1)}), bf16[16,32,384]{2,1,0:T(8,128)(2,1)S(1)}, u32[]{:S(2)}, u32[]{:S(2)}) async-start(bf16[16,32,384]{2,1,0:T(8,128)(2,1)} %bitcast.8), calls=%async_computation | async-start | bytes 786432 | tf_op jit(solution)/shard_map/all_to_all | solution.py:208
  22.3 0.1 stack.35.s_ref
  22.4 0.0 collective-permute-done.2.x_ref
  22.4 0.6 copy.8.refs_1_
  23.0 1.9 %collective-permute-start.5 = (bf16[384,384]{1,0:T(8,128)(2,1)S(1)}, bf16[384,384]{1,0:T(8,128)(2,1)S(1)}, u32[]{:S(2)}, u32[]{:S(2)}) collective-permute-start(bf16[384,384]{1,0:T(8,128)(2,1)S(1)} %fusion.refs_0_), channel_id=1, source_target_pairs={{0,16},{16,0},{1,17},{17,1},{2,18},{18,2},{3,19},{19,3},{4,20},{20... | collective-permute-start | bytes 884744 | tf_op jit(solution)/shard_map/ppermute | solution.py:39
  24.9 3.8 %collective-permute-start.3 = (bf16[384,384]{1,0:T(8,128)(2,1)S(1)}, bf16[384,384]{1,0:T(8,128)(2,1)S(1)}, u32[]{:S(2)}, u32[]{:S(2)}) collective-permute-start(bf16[384,384]{1,0:T(8,128)(2,1)S(1)} %fusion.refs_0_), channel_id=1, source_target_pairs={{0,4},{4,0},{1,5},{5,1},{2,6},{6,2},{3,7},{7,3},{8,12},{12,8},{9,1... | collective-permute-start | bytes 884744 | tf_op jit(solution)/shard_map/ppermute | solution.py:39
  28.7 2.1 %collective-permute-start.6 = (bf16[384,384]{1,0:T(8,128)(2,1)S(1)}, bf16[384,384]{1,0:T(8,128)(2,1)S(1)}, u32[]{:S(2)}, u32[]{:S(2)}) collective-permute-start(bf16[384,384]{1,0:T(8,128)(2,1)S(1)} %copy.8.refs_1_), channel_id=1, source_target_pairs={{0,16},{16,0},{1,17},{17,1},{2,18},{18,2},{3,19},{19,3},{4,20},{20... | collective-permute-start | bytes 884744 | tf_op jit(solution)/shard_map/ppermute | solution.py:39
  30.9 2.2 %collective-permute-start.4 = (bf16[384,384]{1,0:T(8,128)(2,1)S(1)}, bf16[384,384]{1,0:T(8,128)(2,1)S(1)}, u32[]{:S(2)}, u32[]{:S(2)}) collective-permute-start(bf16[384,384]{1,0:T(8,128)(2,1)S(1)} %copy.8.refs_1_), channel_id=1, source_target_pairs={{0,4},{4,0},{1,5},{5,1},{2,6},{6,2},{3,7},{7,3},{8,12},{12,8},{9,1... | collective-permute-start | bytes 884744 | tf_op jit(solution)/shard_map/ppermute | solution.py:39
  33.1 10.2 %all-to-all-done.xa_ref = bf16[16,32,384]{2,1,0:T(8,128)(2,1)S(1)} async-done(((bf16[16,32,384]{2,1,0:T(8,128)(2,1)}), bf16[16,32,384]{2,1,0:T(8,128)(2,1)S(1)}, u32[]{:S(2)}, u32[]{:S(2)}) %all-to-all-start) | async-done | bytes 393248 | tf_op jit(solution)/shard_map/all_to_all | solution.py:208
  43.3 3.1 %collective-permute-start.9 = (bf16[16,32,384]{2,1,0:T(8,128)(2,1)S(1)}, bf16[16,32,384]{2,1,0:T(8,128)(2,1)S(1)}, u32[]{:S(2)}, u32[]{:S(2)}) collective-permute-start(bf16[16,32,384]{2,1,0:T(8,128)(2,1)S(1)} %all-to-all-done.xa_ref), channel_id=1, source_target_pairs={{0,256},{128,384},{256,0},{384,128},{1,257},{129,385},{257,1},{385... | collective-permute-start | bytes 1179656 | tf_op jit(solution)/shard_map/ppermute | solution.py:35
  46.4 0.0 collective-permute-done.5.refs_4_
  46.4 1.9 %collective-permute-start.1 = (bf16[16,32,384]{2,1,0:T(8,128)(2,1)S(1)}, bf16[16,32,384]{2,1,0:T(8,128)(2,1)S(1)}, u32[]{:S(2)}, u32[]{:S(2)}) collective-permute-start(bf16[16,32,384]{2,1,0:T(8,128)(2,1)S(1)} %all-to-all-done.xa_ref), channel_id=1, source_target_pairs={{0,384},{128,0},{256,128},{384,256},{1,385},{129,1},{257,129},{385... | collective-permute-start | bytes 1179656 | tf_op jit(solution)/shard_map/ppermute | solution.py:35
  48.4 0.0 collective-permute-done.3.refs_2_
  48.4 5.1 %collective-permute-start = (bf16[16,32,384]{2,1,0:T(8,128)(2,1)S(1)}, bf16[16,32,384]{2,1,0:T(8,128)(2,1)S(1)}, u32[]{:S(2)}, u32[]{:S(2)}) collective-permute-start(bf16[16,32,384]{2,1,0:T(8,128)(2,1)S(1)} %all-to-all-done.xa_ref), channel_id=1, source_target_pairs={{0,128},{128,256},{256,384},{384,0},{1,129},{129,257},{257,385},{3... | collective-permute-start | bytes 1179656 | tf_op jit(solution)/shard_map/ppermute | solution.py:35
  53.5 0.0 collective-permute-done.6.refs_5_
  53.5 1.9 %collective-permute-start.7 = (bf16[384,384]{1,0:T(8,128)(2,1)S(1)}, bf16[384,384]{1,0:T(8,128)(2,1)S(1)}, u32[]{:S(2)}, u32[]{:S(2)}) collective-permute-start(bf16[384,384]{1,0:T(8,128)(2,1)S(1)} %collective-permute-done.3.refs_2_), channel_id=1, source_target_pairs={{0,16},{16,0},{1,17},{17,1},{2,18},{18,2},{3,19},{19,3},{4,20},{20... | collective-permute-start | bytes 884744 | tf_op jit(solution)/shard_map/ppermute | solution.py:39
  55.4 0.0 collective-permute-done.4.refs_3_
  55.5 2.4 %collective-permute-start.8 = (bf16[384,384]{1,0:T(8,128)(2,1)S(1)}, bf16[384,384]{1,0:T(8,128)(2,1)S(1)}, u32[]{:S(2)}, u32[]{:S(2)}) collective-permute-start(bf16[384,384]{1,0:T(8,128)(2,1)S(1)} %collective-permute-done.4.refs_3_), channel_id=1, source_target_pairs={{0,16},{16,0},{1,17},{17,1},{2,18},{18,2},{3,19},{19,3},{4,20},{20... | collective-permute-start | bytes 884744 | tf_op jit(solution)/shard_map/ppermute | solution.py:39
  57.9 0.0 collective-permute-done.7.refs_6_
  57.9 1.2 collective-permute-done.8.refs_7_
  59.1 1.3 %prep.1 = (bf16[1536,768]{1,0:T(8,128)(2,1)S(1)}, f32[8,768]{1,0:T(8,128)S(1)}) custom-call(s32[8]{0:T(128)S(1)} %stack.35.s_ref, bf16[384,384]{1,0:T(8,128)(2,1)S(1)} %fusion.refs_0_, bf16[384,384]{1,0:T(8,128)(2,1)S(1)} %copy.8.refs_1_, bf16[384,384]{1,0:T(8,128)(2,1)S(1)} %collective-permute-done.3.refs_2_, ...), custom_call_target="tpu_custom_call" | custom-call | tf_op jit(solution)/shard_map/prep/pallas_call | solution.py:222
  60.3 0.0 collective-permute-done.9.xb_ref
  60.3 1.8 %project.2 = (bf16[8,64,384]{2,1,0:T(8,128)(2,1)S(1)}, f32[8,256]{1,0:T(8,128)S(1)}) custom-call(s32[8]{0:T(128)S(1)} %stack.35.s_ref, bf16[16,32,384]{2,1,0:T(8,128)(2,1)S(1)} %all-to-all-done.xa_ref, bf16[16,32,384]{2,1,0:T(8,128)(2,1)S(1)} %collective-permute-done.9.xb_ref, bf16[1536,768]{1,0:T(8,128)(2,1)S(1)} %get-tuple-element.16.w_ref, ...), custom_call_target="tpu_custom_call" | custom-call | tf_op jit(solution)/shard_map/project/pallas_call | solution.py:229
  62.2 1.4 %collective-permute-done.1.xb_ref = bf16[16,32,384]{2,1,0:T(8,128)(2,1)S(1)} collective-permute-done((bf16[16,32,384]{2,1,0:T(8,128)(2,1)S(1)}, bf16[16,32,384]{2,1,0:T(8,128)(2,1)S(1)}, u32[]{:S(2)}, u32[]{:S(2)}) %collective-permute-start.1) | collective-permute-done | bytes 393248 | tf_op jit(solution)/shard_map/ppermute | solution.py:35
  63.6 0.0 collective-permute-done.xa_ref
  63.6 0.0 copy-start.1
  63.6 0.0 copy-start.2
  63.6 1.8 %project.3 = (bf16[8,144,384]{2,1,0:T(8,128)(2,1)S(1)}, f32[8,256]{1,0:T(8,128)}) custom-call(s32[8]{0:T(128)S(1)} %stack.35.s_ref, bf16[16,32,384]{2,1,0:T(8,128)(2,1)S(1)} %collective-permute-done.xa_ref, bf16[16,32,384]{2,1,0:T(8,128)(2,1)S(1)} %collective-permute-done.1.xb_ref, bf16[1536,768]{1,0:T(8,128)(2,1)S(1)} %get-tuple-element.16.w_ref, ...), custom_call_target="tpu_custom_call" | custom-call | tf_op jit(solution)/shard_map/project/pallas_call | solution.py:229
  65.4 20.6 %all_to_all.20.r_ref = bf16[8,144,384]{2,1,0:T(8,128)(2,1)S(1)} all-to-all(bf16[8,144,384]{2,1,0:T(8,128)(2,1)S(1)} %get-tuple-element.20), channel_id=1, replica_groups=mesh['y'=4,'zh'=4,'core'=2,'xa'=2,'xb'=2,'zg'=2,'zr'=2] {'core','xa','zr'}, dimensions={0} | all-to-all | bytes 1769472 | tf_op jit(solution)/shard_map/all_to_all | solution.py:238
  86.0 0.0 copy-done.1
  86.0 0.0 copy-done.2
  86.0 2.1 %norm.1 = (bf16[256,128]{1,0:T(8,128)(2,1)S(1)}, bf16[4,256,256]{2,1,0:T(8,128)(2,1)}) custom-call(s32[8]{0:T(128)S(1)} %stack.35.s_ref, bf16[8,144,384]{2,1,0:T(8,128)(2,1)S(1)} %all_to_all.20.r_ref, f32[1,128]{1,0:T(1,128)S(1)} %copy-done.1, f32[1,128]{1,0:T(1,128)S(1)} %copy-done.2), custom_call_target="tpu_custom_call" | custom-call | flops 3932160 | bytes 2097152 | tf_op jit(solution)/shard_map/norm/pallas_call | solution.py:239
  88.1 3.5 %all-to-all-start.2 = ((bf16[4,256,256]{2,1,0:T(8,128)(2,1)}), bf16[4,256,256]{2,1,0:T(8,128)(2,1)S(1)}, u32[]{:S(2)}, u32[]{:S(2)}) async-start(bf16[4,256,256]{2,1,0:T(8,128)(2,1)} %get-tuple-element.22), calls=%async_computation.2 | async-start | bytes 1048576 | tf_op jit(solution)/shard_map/all_to_all | solution.py:246
  91.5 7.9 %collective-permute-start.12 = (bf16[256,128]{1,0:T(8,128)(2,1)S(1)}, bf16[256,128]{1,0:T(8,128)(2,1)S(1)}, u32[]{:S(2)}, u32[]{:S(2)}) collective-permute-start(bf16[256,128]{1,0:T(8,128)(2,1)S(1)} %get-tuple-element.21.q0), channel_id=1, source_target_pairs={{0,6},{2,4},{4,2},{6,0},{1,7},{3,5},{5,3},{7,1},{8,14},{10,12},{12... | collective-permute-start | bytes 196616 | tf_op jit(solution)/shard_map/ppermute | solution.py:39
  99.4 2.1 %collective-permute-start.11 = (bf16[256,128]{1,0:T(8,128)(2,1)S(1)}, bf16[256,128]{1,0:T(8,128)(2,1)S(1)}, u32[]{:S(2)}, u32[]{:S(2)}) collective-permute-start(bf16[256,128]{1,0:T(8,128)(2,1)S(1)} %get-tuple-element.21.q0), channel_id=1, source_target_pairs={{0,4},{2,6},{4,0},{6,2},{1,5},{3,7},{5,1},{7,3},{8,12},{10,14},{12... | collective-permute-start | bytes 196616 | tf_op jit(solution)/shard_map/ppermute | solution.py:39
  101.5 2.3 %collective-permute-start.10 = (bf16[256,128]{1,0:T(8,128)(2,1)S(1)}, bf16[256,128]{1,0:T(8,128)(2,1)S(1)}, u32[]{:S(2)}, u32[]{:S(2)}) collective-permute-start(bf16[256,128]{1,0:T(8,128)(2,1)S(1)} %get-tuple-element.21.q0), channel_id=1, source_target_pairs={{0,2},{2,0},{4,6},{6,4},{1,3},{3,1},{5,7},{7,5},{8,10},{10,8},{12,... | collective-permute-start | bytes 196616 | tf_op jit(solution)/shard_map/ppermute | solution.py:39
  103.8 0.0 collective-permute-done.12.q3
  103.8 1.7 %collective-permute-done.11.q2 = bf16[256,128]{1,0:T(8,128)(2,1)S(1)} collective-permute-done((bf16[256,128]{1,0:T(8,128)(2,1)S(1)}, bf16[256,128]{1,0:T(8,128)(2,1)S(1)}, u32[]{:S(2)}, u32[]{:S(2)}) %collective-permute-start.11) | collective-permute-done | bytes 65568 | tf_op jit(solution)/shard_map/ppermute | solution.py:39
  105.6 3.5 %collective-permute-done.10.q1 = bf16[256,128]{1,0:T(8,128)(2,1)S(1)} collective-permute-done((bf16[256,128]{1,0:T(8,128)(2,1)S(1)}, bf16[256,128]{1,0:T(8,128)(2,1)S(1)}, u32[]{:S(2)}, u32[]{:S(2)}) %collective-permute-start.10) | collective-permute-done | bytes 65568 | tf_op jit(solution)/shard_map/ppermute | solution.py:39
  109.1 0.0 all-to-all-done.2.kv_ref
  109.1 2.0 %attend.1 = bf16[4,144,256]{2,1,0:T(8,128)(2,1)S(1)} custom-call(s32[8]{0:T(128)S(1)} %stack.35.s_ref, bf16[256,128]{1,0:T(8,128)(2,1)S(1)} %get-tuple-element.21.q0, bf16[256,128]{1,0:T(8,128)(2,1)S(1)} %collective-permute-done.10.q1, bf16[256,128]{1,0:T(8,128)(2,1)S(1)} %collective-permute-done.11.q2, bf16[256,128]{1,0:T(8,128)(2,1)S(1)} %collective-permute-done.12.q3, ...), custom_call_target="tpu_custom_call" | custom-call | flops 536870912 | bytes 2097152 | tf_op jit(solution)/shard_map/attend/pallas_call | solution.py:247
  111.1 12.3 %all_to_all.21.r_ref = bf16[4,144,256]{2,1,0:T(8,128)(2,1)S(1)} all-to-all(bf16[4,144,256]{2,1,0:T(8,128)(2,1)S(1)} %attend.1), channel_id=1, replica_groups=mesh['y'=4,'zh'=4,'core'=2,'xa'=2,'xb'=2,'zg'=2,'zr'=2] {'xb','zg'}, dimensions={0} | all-to-all | bytes 589824 | tf_op jit(solution)/shard_map/all_to_all | solution.py:253
  123.4 1.3 %combine.1 = f32[256,128]{1,0:T(8,128)} custom-call(s32[8]{0:T(128)S(1)} %stack.35.s_ref, bf16[4,144,256]{2,1,0:T(8,128)(2,1)S(1)} %all_to_all.21.r_ref), custom_call_target="tpu_custom_call" | custom-call | flops 262144 | bytes 1048576 | tf_op jit(solution)/shard_map/combine/pallas_call | solution.py:254
Async XLA Ops:
  1.1 21.3 %collective-permute-start.2 = (bf16[384,384]{1,0:T(8,128)(2,1)S(1)}, bf16[384,384]{1,0:T(8,128)(2,1)S(1)}, u32[]{:S(2)}, u32[]{:S(2)}) collective-permute-start(bf16[384,384]{1,0:T(8,128)(2,1)S(1)} %fusion.refs_0_), channel_id=1, source_target_pairs={{0,2},{2,0},{1,3},{3,1},{4,6},{6,4},{5,7},{7,5},{8,10},{10,8},{9,1... | collective-permute-start | bytes 884744 | tf_op jit(solution)/shard_map/ppermute | solution.py:39
  6.3 0.9 copy-start
  8.0 35.3 %all-to-all-start = ((bf16[16,32,384]{2,1,0:T(8,128)(2,1)}), bf16[16,32,384]{2,1,0:T(8,128)(2,1)S(1)}, u32[]{:S(2)}, u32[]{:S(2)}) async-start(bf16[16,32,384]{2,1,0:T(8,128)(2,1)} %bitcast.8), calls=%async_computation | async-start | bytes 786432 | tf_op jit(solution)/shard_map/all_to_all | solution.py:208
  23.0 23.4 %collective-permute-start.5 = (bf16[384,384]{1,0:T(8,128)(2,1)S(1)}, bf16[384,384]{1,0:T(8,128)(2,1)S(1)}, u32[]{:S(2)}, u32[]{:S(2)}) collective-permute-start(bf16[384,384]{1,0:T(8,128)(2,1)S(1)} %fusion.refs_0_), channel_id=1, source_target_pairs={{0,16},{16,0},{1,17},{17,1},{2,18},{18,2},{3,19},{19,3},{4,20},{20... | collective-permute-start | bytes 884744 | tf_op jit(solution)/shard_map/ppermute | solution.py:39
  24.9 23.4 %collective-permute-start.3 = (bf16[384,384]{1,0:T(8,128)(2,1)S(1)}, bf16[384,384]{1,0:T(8,128)(2,1)S(1)}, u32[]{:S(2)}, u32[]{:S(2)}) collective-permute-start(bf16[384,384]{1,0:T(8,128)(2,1)S(1)} %fusion.refs_0_), channel_id=1, source_target_pairs={{0,4},{4,0},{1,5},{5,1},{2,6},{6,2},{3,7},{7,3},{8,12},{12,8},{9,1... | collective-permute-start | bytes 884744 | tf_op jit(solution)/shard_map/ppermute | solution.py:39
  28.7 24.8 %collective-permute-start.6 = (bf16[384,384]{1,0:T(8,128)(2,1)S(1)}, bf16[384,384]{1,0:T(8,128)(2,1)S(1)}, u32[]{:S(2)}, u32[]{:S(2)}) collective-permute-start(bf16[384,384]{1,0:T(8,128)(2,1)S(1)} %copy.8.refs_1_), channel_id=1, source_target_pairs={{0,16},{16,0},{1,17},{17,1},{2,18},{18,2},{3,19},{19,3},{4,20},{20... | collective-permute-start | bytes 884744 | tf_op jit(solution)/shard_map/ppermute | solution.py:39
  30.9 24.6 %collective-permute-start.4 = (bf16[384,384]{1,0:T(8,128)(2,1)S(1)}, bf16[384,384]{1,0:T(8,128)(2,1)S(1)}, u32[]{:S(2)}, u32[]{:S(2)}) collective-permute-start(bf16[384,384]{1,0:T(8,128)(2,1)S(1)} %copy.8.refs_1_), channel_id=1, source_target_pairs={{0,4},{4,0},{1,5},{5,1},{2,6},{6,2},{3,7},{7,3},{8,12},{12,8},{9,1... | collective-permute-start | bytes 884744 | tf_op jit(solution)/shard_map/ppermute | solution.py:39
  43.3 17.1 %collective-permute-start.9 = (bf16[16,32,384]{2,1,0:T(8,128)(2,1)S(1)}, bf16[16,32,384]{2,1,0:T(8,128)(2,1)S(1)}, u32[]{:S(2)}, u32[]{:S(2)}) collective-permute-start(bf16[16,32,384]{2,1,0:T(8,128)(2,1)S(1)} %all-to-all-done.xa_ref), channel_id=1, source_target_pairs={{0,256},{128,384},{256,0},{384,128},{1,257},{129,385},{257,1},{385... | collective-permute-start | bytes 1179656 | tf_op jit(solution)/shard_map/ppermute | solution.py:35
  46.4 17.2 %collective-permute-start.1 = (bf16[16,32,384]{2,1,0:T(8,128)(2,1)S(1)}, bf16[16,32,384]{2,1,0:T(8,128)(2,1)S(1)}, u32[]{:S(2)}, u32[]{:S(2)}) collective-permute-start(bf16[16,32,384]{2,1,0:T(8,128)(2,1)S(1)} %all-to-all-done.xa_ref), channel_id=1, source_target_pairs={{0,384},{128,0},{256,128},{384,256},{1,385},{129,1},{257,129},{385... | collective-permute-start | bytes 1179656 | tf_op jit(solution)/shard_map/ppermute | solution.py:35
  48.4 15.2 %collective-permute-start = (bf16[16,32,384]{2,1,0:T(8,128)(2,1)S(1)}, bf16[16,32,384]{2,1,0:T(8,128)(2,1)S(1)}, u32[]{:S(2)}, u32[]{:S(2)}) collective-permute-start(bf16[16,32,384]{2,1,0:T(8,128)(2,1)S(1)} %all-to-all-done.xa_ref), channel_id=1, source_target_pairs={{0,128},{128,256},{256,384},{384,0},{1,129},{129,257},{257,385},{3... | collective-permute-start | bytes 1179656 | tf_op jit(solution)/shard_map/ppermute | solution.py:35
  53.5 4.4 %collective-permute-start.7 = (bf16[384,384]{1,0:T(8,128)(2,1)S(1)}, bf16[384,384]{1,0:T(8,128)(2,1)S(1)}, u32[]{:S(2)}, u32[]{:S(2)}) collective-permute-start(bf16[384,384]{1,0:T(8,128)(2,1)S(1)} %collective-permute-done.3.refs_2_), channel_id=1, source_target_pairs={{0,16},{16,0},{1,17},{17,1},{2,18},{18,2},{3,19},{19,3},{4,20},{20... | collective-permute-start | bytes 884744 | tf_op jit(solution)/shard_map/ppermute | solution.py:39
  55.5 3.6 %collective-permute-start.8 = (bf16[384,384]{1,0:T(8,128)(2,1)S(1)}, bf16[384,384]{1,0:T(8,128)(2,1)S(1)}, u32[]{:S(2)}, u32[]{:S(2)}) collective-permute-start(bf16[384,384]{1,0:T(8,128)(2,1)S(1)} %collective-permute-done.4.refs_3_), channel_id=1, source_target_pairs={{0,16},{16,0},{1,17},{17,1},{2,18},{18,2},{3,19},{19,3},{4,20},{20... | collective-permute-start | bytes 884744 | tf_op jit(solution)/shard_map/ppermute | solution.py:39
  63.6 22.4 %copy-start.1 = (f32[1,128]{1,0:T(1,128)S(1)}, f32[1,128]{1,0:T(1,128)}, u32[]{:S(2)}) copy-start(f32[1,128]{1,0:T(1,128)} %qg_ref.1) | copy-start | bytes 1540
  63.6 22.4 %copy-start.2 = (f32[1,128]{1,0:T(1,128)S(1)}, f32[1,128]{1,0:T(1,128)}, u32[]{:S(2)}) copy-start(f32[1,128]{1,0:T(1,128)} %kg_ref.1) | copy-start | bytes 1540
  88.1 21.0 %all-to-all-start.2 = ((bf16[4,256,256]{2,1,0:T(8,128)(2,1)}), bf16[4,256,256]{2,1,0:T(8,128)(2,1)S(1)}, u32[]{:S(2)}, u32[]{:S(2)}) async-start(bf16[4,256,256]{2,1,0:T(8,128)(2,1)} %get-tuple-element.22), calls=%async_computation.2 | async-start | bytes 1048576 | tf_op jit(solution)/shard_map/all_to_all | solution.py:246
  91.5 12.3 %collective-permute-start.12 = (bf16[256,128]{1,0:T(8,128)(2,1)S(1)}, bf16[256,128]{1,0:T(8,128)(2,1)S(1)}, u32[]{:S(2)}, u32[]{:S(2)}) collective-permute-start(bf16[256,128]{1,0:T(8,128)(2,1)S(1)} %get-tuple-element.21.q0), channel_id=1, source_target_pairs={{0,6},{2,4},{4,2},{6,0},{1,7},{3,5},{5,3},{7,1},{8,14},{10,12},{12... | collective-permute-start | bytes 196616 | tf_op jit(solution)/shard_map/ppermute | solution.py:39
  99.4 6.2 %collective-permute-start.11 = (bf16[256,128]{1,0:T(8,128)(2,1)S(1)}, bf16[256,128]{1,0:T(8,128)(2,1)S(1)}, u32[]{:S(2)}, u32[]{:S(2)}) collective-permute-start(bf16[256,128]{1,0:T(8,128)(2,1)S(1)} %get-tuple-element.21.q0), channel_id=1, source_target_pairs={{0,4},{2,6},{4,0},{6,2},{1,5},{3,7},{5,1},{7,3},{8,12},{10,14},{12... | collective-permute-start | bytes 196616 | tf_op jit(solution)/shard_map/ppermute | solution.py:39
  101.5 7.6 %collective-permute-start.10 = (bf16[256,128]{1,0:T(8,128)(2,1)S(1)}, bf16[256,128]{1,0:T(8,128)(2,1)S(1)}, u32[]{:S(2)}, u32[]{:S(2)}) collective-permute-start(bf16[256,128]{1,0:T(8,128)(2,1)S(1)} %get-tuple-element.21.q0), channel_id=1, source_target_pairs={{0,2},{2,0},{4,6},{6,4},{1,3},{3,1},{5,7},{7,5},{8,10},{10,8},{12,... | collective-permute-start | bytes 196616 | tf_op jit(solution)/shard_map/ppermute | solution.py:39

commit v7 on v5

--- a/solution.py
+++ b/solution.py
@@ -144,8 +144,8 @@
         kv_ref[x, :, HS : 2 * HS] = values
 
 
-def attend_kernel(s_ref, q0, q1, q2, q3, kv_ref, out_ref, qs_ref):
-    for k, q_ref in enumerate((q0, q1, q2, q3)):
+def attend_kernel(s_ref, q0, q3, q1, q2, kv_ref, out_ref, qs_ref):
+    for k, q_ref in ((0, q0), (3, q3), (1, q1), (2, q2)):
         quarter = s_ref[4 + k]
         for a in range(4):
             for half in range(2):
@@ -221,7 +221,7 @@
         3, 24, 10 * 8 * TB * FB, 2 << 20, name="norm",
     )(where, received, q_gain, k_gain)
 
-    qs = [q] + [swap(q, GATHER, k, 4) for k in (1, 2, 3)]
+    qs = [q] + [swap(q, GATHER, k, 4) for k in (3, 1, 2)]
     kvs = lax.all_to_all(kv, REDUCE, split_axis=0, concat_axis=0, tiled=True)
     partial = call(
         attend_kernel,

time: 126 us -> 128 us (1.016)
  no operation moved by 1% of the time
where the time goes in v7:
time: 128 us; the launch traced here: 126 us
  starting transfers between devices  59.5 us (46%)
  blocking collectives  32.9 us (26%)
  waiting for transfers between devices  19.3 us (15%)
  Pallas kernels  10.9 us (9%)
  local copies, waits for them, and re-layouts  1.78 us (1%)
    ppermute x10, starting transfers between devices, swap(): return lax.ppermute(x, axis, [(i, i ^ k) for i in range(n)])  31.5 us
    all_to_all x1, blocking collectives, body(): lax.all_to_all(second, ('core',) + REDUCE, split_axis=0, concat_axis=0, t...  20.9 us
    all_to_all x1, starting transfers between devices, body(): lax.all_to_all(jnp.broadcast_to(tokens.reshape(1, 4, QT, FB), (4, 4, QT,...  14.3 us
    all_to_all x1, blocking collectives, body(): lax.all_to_all(partial, GATHER, split_axis=0, concat_axis=0, tiled=True)  12 us
    all_to_all x1, waiting for transfers between devices, body(): lax.all_to_all(jnp.broadcast_to(tokens.reshape(1, 4, QT, FB), (4, 4, QT,...  10.2 us
    ppermute x3, starting transfers between devices, shift(): return lax.ppermute(x, axis, [(i, (i + k) % 4) for i in range(4)])  10.2 us
    ppermute x10, waiting for transfers between devices, swap(): return lax.ppermute(x, axis, [(i, i ^ k) for i in range(n)])  7.63 us
    pallas_call x2, Pallas kernels, project(): call(project_kernel, (jax.ShapeDtypeStruct((8, rows, FB), bf16), jax.Shap...  3.66 us
  transfers between devices with their start and end apart: 15, of which 5 were waited for; matrix products, arithmetic and copies ran while one was open for 1% of the time, Pallas kernels for 3%

profile of v7, /device:TPU:24, one launch (start us, length us, event | category | flops | bytes accessed | tf_op | source)
XLA Modules:
  0.0 125.6 jit_solution(10366626014045072906)
XLA Ops:
  0.0 1.1 fusion.refs_0_
  1.1 5.2 %collective-permute-start.2 = (bf16[384,384]{1,0:T(8,128)(2,1)S(1)}, bf16[384,384]{1,0:T(8,128)(2,1)S(1)}, u32[]{:S(2)}, u32[]{:S(2)}) collective-permute-start(bf16[384,384]{1,0:T(8,128)(2,1)S(1)} %fusion.refs_0_), channel_id=1, source_target_pairs={{0,2},{2,0},{1,3},{3,1},{4,6},{6,4},{5,7},{7,5},{8,10},{10,8},{9,1... | collective-permute-start | bytes 884744 | tf_op jit(solution)/shard_map/ppermute | solution.py:39
  6.3 1.7 %broadcast_in_dim.9 = bf16[4,4,32,384]{3,2,1,0:T(8,128)(2,1)} broadcast(bf16[4,32,384]{2,1,0:T(8,128)(2,1)} %bitcast.16), dimensions={1,2,3} | broadcast | bytes 491520 | tf_op jit(solution)/shard_map/broadcast_in_dim | solution.py:188
  8.0 14.3 %all-to-all-start = ((bf16[16,32,384]{2,1,0:T(8,128)(2,1)}), bf16[16,32,384]{2,1,0:T(8,128)(2,1)S(1)}, u32[]{:S(2)}, u32[]{:S(2)}) async-start(bf16[16,32,384]{2,1,0:T(8,128)(2,1)} %bitcast.9), calls=%async_computation | async-start | bytes 786432 | tf_op jit(solution)/shard_map/all_to_all | solution.py:187
  22.3 0.1 stack.35.s_ref
  22.4 0.0 collective-permute-done.2.x_ref
  22.4 0.6 copy.8.refs_1_
  23.0 1.9 %collective-permute-start.5 = (bf16[384,384]{1,0:T(8,128)(2,1)S(1)}, bf16[384,384]{1,0:T(8,128)(2,1)S(1)}, u32[]{:S(2)}, u32[]{:S(2)}) collective-permute-start(bf16[384,384]{1,0:T(8,128)(2,1)S(1)} %fusion.refs_0_), channel_id=1, source_target_pairs={{0,16},{16,0},{1,17},{17,1},{2,18},{18,2},{3,19},{19,3},{4,20},{20... | collective-permute-start | bytes 884744 | tf_op jit(solution)/shard_map/ppermute | solution.py:39
  24.9 3.8 %collective-permute-start.3 = (bf16[384,384]{1,0:T(8,128)(2,1)S(1)}, bf16[384,384]{1,0:T(8,128)(2,1)S(1)}, u32[]{:S(2)}, u32[]{:S(2)}) collective-permute-start(bf16[384,384]{1,0:T(8,128)(2,1)S(1)} %fusion.refs_0_), channel_id=1, source_target_pairs={{0,4},{4,0},{1,5},{5,1},{2,6},{6,2},{3,7},{7,3},{8,12},{12,8},{9,1... | collective-permute-start | bytes 884744 | tf_op jit(solution)/shard_map/ppermute | solution.py:39
  28.7 2.1 %collective-permute-start.6 = (bf16[384,384]{1,0:T(8,128)(2,1)S(1)}, bf16[384,384]{1,0:T(8,128)(2,1)S(1)}, u32[]{:S(2)}, u32[]{:S(2)}) collective-permute-start(bf16[384,384]{1,0:T(8,128)(2,1)S(1)} %copy.8.refs_1_), channel_id=1, source_target_pairs={{0,16},{16,0},{1,17},{17,1},{2,18},{18,2},{3,19},{19,3},{4,20},{20... | collective-permute-start | bytes 884744 | tf_op jit(solution)/shard_map/ppermute | solution.py:39
  30.9 2.2 %collective-permute-start.4 = (bf16[384,384]{1,0:T(8,128)(2,1)S(1)}, bf16[384,384]{1,0:T(8,128)(2,1)S(1)}, u32[]{:S(2)}, u32[]{:S(2)}) collective-permute-start(bf16[384,384]{1,0:T(8,128)(2,1)S(1)} %copy.8.refs_1_), channel_id=1, source_target_pairs={{0,4},{4,0},{1,5},{5,1},{2,6},{6,2},{3,7},{7,3},{8,12},{12,8},{9,1... | collective-permute-start | bytes 884744 | tf_op jit(solution)/shard_map/ppermute | solution.py:39
  33.1 10.2 %all-to-all-done.xa_ref = bf16[16,32,384]{2,1,0:T(8,128)(2,1)S(1)} async-done(((bf16[16,32,384]{2,1,0:T(8,128)(2,1)}), bf16[16,32,384]{2,1,0:T(8,128)(2,1)S(1)}, u32[]{:S(2)}, u32[]{:S(2)}) %all-to-all-start) | async-done | bytes 393248 | tf_op jit(solution)/shard_map/all_to_all | solution.py:187
  43.3 3.1 %collective-permute-start.9 = (bf16[16,32,384]{2,1,0:T(8,128)(2,1)S(1)}, bf16[16,32,384]{2,1,0:T(8,128)(2,1)S(1)}, u32[]{:S(2)}, u32[]{:S(2)}) collective-permute-start(bf16[16,32,384]{2,1,0:T(8,128)(2,1)S(1)} %all-to-all-done.xa_ref), channel_id=1, source_target_pairs={{0,256},{128,384},{256,0},{384,128},{1,257},{129,385},{257,1},{385... | collective-permute-start | bytes 1179656 | tf_op jit(solution)/shard_map/ppermute | solution.py:35
  46.4 0.0 collective-permute-done.5.refs_4_
  46.4 1.9 %collective-permute-start.1 = (bf16[16,32,384]{2,1,0:T(8,128)(2,1)S(1)}, bf16[16,32,384]{2,1,0:T(8,128)(2,1)S(1)}, u32[]{:S(2)}, u32[]{:S(2)}) collective-permute-start(bf16[16,32,384]{2,1,0:T(8,128)(2,1)S(1)} %all-to-all-done.xa_ref), channel_id=1, source_target_pairs={{0,384},{128,0},{256,128},{384,256},{1,385},{129,1},{257,129},{385... | collective-permute-start | bytes 1179656 | tf_op jit(solution)/shard_map/ppermute | solution.py:35
  48.3 0.0 collective-permute-done.3.refs_2_
  48.4 5.1 %collective-permute-start = (bf16[16,32,384]{2,1,0:T(8,128)(2,1)S(1)}, bf16[16,32,384]{2,1,0:T(8,128)(2,1)S(1)}, u32[]{:S(2)}, u32[]{:S(2)}) collective-permute-start(bf16[16,32,384]{2,1,0:T(8,128)(2,1)S(1)} %all-to-all-done.xa_ref), channel_id=1, source_target_pairs={{0,128},{128,256},{256,384},{384,0},{1,129},{129,257},{257,385},{3... | collective-permute-start | bytes 1179656 | tf_op jit(solution)/shard_map/ppermute | solution.py:35
  53.5 0.0 collective-permute-done.6.refs_5_
  53.5 1.9 %collective-permute-start.7 = (bf16[384,384]{1,0:T(8,128)(2,1)S(1)}, bf16[384,384]{1,0:T(8,128)(2,1)S(1)}, u32[]{:S(2)}, u32[]{:S(2)}) collective-permute-start(bf16[384,384]{1,0:T(8,128)(2,1)S(1)} %collective-permute-done.3.refs_2_), channel_id=1, source_target_pairs={{0,16},{16,0},{1,17},{17,1},{2,18},{18,2},{3,19},{19,3},{4,20},{20... | collective-permute-start | bytes 884744 | tf_op jit(solution)/shard_map/ppermute | solution.py:39
  55.4 0.0 collective-permute-done.4.refs_3_
  55.4 2.4 %collective-permute-start.8 = (bf16[384,384]{1,0:T(8,128)(2,1)S(1)}, bf16[384,384]{1,0:T(8,128)(2,1)S(1)}, u32[]{:S(2)}, u32[]{:S(2)}) collective-permute-start(bf16[384,384]{1,0:T(8,128)(2,1)S(1)} %collective-permute-done.4.refs_3_), channel_id=1, source_target_pairs={{0,16},{16,0},{1,17},{17,1},{2,18},{18,2},{3,19},{19,3},{4,20},{20... | collective-permute-start | bytes 884744 | tf_op jit(solution)/shard_map/ppermute | solution.py:39
  57.9 0.0 collective-permute-done.7.refs_6_
  57.9 1.2 collective-permute-done.8.refs_7_
  59.1 1.3 %prep.1 = (bf16[1536,768]{1,0:T(8,128)(2,1)S(1)}, f32[8,768]{1,0:T(8,128)S(1)}) custom-call(s32[8]{0:T(128)S(1)} %stack.35.s_ref, bf16[384,384]{1,0:T(8,128)(2,1)S(1)} %fusion.refs_0_, bf16[384,384]{1,0:T(8,128)(2,1)S(1)} %copy.8.refs_1_, bf16[384,384]{1,0:T(8,128)(2,1)S(1)} %collective-permute-done.3.refs_2_, ...), custom_call_target="tpu_custom_call" | custom-call | tf_op jit(solution)/shard_map/prep/pallas_call | solution.py:201
  60.3 0.0 collective-permute-done.9.xb_ref
  60.3 1.8 %project.2 = (bf16[8,64,384]{2,1,0:T(8,128)(2,1)S(1)}, f32[8,256]{1,0:T(8,128)S(1)}) custom-call(s32[8]{0:T(128)S(1)} %stack.35.s_ref, bf16[16,32,384]{2,1,0:T(8,128)(2,1)S(1)} %all-to-all-done.xa_ref, bf16[16,32,384]{2,1,0:T(8,128)(2,1)S(1)} %collective-permute-done.9.xb_ref, bf16[1536,768]{1,0:T(8,128)(2,1)S(1)} %get-tuple-element.16.w_ref, ...), custom_call_target="tpu_custom_call" | custom-call | tf_op jit(solution)/shard_map/project/pallas_call | solution.py:208
  62.2 1.4 %collective-permute-done.1.xb_ref = bf16[16,32,384]{2,1,0:T(8,128)(2,1)S(1)} collective-permute-done((bf16[16,32,384]{2,1,0:T(8,128)(2,1)S(1)}, bf16[16,32,384]{2,1,0:T(8,128)(2,1)S(1)}, u32[]{:S(2)}, u32[]{:S(2)}) %collective-permute-start.1) | collective-permute-done | bytes 393248 | tf_op jit(solution)/shard_map/ppermute | solution.py:35
  63.6 0.0 collective-permute-done.xa_ref
  63.6 0.0 copy-start
  63.6 0.0 copy-start.1
  63.6 1.8 %project.3 = (bf16[8,144,384]{2,1,0:T(8,128)(2,1)S(1)}, f32[8,256]{1,0:T(8,128)}) custom-call(s32[8]{0:T(128)S(1)} %stack.35.s_ref, bf16[16,32,384]{2,1,0:T(8,128)(2,1)S(1)} %collective-permute-done.xa_ref, bf16[16,32,384]{2,1,0:T(8,128)(2,1)S(1)} %collective-permute-done.1.xb_ref, bf16[1536,768]{1,0:T(8,128)(2,1)S(1)} %get-tuple-element.16.w_ref, ...), custom_call_target="tpu_custom_call" | custom-call | tf_op jit(solution)/shard_map/project/pallas_call | solution.py:208
  65.4 20.9 %all_to_all.20.r_ref = bf16[8,144,384]{2,1,0:T(8,128)(2,1)S(1)} all-to-all(bf16[8,144,384]{2,1,0:T(8,128)(2,1)S(1)} %get-tuple-element.20), channel_id=1, replica_groups=mesh['y'=4,'zh'=4,'core'=2,'xa'=2,'xb'=2,'zg'=2,'zr'=2] {'core','xa','zr'}, dimensions={0} | all-to-all | bytes 1769472 | tf_op jit(solution)/shard_map/all_to_all | solution.py:217
  86.3 0.0 copy-done
  86.3 0.0 copy-done.1
  86.3 2.1 %norm.1 = (bf16[256,128]{1,0:T(8,128)(2,1)S(1)}, bf16[4,256,256]{2,1,0:T(8,128)(2,1)}) custom-call(s32[8]{0:T(128)S(1)} %stack.35.s_ref, bf16[8,144,384]{2,1,0:T(8,128)(2,1)S(1)} %all_to_all.20.r_ref, f32[1,128]{1,0:T(1,128)S(1)} %copy-done, f32[1,128]{1,0:T(1,128)S(1)} %copy-done.1), custom_call_target="tpu_custom_call" | custom-call | flops 3932160 | bytes 2097152 | tf_op jit(solution)/shard_map/norm/pallas_call | solution.py:218
  88.4 3.5 %all-to-all-start.2 = ((bf16[4,256,256]{2,1,0:T(8,128)(2,1)}), bf16[4,256,256]{2,1,0:T(8,128)(2,1)S(1)}, u32[]{:S(2)}, u32[]{:S(2)}) async-start(bf16[4,256,256]{2,1,0:T(8,128)(2,1)} %get-tuple-element.22), calls=%async_computation.2 | async-start | bytes 1048576 | tf_op jit(solution)/shard_map/all_to_all | solution.py:225
  91.8 3.3 %collective-permute-start.12 = (bf16[256,128]{1,0:T(8,128)(2,1)S(1)}, bf16[256,128]{1,0:T(8,128)(2,1)S(1)}, u32[]{:S(2)}, u32[]{:S(2)}) collective-permute-start(bf16[256,128]{1,0:T(8,128)(2,1)S(1)} %get-tuple-element.21.q0), channel_id=1, source_target_pairs={{0,4},{2,6},{4,0},{6,2},{1,5},{3,7},{5,1},{7,3},{8,12},{10,14},{12... | collective-permute-start | bytes 196616 | tf_op jit(solution)/shard_map/ppermute | solution.py:39
  95.2 6.7 %collective-permute-start.11 = (bf16[256,128]{1,0:T(8,128)(2,1)S(1)}, bf16[256,128]{1,0:T(8,128)(2,1)S(1)}, u32[]{:S(2)}, u32[]{:S(2)}) collective-permute-start(bf16[256,128]{1,0:T(8,128)(2,1)S(1)} %get-tuple-element.21.q0), channel_id=1, source_target_pairs={{0,2},{2,0},{4,6},{6,4},{1,3},{3,1},{5,7},{7,5},{8,10},{10,8},{12,... | collective-permute-start | bytes 196616 | tf_op jit(solution)/shard_map/ppermute | solution.py:39
  101.9 1.9 %collective-permute-start.10 = (bf16[256,128]{1,0:T(8,128)(2,1)S(1)}, bf16[256,128]{1,0:T(8,128)(2,1)S(1)}, u32[]{:S(2)}, u32[]{:S(2)}) collective-permute-start(bf16[256,128]{1,0:T(8,128)(2,1)S(1)} %get-tuple-element.21.q0), channel_id=1, source_target_pairs={{0,6},{2,4},{4,2},{6,0},{1,7},{3,5},{5,3},{7,1},{8,14},{10,12},{12... | collective-permute-start | bytes 196616 | tf_op jit(solution)/shard_map/ppermute | solution.py:39
  103.8 0.0 collective-permute-done.12.q2
  103.8 0.6 collective-permute-done.11.q1
  104.5 5.8 %collective-permute-done.10.q3 = bf16[256,128]{1,0:T(8,128)(2,1)S(1)} collective-permute-done((bf16[256,128]{1,0:T(8,128)(2,1)S(1)}, bf16[256,128]{1,0:T(8,128)(2,1)S(1)}, u32[]{:S(2)}, u32[]{:S(2)}) %collective-permute-start.10) | collective-permute-done | bytes 65568 | tf_op jit(solution)/shard_map/ppermute | solution.py:39
  110.3 0.0 all-to-all-done.2.kv_ref
  110.3 2.0 %attend.1 = bf16[4,144,256]{2,1,0:T(8,128)(2,1)S(1)} custom-call(s32[8]{0:T(128)S(1)} %stack.35.s_ref, bf16[256,128]{1,0:T(8,128)(2,1)S(1)} %get-tuple-element.21.q0, bf16[256,128]{1,0:T(8,128)(2,1)S(1)} %collective-permute-done.10.q3, bf16[256,128]{1,0:T(8,128)(2,1)S(1)} %collective-permute-done.11.q1, bf16[256,128]{1,0:T(8,128)(2,1)S(1)} %collective-permute-done.12.q2, ...), custom_call_target="tpu_custom_call" | custom-call | flops 536870912 | bytes 2097152 | tf_op jit(solution)/shard_map/attend/pallas_call | solution.py:226
  112.3 12.0 %all_to_all.21.r_ref = bf16[4,144,256]{2,1,0:T(8,128)(2,1)S(1)} all-to-all(bf16[4,144,256]{2,1,0:T(8,128)(2,1)S(1)} %attend.1), channel_id=1, replica_groups=mesh['y'=4,'zh'=4,'core'=2,'xa'=2,'xb'=2,'zg'=2,'zr'=2] {'xb','zg'}, dimensions={0} | all-to-all | bytes 589824 | tf_op jit(solution)/shard_map/all_to_all | solution.py:232
  124.3 1.3 %combine.1 = f32[256,128]{1,0:T(8,128)} custom-call(s32[8]{0:T(128)S(1)} %stack.35.s_ref, bf16[4,144,256]{2,1,0:T(8,128)(2,1)S(1)} %all_to_all.21.r_ref), custom_call_target="tpu_custom_call" | custom-call | flops 262144 | bytes 1048576 | tf_op jit(solution)/shard_map/combine/pallas_call | solution.py:233
Async XLA Ops:
  1.1 21.3 %collective-permute-start.2 = (bf16[384,384]{1,0:T(8,128)(2,1)S(1)}, bf16[384,384]{1,0:T(8,128)(2,1)S(1)}, u32[]{:S(2)}, u32[]{:S(2)}) collective-permute-start(bf16[384,384]{1,0:T(8,128)(2,1)S(1)} %fusion.refs_0_), channel_id=1, source_target_pairs={{0,2},{2,0},{1,3},{3,1},{4,6},{6,4},{5,7},{7,5},{8,10},{10,8},{9,1... | collective-permute-start | bytes 884744 | tf_op jit(solution)/shard_map/ppermute | solution.py:39
  8.0 35.3 %all-to-all-start = ((bf16[16,32,384]{2,1,0:T(8,128)(2,1)}), bf16[16,32,384]{2,1,0:T(8,128)(2,1)S(1)}, u32[]{:S(2)}, u32[]{:S(2)}) async-start(bf16[16,32,384]{2,1,0:T(8,128)(2,1)} %bitcast.9), calls=%async_computation | async-start | bytes 786432 | tf_op jit(solution)/shard_map/all_to_all | solution.py:187
  23.0 23.4 %collective-permute-start.5 = (bf16[384,384]{1,0:T(8,128)(2,1)S(1)}, bf16[384,384]{1,0:T(8,128)(2,1)S(1)}, u32[]{:S(2)}, u32[]{:S(2)}) collective-permute-start(bf16[384,384]{1,0:T(8,128)(2,1)S(1)} %fusion.refs_0_), channel_id=1, source_target_pairs={{0,16},{16,0},{1,17},{17,1},{2,18},{18,2},{3,19},{19,3},{4,20},{20... | collective-permute-start | bytes 884744 | tf_op jit(solution)/shard_map/ppermute | solution.py:39
  24.9 23.5 %collective-permute-start.3 = (bf16[384,384]{1,0:T(8,128)(2,1)S(1)}, bf16[384,384]{1,0:T(8,128)(2,1)S(1)}, u32[]{:S(2)}, u32[]{:S(2)}) collective-permute-start(bf16[384,384]{1,0:T(8,128)(2,1)S(1)} %fusion.refs_0_), channel_id=1, source_target_pairs={{0,4},{4,0},{1,5},{5,1},{2,6},{6,2},{3,7},{7,3},{8,12},{12,8},{9,1... | collective-permute-start | bytes 884744 | tf_op jit(solution)/shard_map/ppermute | solution.py:39
  28.7 24.8 %collective-permute-start.6 = (bf16[384,384]{1,0:T(8,128)(2,1)S(1)}, bf16[384,384]{1,0:T(8,128)(2,1)S(1)}, u32[]{:S(2)}, u32[]{:S(2)}) collective-permute-start(bf16[384,384]{1,0:T(8,128)(2,1)S(1)} %copy.8.refs_1_), channel_id=1, source_target_pairs={{0,16},{16,0},{1,17},{17,1},{2,18},{18,2},{3,19},{19,3},{4,20},{20... | collective-permute-start | bytes 884744 | tf_op jit(solution)/shard_map/ppermute | solution.py:39
  30.9 24.6 %collective-permute-start.4 = (bf16[384,384]{1,0:T(8,128)(2,1)S(1)}, bf16[384,384]{1,0:T(8,128)(2,1)S(1)}, u32[]{:S(2)}, u32[]{:S(2)}) collective-permute-start(bf16[384,384]{1,0:T(8,128)(2,1)S(1)} %copy.8.refs_1_), channel_id=1, source_target_pairs={{0,4},{4,0},{1,5},{5,1},{2,6},{6,2},{3,7},{7,3},{8,12},{12,8},{9,1... | collective-permute-start | bytes 884744 | tf_op jit(solution)/shard_map/ppermute | solution.py:39
  43.3 17.1 %collective-permute-start.9 = (bf16[16,32,384]{2,1,0:T(8,128)(2,1)S(1)}, bf16[16,32,384]{2,1,0:T(8,128)(2,1)S(1)}, u32[]{:S(2)}, u32[]{:S(2)}) collective-permute-start(bf16[16,32,384]{2,1,0:T(8,128)(2,1)S(1)} %all-to-all-done.xa_ref), channel_id=1, source_target_pairs={{0,256},{128,384},{256,0},{384,128},{1,257},{129,385},{257,1},{385... | collective-permute-start | bytes 1179656 | tf_op jit(solution)/shard_map/ppermute | solution.py:35
  46.4 17.2 %collective-permute-start.1 = (bf16[16,32,384]{2,1,0:T(8,128)(2,1)S(1)}, bf16[16,32,384]{2,1,0:T(8,128)(2,1)S(1)}, u32[]{:S(2)}, u32[]{:S(2)}) collective-permute-start(bf16[16,32,384]{2,1,0:T(8,128)(2,1)S(1)} %all-to-all-done.xa_ref), channel_id=1, source_target_pairs={{0,384},{128,0},{256,128},{384,256},{1,385},{129,1},{257,129},{385... | collective-permute-start | bytes 1179656 | tf_op jit(solution)/shard_map/ppermute | solution.py:35
  48.4 15.2 %collective-permute-start = (bf16[16,32,384]{2,1,0:T(8,128)(2,1)S(1)}, bf16[16,32,384]{2,1,0:T(8,128)(2,1)S(1)}, u32[]{:S(2)}, u32[]{:S(2)}) collective-permute-start(bf16[16,32,384]{2,1,0:T(8,128)(2,1)S(1)} %all-to-all-done.xa_ref), channel_id=1, source_target_pairs={{0,128},{128,256},{256,384},{384,0},{1,129},{129,257},{257,385},{3... | collective-permute-start | bytes 1179656 | tf_op jit(solution)/shard_map/ppermute | solution.py:35
  53.5 4.4 %collective-permute-start.7 = (bf16[384,384]{1,0:T(8,128)(2,1)S(1)}, bf16[384,384]{1,0:T(8,128)(2,1)S(1)}, u32[]{:S(2)}, u32[]{:S(2)}) collective-permute-start(bf16[384,384]{1,0:T(8,128)(2,1)S(1)} %collective-permute-done.3.refs_2_), channel_id=1, source_target_pairs={{0,16},{16,0},{1,17},{17,1},{2,18},{18,2},{3,19},{19,3},{4,20},{20... | collective-permute-start | bytes 884744 | tf_op jit(solution)/shard_map/ppermute | solution.py:39
  55.4 3.6 %collective-permute-start.8 = (bf16[384,384]{1,0:T(8,128)(2,1)S(1)}, bf16[384,384]{1,0:T(8,128)(2,1)S(1)}, u32[]{:S(2)}, u32[]{:S(2)}) collective-permute-start(bf16[384,384]{1,0:T(8,128)(2,1)S(1)} %collective-permute-done.4.refs_3_), channel_id=1, source_target_pairs={{0,16},{16,0},{1,17},{17,1},{2,18},{18,2},{3,19},{19,3},{4,20},{20... | collective-permute-start | bytes 884744 | tf_op jit(solution)/shard_map/ppermute | solution.py:39
  63.6 22.7 %copy-start = (f32[1,128]{1,0:T(1,128)S(1)}, f32[1,128]{1,0:T(1,128)}, u32[]{:S(2)}) copy-start(f32[1,128]{1,0:T(1,128)} %qg_ref.1) | copy-start | bytes 1540
  63.6 22.7 %copy-start.1 = (f32[1,128]{1,0:T(1,128)S(1)}, f32[1,128]{1,0:T(1,128)}, u32[]{:S(2)}) copy-start(f32[1,128]{1,0:T(1,128)} %kg_ref.1) | copy-start | bytes 1540
  88.4 21.9 %all-to-all-start.2 = ((bf16[4,256,256]{2,1,0:T(8,128)(2,1)}), bf16[4,256,256]{2,1,0:T(8,128)(2,1)S(1)}, u32[]{:S(2)}, u32[]{:S(2)}) async-start(bf16[4,256,256]{2,1,0:T(8,128)(2,1)} %get-tuple-element.22), calls=%async_computation.2 | async-start | bytes 1048576 | tf_op jit(solution)/shard_map/all_to_all | solution.py:225
  91.8 12.0 %collective-permute-start.12 = (bf16[256,128]{1,0:T(8,128)(2,1)S(1)}, bf16[256,128]{1,0:T(8,128)(2,1)S(1)}, u32[]{:S(2)}, u32[]{:S(2)}) collective-permute-start(bf16[256,128]{1,0:T(8,128)(2,1)S(1)} %get-tuple-element.21.q0), channel_id=1, source_target_pairs={{0,4},{2,6},{4,0},{6,2},{1,5},{3,7},{5,1},{7,3},{8,12},{10,14},{12... | collective-permute-start | bytes 196616 | tf_op jit(solution)/shard_map/ppermute | solution.py:39
  95.2 9.3 %collective-permute-start.11 = (bf16[256,128]{1,0:T(8,128)(2,1)S(1)}, bf16[256,128]{1,0:T(8,128)(2,1)S(1)}, u32[]{:S(2)}, u32[]{:S(2)}) collective-permute-start(bf16[256,128]{1,0:T(8,128)(2,1)S(1)} %get-tuple-element.21.q0), channel_id=1, source_target_pairs={{0,2},{2,0},{4,6},{6,4},{1,3},{3,1},{5,7},{7,5},{8,10},{10,8},{12,... | collective-permute-start | bytes 196616 | tf_op jit(solution)/shard_map/ppermute | solution.py:39
  101.9 8.4 %collective-permute-start.10 = (bf16[256,128]{1,0:T(8,128)(2,1)S(1)}, bf16[256,128]{1,0:T(8,128)(2,1)S(1)}, u32[]{:S(2)}, u32[]{:S(2)}) collective-permute-start(bf16[256,128]{1,0:T(8,128)(2,1)S(1)} %get-tuple-element.21.q0), channel_id=1, source_target_pairs={{0,6},{2,4},{4,2},{6,0},{1,7},{3,5},{5,3},{7,1},{8,14},{10,12},{12... | collective-permute-start | bytes 196616 | tf_op jit(solution)/shard_map/ppermute | solution.py:39
